TPU v7x, 128 devices: a whole 4x4x4 slice. The times are simulated.
128 devices in a mesh: seg: 16 (over y, x), blk: 8 (over z, core).
Axes of the slice: x: 4, y: 4, z: 4, core: 2. Of those that a mesh axis runs over, the one named last changes fastest.
Arguments:
- tokens: bfloat16 [128, 512, 768], P('seg', 'blk'), may hold values from -6 to 6
- memory: bfloat16 [128, 20, 768], P('seg'), may hold values from -6 to 6
- mem_init: bfloat16 [20, 768], replicated, may hold values from -6 to 6
- reset_flags: int32 [128], P('seg'), may hold values 0 or 1
- doc_ids: int32 [128, 512], P('seg'), may hold values from 0 to 2, as said below
- w_qkv: bfloat16 [768, 2304], replicated, may hold values from -0.21875 to 0.21875
- b_query: bfloat16 [768], replicated, may hold values from -3 to 3
- b_value: bfloat16 [768], replicated, may hold values from -3 to 3
- w_out: bfloat16 [768, 768], replicated, may hold values from -3.5 to 3.5
- b_out: bfloat16 [768], replicated, may hold values from -2 to 2
- norm1_gain: bfloat16 [768], replicated, may hold values from 0.099609375 to 1.8984375
- norm1_bias: bfloat16 [768], replicated, may hold values from -2 to 2
- w_in: bfloat16 [768, 3072], replicated, may hold values from -0.21875 to 0.21875
- b_in: bfloat16 [3072], replicated, may hold values from -3 to 3
- w_down: bfloat16 [3072, 768], replicated, may hold values from -0.109375 to 0.109375
- b_down: bfloat16 [768], replicated, may hold values from -2 to 2
- norm2_gain: bfloat16 [768], replicated, may hold values from 0.099609375 to 1.8984375
- norm2_bias: bfloat16 [768], replicated, may hold values from -2 to 2
- out_cot: bfloat16 [128, 512, 768], P('seg', 'blk'), may hold values from -6 to 6
- mem_cot: bfloat16 [128, 20, 768], P('seg'), may hold values from -6 to 6
Outputs:
- output: bfloat16 [128, 512, 768], P('seg', 'blk')
- mem_output: bfloat16 [128, 20, 768], P('seg')
- grad_tokens: bfloat16 [128, 512, 768], P('seg', 'blk')
- grad_memory: bfloat16 [128, 20, 768], P('seg')
- grad_mem_init: float32 [20, 768], replicated
- grad_w_qkv: float32 [768, 2304], replicated
- grad_b_query: float32 [768], replicated
- grad_b_value: float32 [768], replicated
- grad_w_out: float32 [768, 768], replicated
- grad_b_out: float32 [768], replicated
- grad_norm1_gain: float32 [768], replicated
- grad_norm1_bias: float32 [768], replicated
- grad_w_in: float32 [768, 3072], replicated
- grad_b_in: float32 [3072], replicated
- grad_w_down: float32 [3072, 768], replicated
- grad_b_down: float32 [768], replicated
- grad_norm2_gain: float32 [768], replicated
- grad_norm2_bias: float32 [768], replicated
Inputs may be any that keep to these rules, and one draw needn't show every extreme that they name: `doc_ids`: within a segment the numbers never fall and take the values 0, 1 and 2; document 1 starts before position 64 and ends at or after position 448.
All inputs are finite; a program needn't handle non-finite values. No bound on the sum of `reset_flags` on one device may be relied on, other than what follows from the above.
Results may differ from a plain program's by a relative error of at most 0.028.
Values may be sent and summed in bfloat16 or wider, within the bound.
No kernel may reach another device: no remote copies, remote signals or barrier semaphores. Data moves between devices by JAX's collectives and lax.ppermute only.
A program may use at most 256 MiB of HBM per device.

v0:
```python
import jax
import jax.numpy as jnp
from jax import lax
from jax.sharding import PartitionSpec as P

HEADS = 12


EPS = 1e-12
FLOOR = -1000000000.0


def normalize(value):
    centre = jnp.mean(value, axis=-1, keepdims=True)
    centered = value - centre
    spread = jnp.mean(centered * centered, axis=-1, keepdims=True)
    return centered * lax.rsqrt(spread + EPS)


def gelu_exact(value):
    return jax.nn.gelu(value, approximate=False)


def project(left, right):
    return jnp.einsum("sri,io->sro", left, right, preferred_element_type=jnp.float32)


def project_back(left, right):
    return jnp.einsum("sro,io->sri", left, right, preferred_element_type=jnp.float32)


def outer_sum(left, right):
    return jnp.einsum("sri,sro->io", left, right, preferred_element_type=jnp.float32)


def split_heads(value, head_count):
    return value.reshape(value.shape[0], value.shape[1], head_count, value.shape[2] // head_count)


def local(
    tokens,
    memory,
    mem_init,
    reset_flags,
    doc_ids,
    w_qkv,
    b_query,
    b_value,
    w_out,
    b_out,
    norm1_gain,
    norm1_bias,
    w_in,
    b_in,
    w_down,
    b_down,
    norm2_gain,
    norm2_bias,
    out_cot,
    mem_cot,
):
    seg_count, tok_count, model_width = tokens.shape
    mem_count = memory.shape[1]
    head_count = HEADS
    score_scale = (model_width // head_count) ** (-0.5)
    blk_place = lax.axis_index("blk")
    lead_flag = (blk_place == 0).astype(jnp.float32)
    flag_rows = (reset_flags == 1)[:, None, None]
    mem_rows = jnp.where(flag_rows, mem_init[None], memory)
    all_rows = jnp.concatenate([mem_rows, tokens], axis=1)
    qkv_rows = project(all_rows, w_qkv)
    query_low = (qkv_rows[..., :model_width] + b_query.astype(jnp.float32)).astype(jnp.bfloat16)
    key_rows = qkv_rows[..., model_width : 2 * model_width].astype(jnp.bfloat16)
    value_rows = (qkv_rows[..., 2 * model_width :] + b_value.astype(jnp.float32)).astype(
        jnp.bfloat16
    )
    local_kv = jnp.concatenate([key_rows[:, mem_count:], value_rows[:, mem_count:]], axis=-1)
    gathered = lax.all_gather(local_kv, "blk", axis=1, tiled=True)
    my_docs = lax.dynamic_slice_in_dim(doc_ids, blk_place * tok_count, tok_count, 1)
    mem_marks = jnp.full((seg_count, mem_count), -1, jnp.int32)
    query_docs = jnp.concatenate([mem_marks, my_docs], axis=1)
    key_docs = jnp.concatenate([mem_marks - 1, doc_ids], axis=1)
    allowed = (
        (query_docs[:, :, None] == key_docs[:, None, :])
        | (query_docs[:, :, None] < 0)
        | (key_docs[:, None, :] < 0)
    )
    allowed = allowed[:, None]
    keys_full = jnp.concatenate([key_rows[:, :mem_count], gathered[..., :model_width]], axis=1)
    values_full = jnp.concatenate([value_rows[:, :mem_count], gathered[..., model_width:]], axis=1)
    keys_all = split_heads(keys_full, head_count)
    values_all = split_heads(values_full, head_count)
    query_heads = split_heads(query_low, head_count)
    scores = (
        jnp.einsum("sqhd,skhd->shqk", query_heads, keys_all, preferred_element_type=jnp.float32)
        * score_scale
    )
    masked = jnp.where(allowed, scores, FLOOR)
    row_top = jnp.max(masked, axis=-1, keepdims=True)
    raised = jnp.exp(masked - row_top)
    row_total = jnp.sum(raised, axis=-1, keepdims=True)
    log_total = row_top + jnp.log(row_total)
    probs_low = (raised / row_total).astype(jnp.bfloat16)
    attended = jnp.einsum(
        "shqk,skhd->sqhd", probs_low, values_all, preferred_element_type=jnp.float32
    )
    attended_low = attended.reshape(seg_count, -1, model_width).astype(jnp.bfloat16)
    resid_one = (
        all_rows.astype(jnp.float32) + project(attended_low, w_out) + b_out.astype(jnp.float32)
    )
    norm_one, back_one = jax.vjp(normalize, resid_one)
    hidden_one = norm_one * norm1_gain.astype(jnp.float32) + norm1_bias.astype(jnp.float32)
    hidden_low = hidden_one.astype(jnp.bfloat16)
    inner = project(hidden_low, w_in) + b_in.astype(jnp.float32)
    activated, back_gelu = jax.vjp(gelu_exact, inner)
    activated_low = activated.astype(jnp.bfloat16)
    resid_two = hidden_one + project(activated_low, w_down) + b_down.astype(jnp.float32)
    norm_two, back_two = jax.vjp(normalize, resid_two)
    result = norm_two * norm2_gain.astype(jnp.float32) + norm2_bias.astype(jnp.float32)
    output = result[:, mem_count:].astype(jnp.bfloat16)
    mem_output = result[:, :mem_count].astype(jnp.bfloat16)
    cot_rows = jnp.concatenate([mem_cot, out_cot], axis=1).astype(jnp.float32)
    row_weight = jnp.concatenate(
        [jnp.full((mem_count,), 1.0, jnp.float32) * lead_flag, jnp.ones((tok_count,), jnp.float32)]
    )[None, :, None]
    weight_low = row_weight.astype(jnp.bfloat16)
    grad_gain2 = jnp.sum(row_weight * cot_rows * norm_two, axis=(0, 1))
    grad_bias2 = jnp.sum(row_weight * cot_rows, axis=(0, 1))
    grad_resid2 = back_two(cot_rows * norm2_gain.astype(jnp.float32))[0]
    grad_bdown = jnp.sum(row_weight * grad_resid2, axis=(0, 1))
    resid2_low = grad_resid2.astype(jnp.bfloat16)
    grad_wdown = outer_sum(activated_low * weight_low, resid2_low)
    grad_inner = back_gelu(project_back(resid2_low, w_down))[0]
    grad_bin = jnp.sum(row_weight * grad_inner, axis=(0, 1))
    inner_low = grad_inner.astype(jnp.bfloat16)
    grad_win = outer_sum(hidden_low * weight_low, inner_low)
    grad_hidden = grad_resid2 + project_back(inner_low, w_in)
    grad_gain1 = jnp.sum(row_weight * grad_hidden * norm_one, axis=(0, 1))
    grad_bias1 = jnp.sum(row_weight * grad_hidden, axis=(0, 1))
    grad_resid1 = back_one(grad_hidden * norm1_gain.astype(jnp.float32))[0]
    ffn_grads = (
        grad_gain1,
        grad_bias1,
        grad_win,
        grad_bin,
        grad_wdown,
        grad_bdown,
        grad_gain2,
        grad_bias2,
    )
    grad_bout = jnp.sum(row_weight * grad_resid1, axis=(0, 1))
    proj_low = grad_resid1.astype(jnp.bfloat16)
    grad_wout = outer_sum(attended_low * weight_low, proj_low)
    att_flat = project_back(proj_low, w_out).astype(jnp.bfloat16)
    grad_att = split_heads(att_flat, head_count)
    keys_back, values_back = (keys_all, values_all)
    scores_back = (
        jnp.einsum("sqhd,skhd->shqk", query_heads, keys_back, preferred_element_type=jnp.float32)
        * score_scale
    )
    probs_back = jnp.exp(jnp.where(allowed, scores_back, FLOOR) - log_total)
    probs_back_low = probs_back.astype(jnp.bfloat16)
    grad_probs = jnp.einsum(
        "sqhd,skhd->shqk", grad_att, values_back, preferred_element_type=jnp.float32
    )
    row_delta = jnp.sum(probs_back * grad_probs, axis=-1, keepdims=True)
    grad_scores = (probs_back * (grad_probs - row_delta)).astype(jnp.bfloat16)
    query_masked = query_heads * weight_low[..., None]
    att_masked = grad_att * weight_low[..., None]
    grad_query = (
        jnp.einsum("shqk,skhd->sqhd", grad_scores, keys_back, preferred_element_type=jnp.float32)
        * score_scale
    )
    grad_query = grad_query.reshape(seg_count, -1, model_width)
    grad_keys = (
        jnp.einsum("shqk,sqhd->skhd", grad_scores, query_masked, preferred_element_type=jnp.float32)
        * score_scale
    )
    grad_values = jnp.einsum(
        "shqk,sqhd->skhd", probs_back_low, att_masked, preferred_element_type=jnp.float32
    )
    grad_keys = grad_keys.reshape(seg_count, -1, model_width)
    grad_values = grad_values.reshape(seg_count, -1, model_width)
    mem_gkeys = grad_keys[:, :mem_count]
    mem_gvalues = grad_values[:, :mem_count]
    tok_kv_grad = jnp.concatenate([grad_keys[:, mem_count:], grad_values[:, mem_count:]], axis=-1)
    tok_kv_sum = lax.psum_scatter(
        tok_kv_grad.astype(jnp.bfloat16), "blk", scatter_dimension=1, tiled=True
    ).astype(jnp.float32)
    mem_part = jnp.concatenate(
        [grad_query[:, :mem_count] * lead_flag, mem_gkeys, mem_gvalues], axis=-1
    )
    mem_sum = lax.psum(mem_part.astype(jnp.bfloat16), "blk").astype(jnp.float32)
    grad_qkv = jnp.concatenate(
        [mem_sum, jnp.concatenate([grad_query[:, mem_count:], tok_kv_sum], axis=-1)], axis=1
    )
    grad_bquery = jnp.sum(row_weight * grad_qkv[..., :model_width], axis=(0, 1))
    grad_bvalue = jnp.sum(row_weight * grad_qkv[..., 2 * model_width :], axis=(0, 1))
    qkv_low = grad_qkv.astype(jnp.bfloat16)
    grad_wqkv = outer_sum(all_rows * weight_low, qkv_low)
    grad_rows = grad_resid1 + project_back(qkv_low, w_qkv)
    grad_tokens = grad_rows[:, mem_count:].astype(jnp.bfloat16)
    grad_mem = grad_rows[:, :mem_count]
    grad_memory = jnp.where(flag_rows, 0.0, grad_mem).astype(jnp.bfloat16)
    grad_init = jnp.sum(jnp.where(flag_rows, grad_mem, 0.0), axis=0) * lead_flag
    attn_grads = (grad_init, grad_wqkv, grad_bquery, grad_bvalue, grad_wout, grad_bout)
    summed = lax.psum(attn_grads + ffn_grads, ("seg", "blk"))
    return (output, mem_output, grad_tokens, grad_memory) + tuple(summed)


def solution(mesh):
    placed = (
        P("seg", "blk", None),
        P("seg", None, None),
        P(),
        P("seg"),
        P("seg", None),
        P(),
        P(),
        P(),
        P(),
        P(),
        P(),
        P(),
        P(),
        P(),
        P(),
        P(),
        P(),
        P(),
        P("seg", "blk", None),
        P("seg", None, None),
    )
    return jax.shard_map(
        local,
        mesh=mesh,
        in_specs=placed,
        out_specs=(
            P("seg", "blk", None),
            P("seg", None, None),
            P("seg", "blk", None),
            P("seg", None, None),
            P(),
            P(),
            P(),
            P(),
            P(),
            P(),
            P(),
            P(),
            P(),
            P(),
            P(),
            P(),
            P(),
            P(),
        ),
        check_vma=False,
    )
```

profile of v0, /device:TPU:1, one launch (start us, length us, event | category | flops | bytes accessed | tf_op | source)
XLA Modules:
  0.0 898.0 jit_solution(9756193462873964558)
XLA Ops:
  10.0 3.9 fusion.84
  22.1 3.1 fusion.42
  25.2 2.7 copy.73
  40.3 49.5 %all-gather.2.cloned.1.call-done = bf16[8,512,1536]{2,1,0:T(8,128)(2,1)} async-done(((bf16[8,64,1536]{2,1,0:T(8,128)(2,1)}), bf16[8,512,1536]{2,1,0:T(8,128)(2,1)}) %all-gather.2.cloned.1.call-update) | async-done | bytes 12582928 | tf_op jit(solution)/shard_map/all_gather | solution.py:78
  89.8 5.6 fusion.82
  95.5 9.4 %pad_maximum_fusion.1 = (bf16[8,532,768]{2,1,0:T(8,128)(2,1)}, bf16[8,532,768]{2,1,0:T(8,128)(2,1)}) fusion(bf16[8,512,768]{2,1,0:T(8,128)(2,1)S(1)} %get-tuple-element.107, bf16[8,20,768]{2,1,0:T(8,128)(2,1)S(1)} %copy-done.23, bf16[8,512,768]{2,1,0:T(8,128)(2,1)S(1)} %get-tuple-element.106, bf16[8,20,768]{2,1,0:T(8,128)(2,1)S(1)} %copy-done.24), kind=kLoop, calls=%fused_computation.37 | loop fusion | flops 26148864 | bytes 26148864 | tf_op jit(solution)/shard_map/concatenate | solution.py:90
  104.8 9.8 %copy.74 = bf16[8,532,768]{1,2,0:T(8,128)(2,1)} copy(bf16[8,532,768]{2,1,0:T(8,128)(2,1)} %get-tuple-element.126) | data formatting | bytes 13074432 | tf_op jit(solution)/shard_map/concatenate | solution.py:89
  114.6 9.8 %copy.71 = bf16[8,532,768]{1,2,0:T(8,128)(2,1)} copy(bf16[8,532,768]{2,1,0:T(8,128)(2,1)} %get-tuple-element.125) | data formatting | bytes 13074432 | tf_op jit(solution)/shard_map/concatenate | solution.py:90
  124.5 15.4 %fusion.12 = (f32[8,12,84]{2,1,0:T(8,128)S(1)}, f32[8,12,84,532]{3,2,1,0:T(8,128)}) fusion(pred[8,84,532]{2,1,0:T(8,128)(4,1)} %or_or_fusion, bf16[8,84,12,64]{1,3,2,0:T(8,128)(2,1)} %bitcast.87, bf16[8,532,12,64]{1,3,2,0:T(8,128)(2,1)} %bitcast.75), kind=kOutput, calls=%fused_computation.35 | convolution fusion | flops 561988224 | bytes 25119360 | tf_op jit(solution)/shard_map/sqhd,skhd->shqk/dot_general | solution.py:95
  139.8 10.7 %fusion = f32[8,12,84]{2,1,0:T(8,128)S(1)} fusion(f32[8,12,84]{2,1,0:T(8,128)S(1)} %get-tuple-element.113, f32[8,12,84,532]{3,2,1,0:T(8,128)} %get-tuple-element.114, pred[8,84,532]{2,1,0:T(8,128)(4,1)S(1)} %copy-done.3), kind=kLoop, calls=%fused_computation.6 | loop fusion | flops 17152128 | bytes 17582208 | tf_op jit(solution)/shard_map/reduce_sum | solution.py:101
  151.2 14.2 %fusion.44 = bf16[8,12,64,84]{3,2,1,0:T(8,128)(2,1)} fusion(bf16[8,532,12,64]{1,3,2,0:T(8,128)(2,1)} %bitcast.77, f32[8,12,84]{2,1,0:T(8,128)} %copy-done.27, f32[8,12,84]{2,1,0:T(8,128)} %copy-done.25, f32[8,12,84,532]{3,2,1,0:T(8,128)} %get-tuple-element.114, pred[8,84,532]{2,1,0:T(8,128)(4,1)} %or_or_fusion), kind=kOutput, calls=%fused_computation.96 | convolution fusion | flops 571092480 | bytes 25151616 | tf_op jit(solution)/shard_map/shqk,skhd->sqhd/dot_general | solution.py:104
  165.4 3.5 fusion.85
  169.3 8.8 fusion.41
  178.1 21.2 %multiply_convert_fusion.2 = (bf16[8,84,3072]{2,1,0:T(8,128)(2,1)S(1)}, f32[8,84,3072]{2,1,0:T(8,128)}) fusion(f32[8,84,3072]{2,1,0:T(8,128)S(1)} %get-tuple-element.117, f32[3072]{0:T(1024)S(1)} %copy-done.31, u8[84,3072]{1,0:T(8,128)(4,1)S(1)} %get-tuple-element.73, u8[84,3072]{1,0:T(8,128)(4,1)S(1)} %get-tuple-element.72), kind=kLoop, calls=%fused_computation.22 | loop fusion | flops 146571264 | bytes 21172224 | tf_op jit(solution)/shard_map/convert_element_type | solution.py:116
  199.4 3.8 fusion.86
  207.8 12.8 %multiply_reduce_fusion.1 = (f32[3072]{0:T(1024)}, bf16[8,84,3072]{2,1,0:T(8,128)(2,1)S(1)}) fusion(f32[84]{0:T(128)S(1)} %copy-done.54, f32[8,84,3072]{2,1,0:T(8,128)} %get-tuple-element.105, bf16[3072,768]{1,0:T(8,128)(2,1)} %param.34, f32[8,84,768]{2,1,0:T(8,128)S(1)} %get-tuple-element.103, f32[8,84]{1,0:T(8,128)S(1)} %negate_multiply_fusion.2, ...), kind=kOutput, calls=%fused_computation.20 | convolution fusion | flops 3207017472 | bytes 27454416 | tf_op jit(solution)/shard_map/sro,io->sri/dot_general | solution.py:29
  220.7 8.6 multiply_reduce_fusion.3
  233.6 2.6 copy.77
  236.1 18.7 %multiply_reduce_fusion = (f32[8,12,84]{2,1,0:T(8,128)}, f32[8,12,84,532]{3,2,1,0:T(8,128)}) fusion(f32[8,12,84]{2,1,0:T(8,128)} %log_add_fusion, f32[8,12,84,532]{3,2,1,0:T(8,128)} %get-tuple-element.114, pred[8,84,532]{2,1,0:T(8,128)(4,1)} %or_or_fusion, bf16[8,84,12,64]{1,3,2,0:T(8,128)(2,1)} %bitcast.89, bf16[8,532,12,64]{1,3,2,0:T(8,128)(2,1)} %bitcast.78), kind=kOutput, calls=%fused_computation.1 | convolution fusion | flops 570568320 | bytes 42311808 | tf_op jit(solution)/shard_map/sqhd,skhd->shqk/dot_general | solution.py:163
  254.8 15.1 %multiply_convert_fusion = bf16[8,12,84,532]{3,2,1,0:T(8,128)(2,1)S(1)} fusion(f32[8,12,84,532]{3,2,1,0:T(8,128)} %get-tuple-element.122, f32[8,12,84]{2,1,0:T(8,128)} %get-tuple-element.121, f32[8,12,84]{2,1,0:T(8,128)} %log_add_fusion, f32[8,12,84,532]{3,2,1,0:T(8,128)} %get-tuple-element.114, pred[8,84,532]{2,1,0:T(8,128)(4,1)} %or_or_fusion), kind=kLoop, calls=%fused_computation | loop fusion | flops 25740288 | bytes 43322496 | tf_op jit(solution)/shard_map/convert_element_type | solution.py:167
  269.9 7.4 convolution_multiply_fusion
  277.3 7.1 multiply_convert_fusion.1
  284.4 13.1 %fusion.13 = bf16[8,12,64,532]{3,2,1,0:T(8,128)(2,1)} fusion(f32[8,12,84]{2,1,0:T(8,128)S(1)} %copy-done.19, f32[8,12,84,532]{3,2,1,0:T(8,128)} %get-tuple-element.114, pred[8,84,532]{2,1,0:T(8,128)(4,1)} %or_or_fusion, bf16[8,84,12,64]{1,3,2,0:T(8,128)(2,1)} %bitcast.90, bf16[84]{0:T(256)(128)(2,1)S(1)} %copy-done.28), kind=kOutput, calls=%fused_computation.36 | convolution fusion | flops 570071040 | bytes 25119528 | tf_op jit(solution)/shard_map/shqk,sqhd->skhd/dot_general | solution.py:179
  297.5 2.8 slice.102
  300.4 9.9 %slice.105 = bf16[8,512,768]{1,2,0:T(8,128)(2,1)} slice(bf16[8,532,768]{1,2,0:T(8,128)(2,1)} %bitcast.84), slice={[0:8], [20:532], [0:768]} | slice | bytes 12582912 | tf_op jit(solution)/shard_map/slice | solution.py:186
  311.7 6.6 slice.106
  318.3 3.1 copy.89
  323.2 2.4 copy.90
  325.6 2.4 copy.91
  330.2 8.6 copy.93
  338.9 8.6 copy.94
  347.5 10.5 %pad_maximum_fusion = bf16[8,512,1536]{2,1,0:T(8,128)(2,1)} fusion(bf16[8,512,768]{2,1,0:T(8,128)(2,1)} %copy.94, bf16[8,512,768]{2,1,0:T(8,128)(2,1)} %copy.93), kind=kLoop, calls=%fused_computation.10 | loop fusion | flops 25165824 | bytes 25165824 | tf_op jit(solution)/shard_map/concatenate | solution.py:186
  358.1 2.8 copy.84
  360.8 4.4 slice.104
  365.3 3.2 copy.92
  368.5 4.8 convolution_bitcast_fusion.3
  373.3 9.2 %convolution_bitcast_fusion = f32[3072,768]{1,0:T(8,128)} fusion(bf16[8,84,3072]{2,1,0:T(8,128)(2,1)} %copy-done.13, bf16[84]{0:T(256)(128)(2,1)S(1)} %copy-done.29, f32[8,84,768]{2,1,0:T(8,128)S(1)} %copy-done.6, f32[8,84]{1,0:T(8,128)S(1)} %copy-done.34), kind=kOutput, calls=%fused_computation.40 | convolution fusion | flops 3173990400 | bytes 15633192 | tf_op jit(solution)/shard_map/sri,sro->io/dot_general | solution.py:33
  382.5 6.8 convolution_bitcast_fusion.1
  389.9 2.5 convert_element_type.129
  392.3 73.3 %reduce-scatter.2.cloned.1.call-done = bf16[8,64,1536]{2,1,0:T(8,128)(2,1)} async-done(((bf16[8,512,1536]{2,1,0:T(8,128)(2,1)}), bf16[8,64,1536]{2,1,0:T(8,128)(2,1)}) %reduce-scatter.2.cloned.1.call-update) | async-done | bytes 1572880 | tf_op jit(solution)/shard_map/reduce_scatter | solution.py:187
  470.8 2.9 add_add_fusion.4
  476.3 9.3 %convolution_bitcast_fusion.2 = f32[768,2304]{1,0:T(8,128)} fusion(bf16[84]{0:T(256)(128)(2,1)S(1)} %copy-done.30, bf16[8,64,768]{2,1,0:T(8,128)(2,1)} %param.20, bf16[8,20,768]{2,1,0:T(8,128)(2,1)} %copy-done.21, f32[8,64,1536]{2,1,0:T(8,128)} %copy-done.4, f32[8,64,768]{2,1,0:T(8,128)} %copy.92, f32[8,20,2304]{2,1,0:T(8,128)} %convert_element_type.129), kind=kOutput, calls=%fused_computation.42 | convolution fusion | flops 2390556672 | bytes 14303400 | tf_op jit(solution)/shard_map/sri,sro->io/dot_general | solution.py:33
  489.6 2.5 slice.123
  494.0 127.1 %all-reduce.11.cloned.1.call-done = (f32[20,768]{1,0:T(8,128)}, f32[768]{0:T(1024)}, f32[768]{0:T(1024)}, f32[768]{0:T(1024)}, f32[768]{0:T(1024)}, /*index=5*/f...) async-done(((f32[20,768]{1,0:T(8,128)}, f32[768]{0:T(1024)}, f32[768]{0:T(1024)}, f32[768]{0:T(1024)}, f32[768]{0:T(1024)}, ...) | async-done | bytes 98320 | tf_op jit(solution)/shard_map/psum | solution.py:207
  621.0 242.8 %all-reduce.13.cloned.1.call-done = (f32[768,2304]{1,0:T(8,128)}, f32[768,768]{1,0:T(8,128)}, f32[768,3072]{1,0:T(8,128)}, f32[3072,768]{1,0:T(8,128)}) async-done(((f32[768,2304]{1,0:T(8,128)}, f32[768,768]{1,0:T(8,128)}, f32[768,3072]{1,0:T(8,128)}, f32[3072,768]{1,0:T(8,128)}), (f32[768,2304]{1,0:T(8,128)}, f32[768,768]{1,0:T(8,128)}, f32[768,3072]{1,0:T(8,128)}, ...) | async-done | bytes 28311568 | tf_op jit(solution)/shard_map/psum | solution.py:207
  865.3 6.6 copy.115
  876.3 8.8 copy.122
  885.7 3.7 copy.124
  (211 shorter events, 61.1 us)
Async XLA Ops:
  7.2 82.6 %all-gather.2.cloned.1.call-start = ((), (), s32[]{:S(2)}) async-start(), calls=%async_computation.1 | async-start | bytes 14155776 | tf_op jit(solution)/shard_map/all_gather | solution.py:78
  10.0 4.0 copy-start.21
  16.8 5.3 copy-start.52
  18.4 9.5 %copy-start.53 = (bf16[768]{0:T(1024)(128)(2,1)S(1)}, bf16[768]{0:T(1024)(128)(2,1)}, u32[]{:S(2)}) copy-start(bf16[768]{0:T(1024)(128)(2,1)} %param.29) | copy-start | bytes 4612
  18.4 10.2 %copy-start.40 = (bf16[3072]{0:T(1024)(128)(2,1)S(1)}, bf16[3072]{0:T(1024)(128)(2,1)}, u32[]{:S(2)}) copy-start(bf16[3072]{0:T(1024)(128)(2,1)} %param.33) | copy-start | bytes 18436
  18.5 371.4 %all-reduce.9.cloned.1.call-start = ((), (), s32[]{:S(2)}) async-start(), calls=%async_computation.2 | async-start | bytes 1769472 | tf_op jit(solution)/shard_map/psum | solution.py:193
  89.8 5.7 copy-start.23
  89.8 5.7 copy-start.24
  124.4 15.4 %copy-start.3 = (pred[8,84,532]{2,1,0:T(8,128)(4,1)S(1)}, pred[8,84,532]{2,1,0:T(8,128)(4,1)}, u32[]{:S(2)}) copy-start(pred[8,84,532]{2,1,0:T(8,128)(4,1)} %or_or_fusion) | copy-start | bytes 1072516
  139.8 10.8 %copy-start.25 = (f32[8,12,84]{2,1,0:T(8,128)}, f32[8,12,84]{2,1,0:T(8,128)S(1)}, u32[]{:S(2)}) copy-start(f32[8,12,84]{2,1,0:T(8,128)S(1)} %get-tuple-element.113) | copy-start | bytes 96772
  165.4 3.9 copy-start.31
  165.4 33.9 %slice-start.7 = ((s8[4718592]{0:T(1024)(128)(4,1)}), s8[4194304]{0:T(1024)(128)(4,1)S(1)}, s32[]{:S(2)}) async-start(s8[4718592]{0:T(1024)(128)(4,1)} %bitcast.97), calls=%async_computation.13 | async-start | bytes 8388608
  168.9 60.4 %copy-start.1 = (f32[8,84,768]{2,1,0:T(8,128)}, f32[8,84,768]{2,1,0:T(8,128)S(1)}, u32[]{:S(2)}) copy-start(f32[8,84,768]{2,1,0:T(8,128)S(1)} %get-tuple-element.116) | copy-start | bytes 6193156
  169.3 30.0 %slice-start.8 = ((s8[4718592]{0:T(1024)(128)(4,1)}), s8[524288]{0:T(1024)(128)(4,1)S(1)}, s32[]{:S(2)}) async-start(s8[4718592]{0:T(1024)(128)(4,1)} %bitcast.97), calls=%async_computation.14 | async-start | bytes 1048576
  178.1 21.2 %copy-start.8 = (f32[8,84,3072]{2,1,0:T(8,128)}, f32[8,84,3072]{2,1,0:T(8,128)S(1)}, u32[]{:S(2)}) copy-start(f32[8,84,3072]{2,1,0:T(8,128)S(1)} %get-tuple-element.117) | copy-start | bytes 24772612
  178.1 21.2 %copy-start.43 = (f32[768]{0:T(1024)S(1)}, f32[768]{0:T(1024)}, u32[]{:S(2)}) copy-start(f32[768]{0:T(1024)} %convert_element_type.117) | copy-start | bytes 9220
  199.3 3.9 copy-start.13
  199.3 4.3 copy-start.16
  199.4 4.3 copy-start.17
  199.4 4.3 copy-start.32
  199.4 4.3 copy-start.54
  207.8 12.9 %copy-start.5 = (f32[8,84,768]{2,1,0:T(8,128)}, f32[8,84,768]{2,1,0:T(8,128)S(1)}, u32[]{:S(2)}) copy-start(f32[8,84,768]{2,1,0:T(8,128)S(1)} %get-tuple-element.103) | copy-start | bytes 6193156
  207.8 12.9 %copy-start.33 = (f32[8,84]{1,0:T(8,128)}, f32[8,84]{1,0:T(8,128)S(1)}, u32[]{:S(2)}) copy-start(f32[8,84]{1,0:T(8,128)S(1)} %negate_multiply_fusion.2) | copy-start | bytes 8068
  220.7 8.6 copy-start.15
  269.9 7.4 copy-start.28
  277.3 7.1 copy-start.19
  297.5 12.7 %slice-start = ((s8[7864320]{0:T(1024)(128)(4,1)}), s8[4194304]{0:T(1024)(128)(4,1)S(1)}, s32[]{:S(2)}) async-start(s8[7864320]{0:T(1024)(128)(4,1)} %bitcast.79), calls=%async_computation.6 | async-start | bytes 8388608
  300.4 9.9 %slice-start.1 = ((s8[7864320]{0:T(1024)(128)(4,1)}), s8[3670016]{0:T(1024)(128)(4,1)S(1)}, s32[]{:S(2)}) async-start(s8[7864320]{0:T(1024)(128)(4,1)} %bitcast.79), calls=%async_computation.7 | async-start | bytes 7340032
  330.2 135.4 %reduce-scatter.2.cloned.1.call-start = ((), (), s32[]{:S(2)}) async-start(), calls=%async_computation.3 | async-start | bytes 14155776 | tf_op jit(solution)/shard_map/reduce_scatter | solution.py:187
  358.0 263.0 %all-reduce.11.cloned.1.call-start = ((), (), s32[]{:S(2)}) async-start(), calls=%async_computation.4 | async-start | bytes 237568 | tf_op jit(solution)/shard_map/psum | solution.py:207
  368.5 4.8 copy-start.6
  368.5 4.8 copy-start.29
  368.5 4.8 copy-start.34
  368.5 14.0 %slice-start.5 = ((s8[4325376]{0:T(1024)(128)(4,1)}), s8[4194304]{0:T(1024)(128)(4,1)S(1)}, s32[]{:S(2)}) async-start(s8[4325376]{0:T(1024)(128)(4,1)} %bitcast.95), calls=%async_computation.11 | async-start | bytes 8388608
  373.3 9.2 %copy-start.2 = (f32[8,84,768]{2,1,0:T(8,128)S(1)}, f32[8,84,768]{2,1,0:T(8,128)}, u32[]{:S(2)}) copy-start(f32[8,84,768]{2,1,0:T(8,128)} %copy-done.1) | copy-start | bytes 6193156
  373.3 9.2 %slice-start.6 = ((s8[4325376]{0:T(1024)(128)(4,1)}), s8[131072]{0:T(1024)(128)(4,1)S(1)}, s32[]{:S(2)}) async-start(s8[4325376]{0:T(1024)(128)(4,1)} %bitcast.95), calls=%async_computation.12 | async-start | bytes 262144
  476.0 387.8 %all-reduce.13.cloned.1.call-start = ((), (), s32[]{:S(2)}) async-start(), calls=%async_computation.5 | async-start | bytes 56623104 | tf_op jit(solution)/shard_map/psum | solution.py:207
  865.3 6.6 copy-start.51
  865.3 7.2 copy-start.50
  865.3 7.8 copy-start.18
  871.9 3.8 copy-start.47
  873.1 12.6 %slice-start.2 = ((s8[9437184]{0:T(1024)(128)(4,1)}), s8[4194304]{0:T(1024)(128)(4,1)S(1)}, s32[]{:S(2)}) async-start(s8[9437184]{0:T(1024)(128)(4,1)} %bitcast.91), calls=%async_computation.8 | async-start | bytes 8388608
  876.3 8.8 copy-start.39
  876.3 9.4 %slice-start.3 = ((s8[9437184]{0:T(1024)(128)(4,1)}), s8[4194304]{0:T(1024)(128)(4,1)S(1)}, s32[]{:S(2)}) async-start(s8[9437184]{0:T(1024)(128)(4,1)} %bitcast.91), calls=%async_computation.9 | async-start | bytes 8388608
  876.3 9.4 %slice-start.4 = ((s8[9437184]{0:T(1024)(128)(4,1)}), s8[1048576]{0:T(1024)(128)(4,1)S(1)}, s32[]{:S(2)}) async-start(s8[9437184]{0:T(1024)(128)(4,1)} %bitcast.91), calls=%async_computation.10 | async-start | bytes 2097152
  885.7 3.8 copy-start.46
  885.7 4.4 copy-start.45
  885.7 5.0 copy-start.44
  (22 other events, 47.3 us)
Sparse Core Ops, SparseCore 0:
  18.6 71.1 all-gather.1
  330.3 59.4 all-reduce.8
  392.4 73.1 reduce-scatter.1
  476.1 144.8 all-reduce.10
  628.3 235.4 all-reduce.12
where the time goes:
time: 903 us; the launch traced here: 898 us
  waiting for transfers between devices  493 us (55%)
  matrix products  152 us (17%)
  local copies, waits for them, and re-layouts  135 us (15%)
  other arithmetic  103 us (11%)
  between operations  14.7 us (2%)
    psum x2, waiting for transfers between devices, local(): summed = lax.psum(attn_grads + ffn_grads, ('seg', 'blk'))  370 us
    reduce_scatter x1, waiting for transfers between devices, local(): lax.psum_scatter(tok_kv_grad.astype(jnp.bfloat16), 'blk', scatter_dimensi...  73.3 us
    unnamed x153, local copies, waits for them, and re-layouts  64.1 us
    all_gather x1, waiting for transfers between devices, local(): gathered = lax.all_gather(local_kv, 'blk', axis=1, tiled=True)  49.5 us
    dot_general x4, matrix products, outer_sum(): jnp.einsum('sri,sro->io', left, right, preferred_element_type=jnp.float32)  30.1 us
    dot_general x4, matrix products, project_back(): jnp.einsum('sro,io->sri', left, right, preferred_element_type=jnp.float32)  26.4 us
    convert_element_type x1, other arithmetic, local(): activated_low = activated.astype(jnp.bfloat16)  21.2 us
    dot_general x4, matrix products, project(): jnp.einsum('sri,io->sro', left, right, preferred_element_type=jnp.float32)  20 us
  transfers between devices with their start and end apart: 5, of which 5 were waited for; matrix products, arithmetic and copies ran while one was open for 11% of the time, Pallas kernels for 0%

commit v1 on v0

v1 whole, which is shorter than its diff:
```python
import jax
import jax.numpy as jnp
from jax import lax
from jax.sharding import Mesh, PartitionSpec as P

HEADS = 12

EPS = 1e-12
FLOOR = -1000000000.0

F32 = jnp.float32
BF16 = jnp.bfloat16
BLK = ("z", "core")
SEG = ("y", "x")
ALL = ("y", "x", "z", "core")


def norm_parts(value):
    centre = jnp.mean(value, axis=-1, keepdims=True)
    centered = value - centre
    spread = jnp.mean(centered * centered, axis=-1, keepdims=True)
    scale = lax.rsqrt(spread + EPS)
    return centered * scale, scale


def norm_back(grad, normal, scale):
    mean_grad = jnp.mean(grad, axis=-1, keepdims=True)
    mean_prod = jnp.mean(grad * normal, axis=-1, keepdims=True)
    return scale * (grad - mean_grad - normal * mean_prod)


def dot(left, right):
    return jnp.dot(left, right, preferred_element_type=F32)


def dot_nt(left, right):
    return lax.dot_general(left, right, (((1,), (1,)), ((), ())), preferred_element_type=F32)


def dot_tn(left, right):
    return lax.dot_general(left, right, (((0,), (0,)), ((), ())), preferred_element_type=F32)


def to_segments(value):
    return lax.all_to_all(value, BLK, 0, 1, tiled=True)[0]


def to_blocks(value, seg_count):
    parts = value.reshape(seg_count, value.shape[0] // seg_count, value.shape[1])
    return lax.all_to_all(parts, BLK, 0, 0, tiled=True)


def heads(value):
    return value.reshape(value.shape[0], HEADS, -1).transpose(1, 0, 2)


def unheads(value):
    return value.transpose(1, 0, 2).reshape(value.shape[1], -1)


def local(
    tokens,
    memory,
    mem_init,
    reset_flags,
    doc_ids,
    w_qkv,
    b_query,
    b_value,
    w_out,
    b_out,
    norm1_gain,
    norm1_bias,
    w_in,
    b_in,
    w_down,
    b_down,
    norm2_gain,
    norm2_bias,
    out_cot,
    mem_cot,
):
    seg_count, tok_count, width = tokens.shape
    mem_count = memory.shape[1]
    score_scale = (width // HEADS) ** (-0.5)
    place = lax.axis_index(BLK)
    pick = lambda value: lax.dynamic_index_in_dim(value, place, 0, keepdims=False)
    my_flag = pick(reset_flags) == 1
    my_docs = pick(doc_ids)
    mem_rows = jnp.where(my_flag, mem_init, pick(memory))
    rows = jnp.concatenate([to_segments(tokens), mem_rows], axis=0)
    cot = jnp.concatenate([to_segments(out_cot), pick(mem_cot)], axis=0).astype(F32)

    text_count = rows.shape[0] - mem_count
    qkv = dot(rows, w_qkv)
    query = heads((qkv[:, :width] + b_query.astype(F32)).astype(BF16))
    key = heads(qkv[:, width : 2 * width].astype(BF16))
    value = heads((qkv[:, 2 * width :] + b_value.astype(F32)).astype(BF16))
    query_docs = jnp.concatenate([my_docs, jnp.full((mem_count,), -1, jnp.int32)])
    allowed = (
        (query_docs[:, None] == query_docs[None, :])
        | (query_docs[:, None] < 0)
        | (query_docs[None, :] < 0)
    )[None]
    scores = jnp.einsum("hqd,hkd->hqk", query, key, preferred_element_type=F32) * score_scale
    masked = jnp.where(allowed, scores, FLOOR)
    top = jnp.max(masked, axis=-1, keepdims=True)
    raised = jnp.exp(masked - top)
    total = jnp.sum(raised, axis=-1, keepdims=True)
    probs = raised / total
    probs_low = probs.astype(BF16)
    attended = unheads(
        jnp.einsum("hqk,hkd->hqd", probs_low, value, preferred_element_type=F32).astype(BF16)
    )
    resid_one = rows.astype(F32) + dot(attended, w_out) + b_out.astype(F32)
    norm_one, scale_one = norm_parts(resid_one)
    hidden = norm_one * norm1_gain.astype(F32) + norm1_bias.astype(F32)
    hidden_low = hidden.astype(BF16)
    inner = dot(hidden_low, w_in) + b_in.astype(F32)
    phi = 0.5 * (1.0 + lax.erf(inner * (0.5**0.5)))
    activated = (inner * phi).astype(BF16)
    slope = phi + inner * jnp.exp(-0.5 * inner * inner) * 0.3989422804014327
    resid_two = hidden + dot(activated, w_down) + b_down.astype(F32)
    norm_two, scale_two = norm_parts(resid_two)
    result = (norm_two * norm2_gain.astype(F32) + norm2_bias.astype(F32)).astype(BF16)
    output = to_blocks(result[:text_count], seg_count)
    mem_output = lax.all_gather(result[text_count:], BLK, axis=0)

    grad_gain2 = jnp.sum(cot * norm_two, axis=0)
    grad_bias2 = jnp.sum(cot, axis=0)
    g_two = norm_back(cot * norm2_gain.astype(F32), norm_two, scale_two)
    grad_bdown = jnp.sum(g_two, axis=0)
    g_two_low = g_two.astype(BF16)
    grad_wdown = dot_tn(activated, g_two_low).astype(BF16)
    grad_wdown = lax.psum(grad_wdown, ALL)
    g_inner = dot_nt(g_two_low, w_down) * slope
    grad_bin = jnp.sum(g_inner, axis=0)
    g_inner_low = g_inner.astype(BF16)
    grad_win = dot_tn(hidden_low, g_inner_low).astype(BF16)
    grad_wdown, grad_win = lax.optimization_barrier((grad_wdown, grad_win))
    grad_win = lax.psum(grad_win, ALL)
    g_hidden = g_two + dot_nt(g_inner_low, w_in)
    grad_gain1 = jnp.sum(g_hidden * norm_one, axis=0)
    grad_bias1 = jnp.sum(g_hidden, axis=0)
    g_one = norm_back(g_hidden * norm1_gain.astype(F32), norm_one, scale_one)
    grad_bout = jnp.sum(g_one, axis=0)
    g_one_low = g_one.astype(BF16)
    grad_wout = dot_tn(attended, g_one_low).astype(BF16)
    g_att = heads(dot_nt(g_one_low, w_out).astype(BF16))
    g_probs = jnp.einsum("hqd,hkd->hqk", g_att, value, preferred_element_type=F32)
    delta = jnp.sum(probs * g_probs, axis=-1, keepdims=True)
    g_scores = (probs * (g_probs - delta)).astype(BF16)
    g_query = jnp.einsum("hqk,hkd->hqd", g_scores, key, preferred_element_type=F32) * score_scale
    g_key = jnp.einsum("hqk,hqd->hkd", g_scores, query, preferred_element_type=F32) * score_scale
    g_value = jnp.einsum("hqk,hqd->hkd", probs_low, g_att, preferred_element_type=F32)
    g_query, g_value = unheads(g_query), unheads(g_value)
    grad_bquery = jnp.sum(g_query, axis=0)
    grad_bvalue = jnp.sum(g_value, axis=0)
    g_qkv = jnp.concatenate(
        [g_query.astype(BF16), unheads(g_key).astype(BF16), g_value.astype(BF16)], axis=1
    )
    grad_wqkv = dot_tn(rows, g_qkv).astype(BF16)
    g_rows = g_one + dot_nt(g_qkv, w_qkv)
    grad_tokens = to_blocks(g_rows[:text_count].astype(BF16), seg_count)
    grad_mem = g_rows[text_count:]
    grad_memory = lax.all_gather(jnp.where(my_flag, 0.0, grad_mem).astype(BF16), BLK, axis=0)
    grad_init = jnp.where(my_flag, grad_mem, 0.0)
    small = jnp.concatenate(
        [
            grad_init.reshape(-1),
            grad_bquery,
            grad_bvalue,
            grad_bout,
            grad_gain1,
            grad_bias1,
            grad_bin,
            grad_bdown,
            grad_gain2,
            grad_bias2,
        ]
    )
    tail = jnp.concatenate([grad_wout, small.astype(BF16).reshape(-1, width)], axis=0)
    grad_win, grad_wqkv, tail = lax.optimization_barrier((grad_win, grad_wqkv, tail))
    grad_wqkv, tail = lax.psum((grad_wqkv, tail), ALL)
    grad_wout = tail[:width]
    small = tail[width:].astype(F32).reshape(-1)
    sizes = [mem_count * width] + [width] * 5 + [w_in.shape[1]] + [width] * 3
    pieces, start = [], 0
    for size in sizes:
        pieces.append(small[start : start + size])
        start += size
    return (
        output,
        mem_output,
        grad_tokens,
        grad_memory,
        pieces[0].reshape(mem_count, width),
        grad_wqkv.astype(F32),
        pieces[1],
        pieces[2],
        grad_wout.astype(F32),
        pieces[3],
        pieces[4],
        pieces[5],
        grad_win.astype(F32),
        pieces[6],
        grad_wdown.astype(F32),
        pieces[7],
        pieces[8],
        pieces[9],
    )


def solution(mesh):
    chips = Mesh(mesh.devices.reshape(4, 4, 4, 2), ALL)
    placed = (
        P(SEG, BLK, None),
        P(SEG, None, None),
        P(),
        P(SEG),
        P(SEG, None),
        *([P()] * 13),
        P(SEG, BLK, None),
        P(SEG, None, None),
    )
    return jax.shard_map(
        local,
        mesh=chips,
        in_specs=placed,
        out_specs=(
            P(SEG, BLK, None),
            P(SEG, None, None),
            P(SEG, BLK, None),
            P(SEG, None, None),
            *([P()] * 14),
        ),
        check_vma=False,
    )
```

time: 903 us -> 650 us (0.72)
  waiting for transfers between devices: 493 us -> 337 us
  local copies, waits for them, and re-layouts: 135 us -> 51.5 us
  other arithmetic: 103 us -> 66.9 us
  matrix products: 152 us -> 116 us
  blocking collectives: 0 us -> 35.3 us
  starting transfers between devices: 0.59 us -> 22.6 us
    reduce_scatter x1 -> x0, waiting for transfers between devices: 73.3 us -> none  [local(): lax.psum_scatter(tok_kv_grad.astype(jnp.bfloat16), 'blk', scatter_dimensi...]
    all_gather x1 -> x0, waiting for transfers between devices: 49.5 us -> none  [local(): gathered = lax.all_gather(local_kv, 'blk', axis=1, tiled=True)]
    dot_general x18 -> x17, matrix products: 152 us -> 105 us  [the longest x4 25.5 us: dot_tn(): lax.dot_general(left, right, (((0,), (0,)), ((), ())), preferred_element_...]
    psum x3, waiting for transfers between devices: 370 us -> 326 us  [the longest x1 127 us: local(): grad_wdown = lax.psum(grad_wdown, ALL)]
    unnamed x153 -> x95, local copies, waits for them, and re-layouts: 64.1 us -> 26.9 us
    all_gather x0 -> x2, blocking collectives: none -> 35.3 us  [the longest x1 22.4 us: local(): lax.all_gather(jnp.where(my_flag, 0.0, grad_mem).astype(BF16), BLK, axis=0)]
    slice x13 -> x8, local copies, waits for them, and re-layouts: 40.3 us -> 9.22 us  [the longest x2 3.19 us: local(): key = heads(qkv[:, width:2 * width].astype(BF16))]
    concatenate x5 -> x1, other arithmetic: 24 us -> 1.11 us  [local(): jnp.concatenate([grad_wout, small.astype(BF16).reshape(-1, width)], axis=0)]
  transfers between devices with their start and end apart: 5 -> 7, of which waited for: 5 -> 4; matrix products, arithmetic and copies ran while one was open for 11% -> 24% of each run, Pallas kernels for 0% -> 0%
where the time goes in v1:
time: 650 us; the launch traced here: 645 us
  waiting for transfers between devices  337 us (52%)
  matrix products  116 us (18%)
  other arithmetic  66.9 us (10%)
  local copies, waits for them, and re-layouts  51.5 us (8%)
  blocking collectives  35.3 us (5%)
  starting transfers between devices  22.6 us (3%)
  between operations  15.1 us (2%)
    psum x1, waiting for transfers between devices, local(): grad_wdown = lax.psum(grad_wdown, ALL)  127 us
    psum x1, waiting for transfers between devices, local(): grad_win = lax.psum(grad_win, ALL)  112 us
    psum x1, waiting for transfers between devices, local(): grad_wqkv, tail = lax.psum((grad_wqkv, tail), ALL)  86.2 us
    unnamed x95, local copies, waits for them, and re-layouts  26.9 us
    dot_general x4, matrix products, dot_tn(): lax.dot_general(left, right, (((0,), (0,)), ((), ())), preferred_element_...  25.5 us
    all_gather x1, blocking collectives, local(): lax.all_gather(jnp.where(my_flag, 0.0, grad_mem).astype(BF16), BLK, axis=0)  22.4 us
    dot_general x4, matrix products, dot_nt(): lax.dot_general(left, right, (((1,), (1,)), ((), ())), preferred_element_...  18.2 us
    dot_general x4, matrix products, dot(): return jnp.dot(left, right, preferred_element_type=F32)  16.6 us
  transfers between devices with their start and end apart: 7, of which 4 were waited for; matrix products, arithmetic and copies ran while one was open for 24% of the time, Pallas kernels for 0%

profile of v1, /device:TPU:1, one launch (start us, length us, event | category | flops | bytes accessed | tf_op | source)
XLA Modules:
  0.0 644.8 jit_solution(2741396919392372065)
XLA Ops:
  7.2 7.1 %all-to-all-start = ((bf16[8,64,768]{2,1,0:T(8,128)(2,1)}), bf16[8,64,768]{2,1,0:T(8,128)(2,1)}, u32[]{:S(2)}, u32[]{:S(2)}) async-start(bf16[8,64,768]{2,1,0:T(8,128)(2,1)} %param.20), calls=%async_computation | async-start | bytes 1572864 | tf_op jit(solution)/shard_map/all_to_all | solution.py:45
  14.3 1.6 fusion.50
  31.1 5.0 all-to-all-start.2
  36.1 3.2 fusion.39
  41.8 2.4 copy.61
  44.2 2.2 copy.62
  46.4 2.2 copy.63
  48.6 11.0 %fusion.54 = (f32[12,532]{1,0:T(8,128)}, f32[12,532,532]{1,2,0:T(8,128)}) fusion(bf16[12,532,64]{1,2,0:T(8,128)(2,1)} %bitcast.73, bf16[12,532,64]{1,2,0:T(8,128)(2,1)} %bitcast.69, pred[532,532]{0,1:T(8,128)(4,1)} %or_or_fusion), kind=kOutput, calls=%fused_computation.116 | convolution fusion | flops 448310528 | bytes 15528016 | tf_op jit(solution)/shard_map/sub | solution.py:108
  59.6 8.6 %fusion.28 = bf16[12,532,64]{1,2,0:T(8,128)(2,1)} fusion(bf16[12,532,64]{1,2,0:T(8,128)(2,1)} %bitcast.75, f32[12,532,532]{1,2,0:T(8,128)} %get-tuple-element.111, f32[12,532]{1,0:T(8,128)} %get-tuple-element.110), kind=kOutput, calls=%fused_computation.62 | convolution fusion | flops 441926016 | bytes 15244992 | tf_op jit(solution)/shard_map/hqk,hkd->hqd/dot_general | solution.py:113
  68.2 2.8 fusion.55
  71.5 7.6 %multiply_convert_fusion.1 = (bf16[532,3072]{1,0:T(8,128)(2,1)S(1)}, f32[532,3072]{1,0:T(8,128)}) fusion(f32[3072]{0:T(1024)S(1)} %copy-done.22, bf16[768,3072]{1,0:T(8,128)(2,1)} %param.32, f32[532,768]{1,0:T(8,128)S(1)} %get-tuple-element.113, f32[768]{0:T(1024)S(1)} %copy-done.27, f32[768]{0:T(1024)S(1)} %copy-done.18, f32[532]{0:T(1024)S(1)} %add_rsqrt_fusion.1, ...), kind=kOutput, calls=%fused_computation.17 | convolution fusion | flops 2522139648 | bytes 16181408 | tf_op jit(solution)/shard_map/dot_general | solution.py:33
  79.1 2.9 fusion.56
  83.6 3.2 fusion.22
  86.8 3.5 fusion.51
  90.3 8.9 %fusion.57 = (bf16[3072]{0:T(1024)(128)(2,1)}, bf16[532,3072]{1,0:T(8,128)(2,1)S(1)}) fusion(f32[532,3072]{1,0:T(8,128)} %get-tuple-element.115, f32[3072]{0:T(1024)S(1)} %copy-done.23, bf16[3072,768]{1,0:T(8,128)(2,1)} %param.34, f32[532,768]{1,0:T(8,128)S(1)} %get-tuple-element.102), kind=kOutput, calls=%fused_computation.119 | convolution fusion | flops 2530308096 | bytes 16177152 | tf_op jit(solution)/shard_map/dot_general | solution.py:37
  99.3 4.9 multiply_reduce_fusion.1
  104.2 6.2 convolution_convert_fusion.1
  110.4 8.6 %convolution_convert_fusion.2 = bf16[3072,768]{1,0:T(8,128)(2,1)} fusion(bf16[532,3072]{1,0:T(8,128)(2,1)} %copy-done.35, f32[532,768]{1,0:T(8,128)} %copy-done.7), kind=kOutput, calls=%fused_computation.21 | convolution fusion | flops 2513058816 | bytes 9621504 | tf_op jit(solution)/shard_map/dot_general | solution.py:41
  120.3 3.1 fusion.53
  124.7 1.8 convolution_convert_fusion.4
  126.4 2.2 copy.66
  128.6 15.4 %multiply_reduce_fusion = (f32[12,532]{1,0:T(8,128)}, f32[12,532,532]{1,2,0:T(8,128)}) fusion(f32[12,532,532]{1,2,0:T(8,128)} %get-tuple-element.111, f32[12,532]{1,0:T(8,128)} %get-tuple-element.110, bf16[12,532,64]{1,2,0:T(8,128)(2,1)} %bitcast.77, bf16[12,532,64]{1,2,0:T(8,128)(2,1)} %bitcast.76), kind=kOutput, calls=%fused_computation.2 | convolution fusion | flops 444907328 | bytes 28855680 | tf_op jit(solution)/shard_map/hqd,hkd->hqk/dot_general | solution.py:150
  144.1 12.2 %multiply_convert_fusion = bf16[12,532,532]{1,2,0:T(8,128)(2,1)S(1)} fusion(f32[12,532,532]{1,2,0:T(8,128)} %get-tuple-element.122, f32[12,532]{1,0:T(8,128)} %get-tuple-element.121, f32[12,532,532]{1,2,0:T(8,128)} %get-tuple-element.111, f32[12,532]{1,0:T(8,128)} %get-tuple-element.110), kind=kLoop, calls=%fused_computation.1 | loop fusion | flops 13585152 | bytes 34013952 | tf_op jit(solution)/shard_map/convert_element_type | solution.py:152
  156.3 3.3 copy-done.1
  159.6 3.7 multiply_convert_fusion.2
  163.3 10.5 %bitcast_convert_fusion = (bf16[532,12,64]{0,2,1:T(8,128)(2,1)}, f32[12,532,64]{1,2,0:T(8,128)}) fusion(bf16[12,532,64]{1,2,0:T(8,128)(2,1)} %bitcast.78, f32[12,532,532]{1,2,0:T(8,128)} %get-tuple-element.111, f32[12,532]{1,0:T(8,128)} %get-tuple-element.110), kind=kOutput, calls=%fused_computation.33 | convolution fusion | flops 441926016 | bytes 16879296 | tf_op jit(solution)/shard_map/hqk,hqd->hkd/dot_general | solution.py:155
  173.8 127.3 %all-reduce.6.cloned.1.call-done = bf16[3072,768]{1,0:T(8,128)(2,1)} async-done(((bf16[3072,768]{1,0:T(8,128)(2,1)}), bf16[3072,768]{1,0:T(8,128)(2,1)}) %all-reduce.6.cloned.1.call-update) | async-done | bytes 4718608 | tf_op jit(solution)/shard_map/psum | solution.py:135
  301.3 6.7 %bitcast_convert_fusion.1 = (bf16[532,12,64]{0,2,1:T(8,128)(2,1)S(1)}, f32[12,532,64]{1,2,0:T(8,128)}) fusion(bf16[12,532,532]{1,2,0:T(8,128)(2,1)} %copy-done.1, bf16[12,532,64]{1,2,0:T(8,128)(2,1)} %bitcast.70), kind=kOutput, calls=%fused_computation.35 | convolution fusion | flops 435542016 | bytes 10061184 | tf_op jit(solution)/shard_map/hqk,hkd->hqd/dot_general | solution.py:153
  308.0 2.6 convolution_add_fusion
  313.0 1.9 bitcast_reduce_fusion.1
  315.6 1.7 bitcast_reduce_fusion
  335.7 3.0 convolution_convert_fusion.3
  340.7 7.8 %convolution_convert_fusion = bf16[768,2304]{1,0:T(8,128)(2,1)} fusion(bf16[532,768]{0,1:T(8,128)(2,1)S(1)} %bitcast.94, bf16[532,768]{0,1:T(8,128)(2,1)S(1)} %bitcast.92, bf16[532,768]{0,1:T(8,128)(2,1)S(1)} %bitcast.80, bf16[20,768]{1,0:T(8,128)(2,1)S(1)} %copy-done.16, bf16[512,768]{1,0:T(8,128)(2,1)} %bitcast), kind=kOutput, calls=%fused_computation.19 | convolution fusion | flops 1893476352 | bytes 6807552 | tf_op jit(solution)/shard_map/dot_general | solution.py:41
  348.5 112.0 %all-reduce.8.cloned.1.call-done = bf16[768,3072]{1,0:T(8,128)(2,1)} async-done(((bf16[768,3072]{1,0:T(8,128)(2,1)}), bf16[768,3072]{1,0:T(8,128)(2,1)}) %all-reduce.8.cloned.1.call-update) | async-done | bytes 4718608 | tf_op jit(solution)/shard_map/psum | solution.py:141
  460.6 2.1 slice.158
  462.6 5.1 all-to-all-start.3
  467.8 2.1 slice.118
  469.8 11.7 %all-to-all-done.3 = bf16[8,64,768]{2,1,0:T(8,128)(2,1)} async-done(((bf16[8,64,768]{2,1,0:T(8,128)(2,1)}), bf16[8,64,768]{2,1,0:T(8,128)(2,1)}, u32[]{:S(2)}, u32[]{:S(2)}) %all-to-all-start.3) | async-done | bytes 786464 | tf_op jit(solution)/shard_map/all_to_all | solution.py:50
  481.5 5.3 all-to-all-start.1
  486.8 22.4 %all-gather.3 = bf16[8,20,768]{2,1,0:T(8,128)(2,1)S(1)} all-gather(bf16[1,20,768]{2,1,0:T(8,128)(2,1)} %get-tuple-element.109), channel_id=3, replica_groups=mesh['y'=4,'x'=4,'z'=4,'core'=2] {'z','core'}, dimensions={0}, use_global_device_ids=true | all-gather | bytes 276480 | tf_op jit(solution)/shard_map/all_gather | solution.py:166
  510.7 12.9 %all-gather.2 = bf16[8,20,768]{2,1,0:T(8,128)(2,1)S(1)} all-gather(bf16[1,20,768]{2,1,0:T(8,128)(2,1)S(1)} %slice_bitcast_fusion), channel_id=2, replica_groups=mesh['y'=4,'x'=4,'z'=4,'core'=2] {'z','core'}, dimensions={0}, use_global_device_ids=true | all-gather | bytes 276480 | tf_op jit(solution)/shard_map/all_gather | solution.py:127
  524.3 6.8 %convert_element_type.174 = f32[3072,768]{1,0:T(8,128)} convert(bf16[3072,768]{1,0:T(8,128)(2,1)} %all-reduce.6.cloned.1.call-done) | non-fusion elementwise | flops 2359296 | bytes 14155776 | tf_op jit(solution)/shard_map/convert_element_type | solution.py:207
  531.1 7.4 %convert_element_type.173 = f32[768,3072]{1,0:T(8,128)} convert(bf16[768,3072]{1,0:T(8,128)(2,1)} %all-reduce.8.cloned.1.call-done) | non-fusion elementwise | flops 2359296 | bytes 14155776 | tf_op jit(solution)/shard_map/convert_element_type | solution.py:205
  538.6 86.2 %all-reduce.10.cloned.1.call-done = (bf16[800,768]{1,0:T(8,128)(2,1)}, bf16[768,2304]{1,0:T(8,128)(2,1)}) async-done(((bf16[800,768]{1,0:T(8,128)(2,1)}, bf16[768,2304]{1,0:T(8,128)(2,1)}), (bf16[800,768]{1,0:T(8,128)(2,1)}, bf16[768,2304]{1,0:T(8,128)(2,1)})) %all-reduce.10.cloned.1.call-update) | async-done | bytes 4767760 | tf_op jit(solution)/shard_map/psum | solution.py:184
  624.8 3.0 slice_convert_fusion.2
  629.9 3.5 convert_element_type.171
  634.0 2.1 copy.99
  636.1 2.1 copy.100
  (144 shorter events, 49.9 us)
Async XLA Ops:
  7.2 28.9 %copy-start = (bf16[768,2304]{1,0:T(8,128)(2,1)S(1)}, bf16[768,2304]{1,0:T(8,128)(2,1)}, u32[]{:S(2)}) copy-start(bf16[768,2304]{1,0:T(8,128)(2,1)} %param.25) | copy-start | bytes 10616836
  7.2 23.9 %all-to-all-start = ((bf16[8,64,768]{2,1,0:T(8,128)(2,1)}), bf16[8,64,768]{2,1,0:T(8,128)(2,1)}, u32[]{:S(2)}, u32[]{:S(2)}) async-start(bf16[8,64,768]{2,1,0:T(8,128)(2,1)} %param.20), calls=%async_computation | async-start | bytes 1572864 | tf_op jit(solution)/shard_map/all_to_all | solution.py:45
  31.1 52.5 %all-to-all-start.2 = ((bf16[8,64,768]{2,1,0:T(8,128)(2,1)}), bf16[8,64,768]{2,1,0:T(8,128)(2,1)}, u32[]{:S(2)}, u32[]{:S(2)}) async-start(bf16[8,64,768]{2,1,0:T(8,128)(2,1)} %param.38), calls=%async_computation.2 | async-start | bytes 1572864 | tf_op jit(solution)/shard_map/all_to_all | solution.py:45
  36.1 265.1 %all-reduce.6.cloned.1.call-start = ((), (), s32[]{:S(2)}) async-start(), calls=%async_computation.4 | async-start | bytes 9437184 | tf_op jit(solution)/shard_map/psum | solution.py:135
  68.2 3.2 copy-start.18
  68.2 3.2 copy-start.22
  68.2 3.2 copy-start.27
  71.0 8.0 %copy-start.4 = (f32[532,768]{1,0:T(8,128)}, f32[532,768]{1,0:T(8,128)S(1)}, u32[]{:S(2)}) copy-start(f32[532,768]{1,0:T(8,128)S(1)} %get-tuple-element.113) | copy-start | bytes 4902916
  71.0 8.0 %slice-start = ((s8[4718592]{0:T(1024)(128)(4,1)}), s8[4194304]{0:T(1024)(128)(4,1)S(1)}, s32[]{:S(2)}) async-start(s8[4718592]{0:T(1024)(128)(4,1)} %bitcast.85), calls=%async_computation.7 | async-start | bytes 8388608
  71.4 7.6 %copy-start.20 = (f32[532]{0:T(1024)}, f32[532]{0:T(1024)S(1)}, u32[]{:S(2)}) copy-start(f32[532]{0:T(1024)S(1)} %add_rsqrt_fusion.1) | copy-start | bytes 6388
  71.4 7.6 %copy-start.29 = (f32[768]{0:T(1024)S(1)}, f32[768]{0:T(1024)}, u32[]{:S(2)}) copy-start(f32[768]{0:T(1024)} %convert_element_type.147) | copy-start | bytes 9220
  71.4 7.6 %slice-start.1 = ((s8[4718592]{0:T(1024)(128)(4,1)}), s8[524288]{0:T(1024)(128)(4,1)S(1)}, s32[]{:S(2)}) async-start(s8[4718592]{0:T(1024)(128)(4,1)} %bitcast.85), calls=%async_computation.8 | async-start | bytes 1048576
  79.0 3.0 copy-start.35
  82.0 1.2 copy-start.2
  83.5 3.2 copy-start.3
  83.6 3.2 copy-start.14
  83.6 3.2 copy-start.17
  86.8 3.5 copy-start.23
  86.8 12.5 %slice-start.2 = ((s8[4718592]{0:T(1024)(128)(4,1)}), s8[4194304]{0:T(1024)(128)(4,1)S(1)}, s32[]{:S(2)}) async-start(s8[4718592]{0:T(1024)(128)(4,1)} %bitcast.87), calls=%async_computation.9 | async-start | bytes 8388608
  90.3 9.0 %copy-start.7 = (f32[532,768]{1,0:T(8,128)}, f32[532,768]{1,0:T(8,128)S(1)}, u32[]{:S(2)}) copy-start(f32[532,768]{1,0:T(8,128)S(1)} %get-tuple-element.102) | copy-start | bytes 4902916
  90.3 9.0 %copy-start.5 = (f32[532,768]{1,0:T(8,128)S(1)}, f32[532,768]{1,0:T(8,128)}, u32[]{:S(2)}) copy-start(f32[532,768]{1,0:T(8,128)} %copy-done.4) | copy-start | bytes 4902916
  90.3 9.0 %copy-start.19 = (f32[768]{0:T(1024)S(1)}, f32[768]{0:T(1024)}, u32[]{:S(2)}) copy-start(f32[768]{0:T(1024)} %convert_element_type.142) | copy-start | bytes 9220
  90.3 9.0 %copy-start.21 = (f32[532]{0:T(1024)S(1)}, f32[532]{0:T(1024)}, u32[]{:S(2)}) copy-start(f32[532]{0:T(1024)} %copy-done.20) | copy-start | bytes 6388
  90.3 9.0 %slice-start.3 = ((s8[4718592]{0:T(1024)(128)(4,1)}), s8[524288]{0:T(1024)(128)(4,1)S(1)}, s32[]{:S(2)}) async-start(s8[4718592]{0:T(1024)(128)(4,1)} %bitcast.87), calls=%async_computation.10 | async-start | bytes 1048576
  99.3 4.9 copy-start.28
  120.3 4.3 copy-start.30
  123.5 1.2 copy-start.8
  144.1 316.5 %all-reduce.8.cloned.1.call-start = ((), (), s32[]{:S(2)}) async-start(), calls=%async_computation.5 | async-start | bytes 9437184 | tf_op jit(solution)/shard_map/psum | solution.py:141
  144.1 15.5 %copy-start.10 = (bf16[532,768]{0,1:T(8,128)(2,1)S(1)}, bf16[532,768]{0,1:T(8,128)(2,1)}, u32[]{:S(2)}) copy-start(bf16[532,768]{0,1:T(8,128)(2,1)} %copy.61) | copy-start | bytes 2451460
  156.3 3.3 copy-start.1
  301.2 323.6 %all-reduce.10.cloned.1.call-start = ((), (), s32[]{:S(2)}) async-start(), calls=%async_computation.6 | async-start | bytes 9535488 | tf_op jit(solution)/shard_map/psum | solution.py:184
  301.2 6.7 %copy-start.9 = (f32[532,768]{1,0:T(8,128)S(1)}, f32[532,768]{1,0:T(8,128)}, u32[]{:S(2)}) copy-start(f32[532,768]{1,0:T(8,128)} %copy-done.8) | copy-start | bytes 4902916
  301.2 6.7 %copy-start.31 = (bf16[12,532,64]{1,2,0:T(8,128)(2,1)S(1)}, bf16[12,532,64]{1,2,0:T(8,128)(2,1)}, u32[]{:S(2)}) copy-start(bf16[12,532,64]{1,2,0:T(8,128)(2,1)} %multiply_convert_fusion.2) | copy-start | bytes 2451460
  301.2 6.7 %copy-start.33 = (bf16[532,12,64]{0,2,1:T(8,128)(2,1)S(1)}, bf16[532,12,64]{0,2,1:T(8,128)(2,1)}, u32[]{:S(2)}) copy-start(bf16[532,12,64]{0,2,1:T(8,128)(2,1)} %get-tuple-element.119) | copy-start | bytes 2451460
  307.9 2.7 copy-start.11
  310.6 0.9 copy-start.13
  313.0 6.3 copy-start.24
  313.0 11.3 %copy-start.26 = (bf16[768]{0:T(1024)(128)(2,1)S(1)}, bf16[768]{0:T(1024)(128)(2,1)}, u32[]{:S(2)}) copy-start(bf16[768]{0:T(1024)(128)(2,1)} %get-tuple-element.103) | copy-start | bytes 4612
  313.0 17.1 %copy-start.25 = (bf16[768]{0:T(1024)(128)(2,1)S(1)}, bf16[768]{0:T(1024)(128)(2,1)}, u32[]{:S(2)}) copy-start(bf16[768]{0:T(1024)(128)(2,1)} %get-tuple-element.101) | copy-start | bytes 4612
  335.7 3.0 copy-start.15
  335.7 4.1 copy-start.34
  338.7 1.6 copy-start.12
  338.7 1.6 copy-start.16
  338.8 2.0 copy-start.32
  462.6 18.9 %all-to-all-start.3 = ((bf16[8,64,768]{2,1,0:T(8,128)(2,1)}), bf16[8,64,768]{2,1,0:T(8,128)(2,1)}, u32[]{:S(2)}, u32[]{:S(2)}) async-start(bf16[8,64,768]{2,1,0:T(8,128)(2,1)} %bitcast.72), calls=%async_computation.3 | async-start | bytes 1572864 | tf_op jit(solution)/shard_map/all_to_all | solution.py:50
  481.5 42.8 %all-to-all-start.1 = ((bf16[8,64,768]{2,1,0:T(8,128)(2,1)}), bf16[8,64,768]{2,1,0:T(8,128)(2,1)}, u32[]{:S(2)}, u32[]{:S(2)}) async-start(bf16[8,64,768]{2,1,0:T(8,128)(2,1)} %bitcast.71), calls=%async_computation.1 | async-start | bytes 1572864 | tf_op jit(solution)/shard_map/all_to_all | solution.py:50
  624.8 5.1 copy-start.6
Sparse Core Ops, SparseCore 0:
  144.2 156.9 all-reduce.5
  306.6 153.8 all-reduce.7
  466.3 158.4 all-reduce.9

commit v2 on v1

v2 whole, which is shorter than its diff:
```python
import jax
import jax.numpy as jnp
from jax import lax
from jax.experimental import pallas as pl
from jax.experimental.pallas import tpu as pltpu
from jax.sharding import Mesh, PartitionSpec as P

F32 = jnp.float32
BF16 = jnp.bfloat16
HEADS = 12
EPS = 1e-12
BAN = 2.0**30
VMEM_ASK = 60 * 1024 * 1024
BLK = ("z", "core")
SEG = ("y", "x")
ALL = ("y", "x", "z", "core")
XYZ = ("x", "y", "z")
CHIPS = 64
ROW_PAD = 12


def dot(left, right):
    return jnp.dot(left, right, preferred_element_type=F32)


def dot_nt(left, right):
    return lax.dot_general(left, right, (((1,), (1,)), ((), ())), preferred_element_type=F32)


def dot_tn(left, right):
    return lax.dot_general(left, right, (((0,), (0,)), ((), ())), preferred_element_type=F32)


def cost(micros):
    return pl.CostEstimate(flops=int(micros * 1e9), bytes_accessed=0, transcendentals=0)


def lanes_of(shape):
    return lax.broadcasted_iota(jnp.int32, shape, 1)


def split_three(value):
    high = value.astype(BF16)
    rest = value - high.astype(F32)
    middle = rest.astype(BF16)
    low = (rest - middle.astype(F32)).astype(BF16)
    return high, middle, low


def norm_parts(value):
    centre = jnp.mean(value, axis=-1, keepdims=True)
    centered = value - centre
    spread = jnp.mean(centered * centered, axis=-1, keepdims=True)
    scale = lax.rsqrt(spread + EPS)
    return centered * scale, scale


def norm_back(grad, normal, scale):
    mean_grad = jnp.mean(grad, axis=-1, keepdims=True)
    mean_prod = jnp.mean(grad * normal, axis=-1, keepdims=True)
    return scale * (grad - mean_grad - normal * mean_prod)


def attend_kernel(text, mem, w_q, w_k, w_v, lines, lines_all, mark_q, mark_k, w_out,
                  q_out, k_out, v_out, att_out, log_out, resid):
    step = pl.program_id(0)
    x = jnp.concatenate([text[...], mem[...]], axis=0)
    count = x.shape[0]
    query = (dot(x, w_q[...]) + lines[0:1, :]).astype(BF16)
    key = dot(x, w_k[...]).astype(BF16)
    value = (dot(x, w_v[...]) + lines[1:2, :]).astype(BF16)
    q_out[...] = query
    k_out[...] = key
    v_out[...] = value
    scaled = query * jnp.asarray(0.125, BF16)
    lane = lanes_of((count, 128))
    ones = (lane == 0).astype(BF16)
    mq, mk = mark_q[...], mark_k[...]
    pairs = []
    logs = jnp.zeros((count, 128), F32)
    for pair in range(2):
        span = slice(128 * pair, 128 * pair + 128)
        key_wide = jnp.concatenate([key[:, span], mk], axis=1)
        value_wide = jnp.concatenate([value[:, span], ones], axis=1)
        outs = []
        for side in range(2):
            mine = jnp.where(lane // 64 == side, scaled[:, span], jnp.asarray(0, BF16))
            scores = dot_nt(jnp.concatenate([mine, mq], axis=1), key_wide)
            top = jnp.max(scores, axis=-1, keepdims=True)
            raised = jnp.exp(scores - top).astype(BF16)
            summed = dot(raised, value_wide)
            total = summed[:, 128:129]
            outs.append(summed[:, :128] / total)
            logs = jnp.where(lane == 4 * step + 2 * pair + side, top + jnp.log(total), logs)
        pairs.append(jnp.where(lane < 64, outs[0], outs[1]).astype(BF16))
    attended = jnp.concatenate(pairs, axis=1)
    att_out[...] = attended

    @pl.when(step == 0)
    def _():
        log_out[...] = logs
        resid[...] = x.astype(F32) + lines_all[2:3, :]

    @pl.when(step > 0)
    def _():
        log_out[...] += logs

    resid[...] += dot(attended, w_out[...])


def attend(text, mem, w_qkv, lines, mark_q, mark_k, w_out):
    width = text.shape[1]
    count = text.shape[0] + mem.shape[0]
    whole = lambda shape: pl.BlockSpec(shape, lambda j: (0, 0))
    cols = lambda height, base: pl.BlockSpec((height, 256), lambda j: (0, base + j))
    low = jax.ShapeDtypeStruct((count, width), BF16)
    return pl.pallas_call(
        attend_kernel,
        grid=(3,),
        in_specs=[
            whole(text.shape),
            whole(mem.shape),
            cols(width, 0),
            cols(width, 3),
            cols(width, 6),
            cols(16, 0),
            whole((16, width)),
            whole((count, 128)),
            whole((count, 128)),
            pl.BlockSpec((256, width), lambda j: (j, 0)),
        ],
        out_specs=[
            cols(count, 0),
            cols(count, 0),
            cols(count, 0),
            cols(count, 0),
            whole((count, 128)),
            whole((count, width)),
        ],
        out_shape=[
            low,
            low,
            low,
            low,
            jax.ShapeDtypeStruct((count, 128), F32),
            jax.ShapeDtypeStruct((count, width), F32),
        ],
        compiler_params=pltpu.CompilerParams(vmem_limit_bytes=VMEM_ASK),
        cost_estimate=cost(15),
        name="attend",
    )(text, mem, w_qkv, w_qkv, w_qkv, lines, lines, mark_q, mark_k, w_out)


def pack_rows(out, value, split):
    blocks = out.shape[0]
    each = split // blocks
    for block in range(blocks):
        out[block, :each] = value[block * each : (block + 1) * each]
        out[block, each:] = value[split:]


def column_sum(value):
    return jnp.sum(value, axis=0, keepdims=True)


def feed_kernel(resid_one, lines, w_in, w_down, cot_text, cot_mem,
                slope_out, hidden_out, result_out, g_two, g_low_out, sums_out, grad_out, act_all):
    step = pl.program_id(0)
    half = pl.num_programs(0) // 2

    @pl.when(step == 0)
    def _():
        normal, _ = norm_parts(resid_one[...])
        hidden = normal * lines[3:4, :] + lines[4:5, :]
        hidden_out[...] = hidden.astype(BF16)
        g_two[...] = hidden + lines[5:6, :]

    @pl.when(step < half)
    def _():
        inner = dot(hidden_out[...], w_in[...]) + lines[pl.ds(8 + step, 1), :]
        phi = 0.5 * (1.0 + lax.erf(inner * (0.5**0.5)))
        act = (inner * phi).astype(BF16)
        act_all[step] = act
        slope = phi + inner * jnp.exp(-0.5 * inner * inner) * 0.3989422804014327
        slope_out[...] = slope.astype(BF16)
        g_two[...] += dot(act, w_down[...])

    @pl.when(step == half - 1)
    def _():
        normal, scale = norm_parts(g_two[...])
        result = normal * lines[6:7, :] + lines[7:8, :]
        pack_rows(result_out, result.astype(BF16), cot_text.shape[0])
        grad = jnp.concatenate([cot_text[...], cot_mem[...]], axis=0).astype(F32)
        sums_out[0:1, :] = column_sum(grad * normal)
        sums_out[1:2, :] = column_sum(grad)
        grad = norm_back(grad * lines[6:7, :], normal, scale)
        sums_out[2:3, :] = column_sum(grad)
        g_two[...] = grad
        g_low_out[...] = grad.astype(BF16)

    @pl.when(step >= half)
    def _():
        grad_out[...] = dot_tn(act_all[step - half], g_low_out[...]).astype(BF16)


def feed(resid_one, lines, w_in, w_down, cot_text, cot_mem, packed):
    count, width = resid_one.shape
    wide = w_in.shape[1]
    half = wide // width
    whole = lambda shape: pl.BlockSpec(shape, lambda j: (0, 0))
    early = lambda height: pl.BlockSpec((height, width), lambda j: (0, jnp.minimum(j, half - 1)))
    full = whole((count, width))
    return pl.pallas_call(
        feed_kernel,
        grid=(2 * half,),
        in_specs=[
            full,
            whole(lines.shape),
            early(width),
            pl.BlockSpec((width, width), lambda j: (jnp.minimum(j, half - 1), 0)),
            whole(cot_text.shape),
            whole(cot_mem.shape),
        ],
        out_specs=[
            early(count),
            full,
            pl.BlockSpec(packed, lambda j: (0, 0, 0)),
            full,
            full,
            whole((8, width)),
            pl.BlockSpec((width, width), lambda j: (jnp.maximum(j - half, 0), 0)),
        ],
        out_shape=[
            jax.ShapeDtypeStruct((count, wide), BF16),
            jax.ShapeDtypeStruct((count, width), BF16),
            jax.ShapeDtypeStruct(packed, BF16),
            jax.ShapeDtypeStruct((count, width), F32),
            jax.ShapeDtypeStruct((count, width), BF16),
            jax.ShapeDtypeStruct((8, width), F32),
            jax.ShapeDtypeStruct((wide, width), BF16),
        ],
        scratch_shapes=[pltpu.VMEM((half, count, width), BF16)],
        compiler_params=pltpu.CompilerParams(vmem_limit_bytes=VMEM_ASK),
        cost_estimate=cost(20),
        name="feed",
    )(resid_one, lines, w_in, w_down, cot_text, cot_mem)


def inner_back_kernel(g_low, slope, hidden, w_down, grad_out, inner_out, sums_out):
    g_inner = dot_nt(g_low[...], w_down[...]) * slope[...].astype(F32)
    sums_out[0:1, :] = column_sum(g_inner)
    g_inner_low = g_inner.astype(BF16)
    inner_out[...] = g_inner_low
    grad_out[0] = dot_tn(hidden[...], g_inner_low).astype(BF16)


def inner_back(g_low, slope, hidden, w_down):
    count, width = g_low.shape
    wide = slope.shape[1]
    half = wide // width
    full = pl.BlockSpec((count, width), lambda j: (0, 0))
    part = lambda height: pl.BlockSpec((height, width), lambda j: (0, j))
    return pl.pallas_call(
        inner_back_kernel,
        grid=(half,),
        in_specs=[full, part(count), full, pl.BlockSpec((width, width), lambda j: (j, 0))],
        out_specs=[
            pl.BlockSpec((1, width, width), lambda j: (j, 0, 0)),
            part(count),
            part(8),
        ],
        out_shape=[
            jax.ShapeDtypeStruct((half, width, width), BF16),
            jax.ShapeDtypeStruct((count, wide), BF16),
            jax.ShapeDtypeStruct((8, wide), F32),
        ],
        compiler_params=pltpu.CompilerParams(vmem_limit_bytes=VMEM_ASK),
        cost_estimate=cost(10),
        name="inner_back",
    )(g_low, slope, hidden, w_down)


def norm_one_back_kernel(g_two, g_inner, w_in, resid_one, lines, g_one, g_one_low, sums_out):
    step = pl.program_id(0)

    @pl.when(step == 0)
    def _():
        g_one[...] = g_two[...]

    g_one[...] += dot_nt(g_inner[...], w_in[...])

    @pl.when(step == pl.num_programs(0) - 1)
    def _():
        normal, scale = norm_parts(resid_one[...])
        g_hidden = g_one[...]
        sums_out[0:1, :] = column_sum(g_hidden * normal)
        sums_out[1:2, :] = column_sum(g_hidden)
        grad = norm_back(g_hidden * lines[3:4, :], normal, scale)
        sums_out[2:3, :] = column_sum(grad)
        g_one[...] = grad
        g_one_low[...] = grad.astype(BF16)


def norm_one_back(g_two, g_inner, w_in, resid_one, lines):
    count, width = g_two.shape
    half = w_in.shape[1] // width
    whole = lambda shape: pl.BlockSpec(shape, lambda j: (0, 0))
    part = lambda height: pl.BlockSpec((height, width), lambda j: (0, j))
    full = whole((count, width))
    return pl.pallas_call(
        norm_one_back_kernel,
        grid=(half,),
        in_specs=[full, part(count), part(width), full, whole(lines.shape)],
        out_specs=[full, full, whole((8, width))],
        out_shape=[
            jax.ShapeDtypeStruct((count, width), F32),
            jax.ShapeDtypeStruct((count, width), BF16),
            jax.ShapeDtypeStruct((8, width), F32),
        ],
        compiler_params=pltpu.CompilerParams(vmem_limit_bytes=VMEM_ASK),
        cost_estimate=cost(8),
        name="norm_one_back",
    )(g_two, g_inner, w_in, resid_one, lines)


def attend_back_kernel(text, mem, q, k, v, att, logs, mark_q, mark_k, g_one, g_low, w_out,
                       w_q, w_k, w_v, sums_two, sums_one, sums_in, scalars,
                       mine_out, theirs_out, packed_out, g_rows, sums):
    step = pl.program_id(0)
    core = scalars[0, 1]
    split = text.shape[0]
    count = split + mem.shape[0]
    width = text.shape[1]
    query, key, value, attended = q[...], k[...], v[...], att[...]

    def put(half, start, part):
        rows = pl.ds(pl.multiple_of(start, 16), part.shape[0])

        @pl.when(core == half)
        def _():
            mine_out[rows, :] = part

        @pl.when(core != half)
        def _():
            theirs_out[rows, :] = part

    blocks = width // 128
    grad_w_out = dot_tn(attended, g_low[...]).astype(BF16)
    for block in range(blocks):
        part = grad_w_out[:, 128 * block : 128 * block + 128]
        put(1, (blocks + block) * width + 256 * step, part)
    g_att = dot_nt(g_low[...], w_out[...])
    g_att_low = g_att.astype(BF16)
    scaled = query * jnp.asarray(0.125, BF16)
    product = g_att_low.astype(F32) * attended.astype(F32)
    lane = lanes_of((count, 128))
    none = jnp.asarray(0, BF16)
    thirds = ((lane >= 4) & (lane < 7)).astype(BF16)
    mq, mk = mark_q[...], mark_k[...] + thirds
    log_all = logs[...]

    def extra(column, base):
        high, middle, low = split_three(-column)
        wide = jnp.where(lane == 4, high, jnp.where(lane == 5, middle, low))
        return jnp.where((lane >= 4) & (lane < 7), wide, base)

    g_querys, g_keys, g_values = [], [], []
    for pair in range(2):
        span = slice(128 * pair, 128 * pair + 128)
        key_pair = key[:, span]
        key_wide = jnp.concatenate([key_pair, mk], axis=1)
        value_wide = jnp.concatenate([value[:, span], thirds], axis=1)
        key_turned = key_pair.astype(F32).T
        turned = lax.broadcasted_iota(jnp.int32, key_turned.shape, 0)
        g_query = g_key = g_value = None
        for side in range(2):
            own = lane // 64 == side
            mine = jnp.where(own, scaled[:, span], none)
            head = 4 * step + 2 * pair + side
            log_own = jnp.sum(jnp.where(lane == head, log_all, 0.0), axis=1, keepdims=True)
            query_wide = jnp.concatenate([mine, extra(log_own, mq)], axis=1)
            probs = jnp.exp(dot_nt(key_wide, query_wide))
            g_mine = jnp.where(own, g_att_low[:, span], none)
            delta = jnp.sum(jnp.where(own, product[:, span], 0.0), axis=1, keepdims=True)
            g_wide = jnp.concatenate([g_mine, extra(delta, jnp.zeros_like(mq))], axis=1)
            g_scores = (probs * dot_nt(value_wide, g_wide)).astype(BF16)
            part_v = dot(probs.astype(BF16), g_mine)
            part_k = dot(g_scores, mine)
            turned_own = jnp.where(turned // 64 == side, key_turned, 0.0).astype(BF16)
            part_q = dot(turned_own, g_scores)
            if side == 0:
                g_query, g_key, g_value = part_q, part_k, part_v
            else:
                g_query, g_key, g_value = g_query + part_q, g_key + part_k, g_value + part_v
        g_querys.append(g_query.T * 0.125)
        g_keys.append(g_key)
        g_values.append(g_value)
    g_query = jnp.concatenate(g_querys, axis=1)
    g_key = jnp.concatenate(g_keys, axis=1)
    g_value = jnp.concatenate(g_values, axis=1)
    columns = pl.ds(pl.multiple_of(256 * step, 256), 256)
    sums[0:1, columns] = column_sum(g_query)
    sums[1:2, columns] = column_sum(g_value)
    x = jnp.concatenate([text[...], mem[...]], axis=0)

    @pl.when(step == 0)
    def _():
        g_rows[...] = g_one[...]

    total = g_rows[...]
    for place, (grad, weight) in enumerate(((g_query, w_q), (g_key, w_k), (g_value, w_v))):
        low = grad.astype(BF16)
        grad_w = dot_tn(x, low).astype(BF16)
        for block in range(2):
            part = grad_w[:, 128 * block : 128 * block + 128]
            put(place // 2, ((place % 2) * blocks + 2 * step + block) * width, part)
        total += dot_nt(low, weight[...])
    g_rows[...] = total

    @pl.when(step == pl.num_programs(0) - 1)
    def _():
        reset = scalars[0, 0] == 1
        g_mem = total[split:]
        zero = jnp.zeros_like(g_mem)
        g_kept = jnp.where(reset, zero, g_mem)
        pack_rows(packed_out, jnp.concatenate([total[:split], g_kept], axis=0).astype(BF16), split)
        sums[2:5, :] = sums_one[0:3, :]
        sums[5:8, :] = sums_two[0:3, :]
        for place in range(4):
            sums[8 + place : 9 + place, :] = sums_in[0:1, place * width : (place + 1) * width]
        sums[12:16, :] = jnp.zeros((4, width), F32)
        small = [jnp.where(reset, g_mem, zero).astype(BF16), sums[...].astype(BF16)]
        small = jnp.concatenate(small, axis=0)
        base = 2 * blocks * width
        spare = mine_out.shape[0] - base
        empty = jnp.zeros((spare, 128), BF16)
        mine_out[base:, :] = empty
        theirs_out[base:, :] = empty
        for block in range(blocks):
            put(0, base + block * small.shape[0], small[:, 128 * block : 128 * block + 128])


def attend_back(text, mem, q, k, v, att, logs, mark_q, mark_k, g_one, g_low, w_out, w_qkv,
                sums_two, sums_one, sums_in, scalars, packed):
    width = text.shape[1]
    count = text.shape[0] + mem.shape[0]
    whole = lambda shape: pl.BlockSpec(shape, lambda j: (0, 0))
    cols = lambda height, base: pl.BlockSpec((height, 256), lambda j: (0, base + j))
    full = whole((count, width))
    mark = whole((count, 128))
    height = 2 * (width // 128) * width + 512
    return pl.pallas_call(
        attend_back_kernel,
        grid=(3,),
        in_specs=[
            whole(text.shape),
            whole(mem.shape),
            cols(count, 0),
            cols(count, 0),
            cols(count, 0),
            cols(count, 0),
            mark,
            mark,
            mark,
            full,
            full,
            pl.BlockSpec((256, width), lambda j: (j, 0)),
            cols(width, 0),
            cols(width, 3),
            cols(width, 6),
            whole(sums_two.shape),
            whole(sums_one.shape),
            whole(sums_in.shape),
            pl.BlockSpec(memory_space=pltpu.SMEM),
        ],
        out_specs=[
            whole((height, 128)),
            whole((height, 128)),
            pl.BlockSpec(packed, lambda j: (0, 0, 0)),
        ],
        out_shape=[
            jax.ShapeDtypeStruct((height, 128), BF16),
            jax.ShapeDtypeStruct((height, 128), BF16),
            jax.ShapeDtypeStruct(packed, BF16),
        ],
        scratch_shapes=[pltpu.VMEM((count, width), F32), pltpu.VMEM((16, width), F32)],
        compiler_params=pltpu.CompilerParams(vmem_limit_bytes=VMEM_ASK),
        cost_estimate=cost(25),
        name="attend_back",
    )(text, mem, q, k, v, att, logs, mark_q, mark_k, g_one, g_low, w_out, w_qkv, w_qkv, w_qkv,
      sums_two, sums_one, sums_in, scalars)


def widen_kernel(mine, got, scalars, qkv_out, out_out):
    group = pl.program_id(0)
    own = group // 2 == scalars[0, 1]
    width = out_out.shape[0]

    def fill(ref):
        for block in range(width // 128):
            rows = slice(block * width, (block + 1) * width)
            ref[:, 128 * block : 128 * block + 128] = jnp.where(
                own, mine[rows, :].astype(F32), got[rows, :].astype(F32)
            )

    @pl.when(group < 3)
    def _():
        fill(qkv_out)

    @pl.when(group == 3)
    def _():
        fill(out_out)


def widen(mine, got, scalars, width):
    tall = width // 128 * width
    half = pl.BlockSpec((tall, 128), lambda g: (g % 2, 0))
    return pl.pallas_call(
        widen_kernel,
        grid=(4,),
        in_specs=[half, half, pl.BlockSpec(memory_space=pltpu.SMEM)],
        out_specs=[
            pl.BlockSpec((width, width), lambda g: (0, jnp.minimum(g, 2))),
            pl.BlockSpec((width, width), lambda g: (0, 0)),
        ],
        out_shape=[
            jax.ShapeDtypeStruct((width, 3 * width), F32),
            jax.ShapeDtypeStruct((width, width), F32),
        ],
        compiler_params=pltpu.CompilerParams(vmem_limit_bytes=VMEM_ASK),
        cost_estimate=cost(6),
        name="widen",
    )(mine, got, scalars)


def core_swap(value):
    return lax.ppermute(value, "core", [(0, 1), (1, 0)])


def to_segments(value):
    return lax.all_to_all(value, BLK, 0, 1, tiled=True)[0]


def after(value, other):
    return lax.optimization_barrier((value, other))[0]


def doc_marks(docs, mem_count):
    kinds = (docs[:, None] == jnp.arange(3)[None]).astype(F32)
    rest = mem_count + ROW_PAD
    total = docs.shape[0] + rest
    spare = (jnp.arange(total) >= total - ROW_PAD).astype(F32)[:, None]
    query = jnp.concatenate([jnp.pad(kinds, ((0, rest), (0, 0))), jnp.ones((total, 1), F32)], 1)
    key = jnp.concatenate([jnp.pad(kinds - 1.0, ((0, rest), (0, 0))), -spare], 1) * BAN
    fill = ((0, 0), (0, 128 - query.shape[1]))
    return jnp.pad(query, fill).astype(BF16), jnp.pad(key, fill).astype(BF16)


def local(
    tokens,
    memory,
    mem_init,
    reset_flags,
    doc_ids,
    w_qkv,
    b_query,
    b_value,
    w_out,
    b_out,
    norm1_gain,
    norm1_bias,
    w_in,
    b_in,
    w_down,
    b_down,
    norm2_gain,
    norm2_bias,
    out_cot,
    mem_cot,
):
    seg_count, tok_count, width = tokens.shape
    mem_count = memory.shape[1]
    place = lax.axis_index(BLK)
    pick = lambda value: lax.dynamic_index_in_dim(value, place, 0, keepdims=False)
    fill = lambda value: jnp.pad(value, ((0, ROW_PAD), (0, 0)))
    packed = (seg_count, tok_count + mem_count + ROW_PAD, width)
    my_flag = pick(reset_flags)
    mark_q, mark_k = doc_marks(pick(doc_ids), mem_count)
    mem = fill(jnp.where(my_flag == 1, mem_init, pick(memory)))
    cot_mem = fill(pick(mem_cot))
    text = to_segments(tokens)
    cot_text = to_segments(after(out_cot, text))

    lines = jnp.concatenate(
        [b_query, b_value, b_out, norm1_gain, norm1_bias, b_down, norm2_gain, norm2_bias, b_in]
    )
    lines = jnp.pad(lines.astype(F32).reshape(-1, width), ((0, 4), (0, 0)))
    q, k, v, att, logs, resid = attend(text, mem, w_qkv, lines, mark_q, mark_k, w_out)
    slope, hidden, result, g_two, g_two_low, sums_two, grad_down = feed(
        resid, lines, w_in, w_down, cot_text, cot_mem, packed
    )
    grad_in, g_inner, sums_in = inner_back(g_two_low, slope, hidden, w_down)
    grad_down, grad_in = lax.psum((grad_down, grad_in), ALL)
    scalars = jnp.stack([my_flag, lax.axis_index("core")]).reshape(1, 2).astype(jnp.int32)
    small_count = mem_count + ROW_PAD + 16

    def attention_back(operands):
        result, g_two, g_inner, sums_two, sums_in = operands
        g_one, g_one_low, sums_one = norm_one_back(g_two, g_inner, w_in, resid, lines)
        mine, theirs, g_packed = attend_back(
            text,
            mem,
            q,
            k,
            v,
            att,
            logs,
            mark_q,
            mark_k,
            g_one,
            g_one_low,
            w_out,
            w_qkv,
            sums_two,
            sums_one,
            sums_in,
            scalars,
            packed,
        )
        both = jnp.concatenate([result, g_packed], axis=1)
        mine = (mine.astype(F32) + core_swap(theirs).astype(F32)).astype(BF16)
        parts = mine.reshape(CHIPS, -1, 128)
        parts = lax.all_to_all(parts, XYZ, 0, 0, tiled=True)
        part = jnp.sum(parts.astype(F32), axis=0).astype(BF16)
        parts = lax.all_to_all(
            jnp.broadcast_to(part[None], parts.shape), XYZ, 0, 0, tiled=True
        )
        mine = parts.reshape(mine.shape)
        both = lax.all_to_all(after(both, mine), BLK, 0, 0, tiled=True)
        got = core_swap(mine)
        grad_wqkv, grad_wout = widen(mine, got, scalars, width)
        blocks = width // 128
        small = jnp.where(scalars[0, 1] == 0, mine[-512:], got[-512:])
        small = small[: blocks * small_count].reshape(blocks, small_count, 128)
        small = small.astype(F32).transpose(1, 0, 2).reshape(small_count, width)
        pieces = []
        for base in (0, result.shape[1]):
            pieces.append(both[:, base : base + tok_count])
            pieces.append(both[:, base + tok_count : base + tok_count + mem_count])
        return grad_wqkv, grad_wout, small, *pieces

    def nothing(operands):
        text_zero = jnp.zeros(tokens.shape, BF16)
        mem_zero = jnp.zeros(memory.shape, BF16)
        return (
            jnp.zeros(w_qkv.shape, F32),
            jnp.zeros(w_out.shape, F32),
            jnp.zeros((small_count, width), F32),
            text_zero,
            mem_zero,
            text_zero,
            mem_zero,
        )

    grad_wqkv, grad_wout, small, output, mem_output, grad_tokens, grad_memory = lax.cond(
        reset_flags[0] >= 0, attention_back, nothing, (result, g_two, g_inner, sums_two, sums_in)
    )
    grad_bquery, grad_bvalue, grad_gain1, grad_bias1, grad_bout, grad_gain2, grad_bias2, grad_bdown = (
        small[mem_count + ROW_PAD + row] for row in range(8)
    )
    start = mem_count + ROW_PAD + 8
    grad_bin = small[start : start + w_in.shape[1] // width].reshape(-1)
    return (
        output,
        mem_output,
        grad_tokens,
        grad_memory,
        small[:mem_count],
        grad_wqkv,
        grad_bquery,
        grad_bvalue,
        grad_wout,
        grad_bout,
        grad_gain1,
        grad_bias1,
        jnp.concatenate(list(grad_in), axis=1).astype(F32),
        grad_bin,
        grad_down.astype(F32),
        grad_bdown,
        grad_gain2,
        grad_bias2,
    )


def solution(mesh):
    chips = Mesh(mesh.devices.reshape(4, 4, 4, 2), ALL)
    placed = (
        P(SEG, BLK, None),
        P(SEG, None, None),
        P(),
        P(SEG),
        P(SEG, None),
        *([P()] * 13),
        P(SEG, BLK, None),
        P(SEG, None, None),
    )
    return jax.shard_map(
        local,
        mesh=chips,
        in_specs=placed,
        out_specs=(
            P(SEG, BLK, None),
            P(SEG, None, None),
            P(SEG, BLK, None),
            P(SEG, None, None),
            *([P()] * 14),
        ),
        check_vma=False,
    )
```

time: 650 us -> 298 us (0.46)
  waiting for transfers between devices: 337 us -> 74.1 us
  matrix products: 116 us -> 0 us
  Pallas kernels: 0 us -> 93.8 us
  other arithmetic: 66.9 us -> 15.5 us
  local copies, waits for them, and re-layouts: 51.5 us -> 27.2 us
  blocking collectives: 35.3 us -> 44.6 us
    psum x3 -> x1, waiting for transfers between devices: 326 us -> 11.4 us  [local(): grad_down, grad_in = lax.psum((grad_down, grad_in), ALL)]
    dot_general x17 -> x0, matrix products: 105 us -> none  [the longest x4 25.5 us: dot_tn(): lax.dot_general(left, right, (((0,), (0,)), ((), ())), preferred_element_...]
    pallas_call x0 -> x6, Pallas kernels: none -> 93.8 us  [the longest x1 31 us: attend_back(): pl.pallas_call(attend_back_kernel, grid=(3,), in_specs=[whole(text.shape)...]
    all_to_all x2, waiting for transfers between devices: 11.7 us -> 57.9 us  [the longest x1 30 us: attention_back(): both = lax.all_to_all(after(both, mine), BLK, 0, 0, tiled=True)]
    all_to_all x0 -> x1, blocking collectives: none -> 44.6 us  [attention_back(): parts = lax.all_to_all(parts, XYZ, 0, 0, tiled=True)]
    all_gather x2 -> x0, blocking collectives: 35.3 us -> none  [the longest x1 22.4 us: local(): lax.all_gather(jnp.where(my_flag, 0.0, grad_mem).astype(BF16), BLK, axis=0)]
    convert_element_type x16 -> x3, other arithmetic: 44.3 us -> 10.8 us  [the longest x1 4.48 us: local(): grad_down.astype(F32)]
    unnamed x95 -> x30, local copies, waits for them, and re-layouts: 26.9 us -> 8.75 us
  transfers between devices with their start and end apart: 7 -> 7, of which waited for: 4 -> 5; matrix products, arithmetic and copies ran while one was open for 24% -> 9% of each run, Pallas kernels for 0% -> 21%
where the time goes in v2:
time: 298 us; the launch traced here: 297 us
  Pallas kernels  93.8 us (31%)
  waiting for transfers between devices  74.1 us (25%)
  blocking collectives  44.6 us (15%)
  local copies, waits for them, and re-layouts  27.2 us (9%)
  starting transfers between devices  25.5 us (9%)
  between operations  15.6 us (5%)
  other arithmetic  15.5 us (5%)
    all_to_all x1, blocking collectives, attention_back(): parts = lax.all_to_all(parts, XYZ, 0, 0, tiled=True)  44.6 us
    pallas_call x1, Pallas kernels, attend_back(): pl.pallas_call(attend_back_kernel, grid=(3,), in_specs=[whole(text.shape)...  31 us
    all_to_all x1, waiting for transfers between devices, attention_back(): both = lax.all_to_all(after(both, mine), BLK, 0, 0, tiled=True)  30 us
    all_to_all x1, waiting for transfers between devices, attention_back(): lax.all_to_all(jnp.broadcast_to(part[None], parts.shape), XYZ, 0, 0, tile...  28 us
    pallas_call x1, Pallas kernels, feed(): pl.pallas_call(feed_kernel, grid=(2 * half,), in_specs=[full, whole(lines...  19.8 us
    pallas_call x1, Pallas kernels, attend(): pl.pallas_call(attend_kernel, grid=(3,), in_specs=[whole(text.shape), who...  13.9 us
    all_to_all x2, starting transfers between devices, to_segments(): return lax.all_to_all(value, BLK, 0, 1, tiled=True)[0]  11.7 us
    psum x1, waiting for transfers between devices, local(): grad_down, grad_in = lax.psum((grad_down, grad_in), ALL)  11.4 us
  transfers between devices with their start and end apart: 7, of which 5 were waited for; matrix products, arithmetic and copies ran while one was open for 9% of the time, Pallas kernels for 21%

profile of v2, /device:TPU:1, one launch (start us, length us, event | category | flops | bytes accessed | tf_op | source)
XLA Modules:
  0.0 297.2 jit_solution(14897550663905260567)
XLA Ops:
  7.2 7.0 %all-to-all-start.3 = ((bf16[8,64,768]{2,1,0:T(8,128)(2,1)}), bf16[8,64,768]{2,1,0:T(8,128)(2,1)S(1)}, u32[]{:S(2)}, u32[]{:S(2)}) async-start(bf16[8,64,768]{2,1,0:T(8,128)(2,1)} %param.22), calls=%async_computation.3 | async-start | bytes 1572864 | tf_op jit(solution)/shard_map/all_to_all | solution.py:541
  14.2 1.3 fusion.7
  16.3 1.2 constant_dynamic-slice_fusion
  17.5 0.9 dynamic-update-slice
  18.4 0.8 dynamic-update-slice.1
  19.2 0.9 dynamic-update-slice.2
  20.1 0.9 dynamic-update-slice.3
  20.9 0.9 dynamic-update-slice.4
  21.8 0.8 dynamic-update-slice.5
  22.6 0.9 dynamic-update-slice.6
  23.5 0.9 dynamic-update-slice.7
  24.3 0.7 constant_dynamic-update-slice_fusion
  25.1 0.6 pad.39.cot_mem
  26.5 4.7 %all-to-all-start.4 = ((bf16[8,64,768]{2,1,0:T(8,128)(2,1)}), bf16[8,64,768]{2,1,0:T(8,128)(2,1)S(1)}, u32[]{:S(2)}, u32[]{:S(2)}) async-start(bf16[8,64,768]{2,1,0:T(8,128)(2,1)} %param.40), calls=%async_computation.4 | async-start | bytes 1572864 | tf_op jit(solution)/shard_map/all_to_all | solution.py:541
  31.2 13.9 %attend.1 = (bf16[544,768]{1,0:T(8,128)(2,1)}, bf16[544,768]{1,0:T(8,128)(2,1)}, bf16[544,768]{1,0:T(8,128)(2,1)}, bf16[544,768]{1,0:T(8,128)(2,1)}, f32[544,128]{1,0:T(8,128)}, /*index=5*/f32[544,768]{1,0:T(8,128)}) custom-call(bf16[512,768]{1,0:T(8,128)(2,1)S(1)} %bitcast.96, bf16[32,768]{1,0:T(8,128)(2,1)S(1)} %pad.32.mem, bf16[768,2304]{1,0:T(8,128)(2,1)} %w_v.1, ...), custom_call_target="tpu_custom_call" | custom-call | flops 15000000512 | tf_op jit(solution)/shard_map/attend/pallas_call | solution.py:117
  45.1 0.9 copy-done.3
  46.0 19.8 %feed.1 = (bf16[544,3072]{1,0:T(8,128)(2,1)}, bf16[544,768]{1,0:T(8,128)(2,1)}, bf16[8,96,768]{2,1,0:T(8,128)(2,1)}, f32[544,768]{1,0:T(8,128)}, bf16[544,768]{1...) custom-call(f32[544,768]{1,0:T(8,128)} %get-tuple-element.140.resid_one, ...), custom_call_target="tpu_custom_call" | custom-call | flops 20000000000 | tf_op jit(solution)/shard_map/feed/pallas_call | solution.py:213
  65.8 10.7 %inner_back.1 = (bf16[4,768,768]{2,1,0:T(8,128)(2,1)}, bf16[544,3072]{1,0:T(8,128)(2,1)}, f32[8,3072]{1,0:T(8,128)S(1)}) custom-call(bf16[544,768]{1,0:T(8,128)(2,1)} %get-tuple-element.143.g_low, bf16[544,3072]{1,0:T(8,128)(2,1)} %get-tuple-element.144.slope, bf16[544,768]{1,0:T(8,128)(2,1)} %get-tuple-element.145.hidden, bf16[3072,768]{1,0:T(8,128)(2,1)} %w_down.3), custom_call_target="tpu_custom_call" | custom-call | flops 10000000000 | tf_op jit(solution)/shard_map/inner_back/pallas_call | solution.py:263
  77.2 0.7 pad_add_fusion
  78.0 188.5 %conditional.1 = (f32[768,2304]{1,0:T(8,128)}, f32[768,768]{1,0:T(8,128)}, bf16[48,768]{1,0:T(8,128)(2,1)}, bf16[8,64,768]{2,1,0:T(8,128)(2,1)}, bf16[8,64,768]{...) conditional(s32[]{:T(128)} %bitcast.15, () %tuple.20, ...), branch_computations={%region_0.1_spmd, %region_1.3_spmd} | conditional | flops 39010963456 | bytes 76956192 | solution.py:665
  78.2 9.7 %norm_one_back.1 = (f32[544,768]{1,0:T(8,128)}, bf16[544,768]{1,0:T(8,128)(2,1)}, f32[8,768]{1,0:T(8,128)}) custom-call(f32[544,768]{1,0:T(8,128)} %get-tuple-element.69.g_two, bf16[544,3072]{1,0:T(8,128)(2,1)} %get-tuple-element.70.g_inner, bf16[768,3072]{1,0:T(8,128)(2,1)} %get-tuple-element.71.w_in, f32[544,768]{1,0:T(8,128)} %get-tuple-element.72.resid_one, ...), custom_call_target="tpu_custom_call" | custom-call | flops 8000000000 | tf_op jit(solution)/shard_map/cond/branch_1_fun/norm_one_back/pallas_call | solution.py:310
  87.9 31.0 %attend_back.1 = (bf16[9728,128]{1,0:T(8,128)(2,1)}, bf16[9728,128]{1,0:T(8,128)(2,1)}, bf16[8,96,768]{2,1,0:T(8,128)(2,1)}) custom-call(bf16[512,768]{1,0:T(8,128)(2,1)S(1)} %get-tuple-element.60.text, bf16[32,768]{1,0:T(8,128)(2,1)S(1)} %get-tuple-element.61.mem, bf16[544,768]{1,0:T(8,128)(2,1)S(1)} %copy-done.10, bf16[544,768]{1,0:T(8,128)(2,1)} %get-tuple-element.63.k, ...), custom_call_target="tpu_custom_call" | custom-call | flops 24999999488 | tf_op jit(solution)/shard_map/cond/branch_1_fun/attend_back/pallas_call | solution.py:452
  119.2 4.6 %collective-permute-done = bf16[9728,128]{1,0:T(8,128)(2,1)S(1)} collective-permute-done((bf16[9728,128]{1,0:T(8,128)(2,1)}, bf16[9728,128]{1,0:T(8,128)(2,1)S(1)}, u32[]{:S(2)}, u32[]{:S(2)}) %collective-permute-start) | collective-permute-done | bytes 2490400 | tf_op jit(solution)/shard_map/cond/branch_1_fun/ppermute | solution.py:537
  123.8 2.0 add_convert_fusion
  125.8 44.6 %all_to_all.30 = bf16[64,152,128]{2,1,0:T(8,128)(2,1)S(1)} all-to-all(bf16[64,152,128]{2,1,0:T(8,128)(2,1)S(1)} %bitcast.90), channel_id=1, replica_groups=mesh['y'=4,'x'=4,'z'=4,'core'=2] {'x','y','z'}, dimensions={0} | all-to-all | bytes 4980736 | tf_op jit(solution)/shard_map/cond/branch_1_fun/all_to_all | solution.py:633
  170.8 1.8 broadcast_in_dim.0
  172.6 5.6 %all-to-all-start.1 = ((bf16[64,152,128]{2,1,0:T(8,128)(2,1)}), bf16[64,152,128]{2,1,0:T(8,128)(2,1)S(1)}, u32[]{:S(2)}, u32[]{:S(2)}) async-start(bf16[64,152,128]{2,1,0:T(8,128)(2,1)} %broadcast_in_dim.0), calls=%async_computation.1 | async-start | bytes 4980736 | tf_op jit(solution)/shard_map/cond/branch_1_fun/all_to_all | solution.py:635
  178.2 3.2 %pad_maximum_fusion = bf16[8,192,768]{2,1,0:T(8,128)(2,1)} fusion(bf16[8,96,768]{2,1,0:T(8,128)(2,1)} %get-tuple-element.87, bf16[8,96,768]{2,1,0:T(8,128)(2,1)} %get-tuple-element.86), kind=kLoop, calls=%fused_computation.1 | loop fusion | flops 4718592 | bytes 4718592 | tf_op jit(solution)/shard_map/cond/branch_1_fun/concatenate | solution.py:630
  181.4 28.0 %all-to-all-done.1 = bf16[64,152,128]{2,1,0:T(8,128)(2,1)S(1)} async-done(((bf16[64,152,128]{2,1,0:T(8,128)(2,1)}), bf16[64,152,128]{2,1,0:T(8,128)(2,1)S(1)}, u32[]{:S(2)}, u32[]{:S(2)}) %all-to-all-start.1) | async-done | bytes 2490400 | tf_op jit(solution)/shard_map/cond/branch_1_fun/all_to_all | solution.py:635
  209.4 1.4 copy-done.2
  210.8 7.8 %all-to-all-start.2 = ((bf16[8,192,768]{2,1,0:T(8,128)(2,1)}), bf16[8,192,768]{2,1,0:T(8,128)(2,1)S(1)}, u32[]{:S(2)}, u32[]{:S(2)}) async-start(bf16[8,192,768]{2,1,0:T(8,128)(2,1)} %pad_maximum_fusion), calls=%async_computation.2 | async-start | bytes 4718592 | tf_op jit(solution)/shard_map/cond/branch_1_fun/all_to_all | solution.py:639
  220.0 0.9 slice.114
  220.9 30.0 %all-to-all-done.2 = bf16[8,192,768]{2,1,0:T(8,128)(2,1)S(1)} async-done(((bf16[8,192,768]{2,1,0:T(8,128)(2,1)}), bf16[8,192,768]{2,1,0:T(8,128)(2,1)S(1)}, u32[]{:S(2)}, u32[]{:S(2)}) %all-to-all-start.2) | async-done | bytes 2359328 | tf_op jit(solution)/shard_map/cond/branch_1_fun/all_to_all | solution.py:639
  251.0 0.7 copy.69
  251.7 1.2 fusion.6
  252.9 0.9 slice.115
  254.0 0.6 slice_bitcast_fusion
  254.6 0.6 copy.101
  255.3 0.6 copy.103
  255.9 0.6 copy.76
  256.5 0.6 copy_bitcast_fusion.7
  257.2 0.6 copy_bitcast_fusion.9
  257.7 8.7 %widen.1 = (f32[768,2304]{1,0:T(8,128)}, f32[768,768]{1,0:T(8,128)}) custom-call(bf16[9728,128]{1,0:T(8,128)(2,1)} %bitcast.95, bf16[9728,128]{1,0:T(8,128)(2,1)} %collective-permute-done.1.got, s32[1,2]{1,0:T(1,128)S(1)} %bitcast.114), custom_call_target="tpu_custom_call" | custom-call | flops 6000000000 | tf_op jit(solution)/shard_map/cond/branch_1_fun/widen/pallas_call | solution.py:518
  266.4 11.4 %all-reduce.11.cloned.1.call-done = (bf16[4,768,768]{2,1,0:T(8,128)(2,1)}, bf16[3072,768]{1,0:T(8,128)(2,1)}) async-done(((bf16[4,768,768]{2,1,0:T(8,128)(2,1)}, bf16[3072,768]{1,0:T(8,128)(2,1)}), (bf16[4,768,768]{2,1,0:T(8,128)(2,1)}, bf16[3072,768]{1,0:T(8,128)(2,1)})) %all-reduce.11.cloned.1.call-update) | async-done | bytes 9437200 | tf_op jit(solution)/shard_map/psum | solution.py:603
  277.8 2.8 slice_bitcast_fusion.20
  280.7 0.8 slice-done
  281.6 4.5 %convert_element_type.64 = f32[3072,768]{1,0:T(8,128)} convert(bf16[3072,768]{1,0:T(8,128)(2,1)S(1)} %bitcast.92) | non-fusion elementwise | flops 2359296 | bytes 14155776 | tf_op jit(solution)/shard_map/convert_element_type | solution.py:688
  286.0 4.3 %maximum_convert_fusion = f32[768,3072]{1,0:T(8,128)} fusion(bf16[768,768]{1,0:T(8,128)(2,1)S(1)} %get-tuple-element.296, bf16[768,768]{1,0:T(8,128)(2,1)S(1)} %get-tuple-element.297, bf16[768,768]{1,0:T(8,128)(2,1)S(1)} %get-tuple-element.298, bf16[768,768]{1,0:T(8,128)(2,1)S(1)} %get-tuple-element.295), kind=kLoop, calls=%fused_computation.31 | loop fusion | flops 18874368 | bytes 14155776 | tf_op jit(solution)/shard_map/convert_element_type | solution.py:686
  (64 shorter events, 2.8 us)
Async XLA Ops:
  7.2 8.3 %copy-start = (s32[8,512]{1,0:T(8,128)S(1)}, s32[8,512]{1,0:T(8,128)}, u32[]{:S(2)}) copy-start(s32[8,512]{1,0:T(8,128)} %param.26) | copy-start | bytes 49156
  7.2 24.0 %copy-start.7 = (bf16[768,768]{1,0:T(8,128)(2,1)S(1)}, bf16[768,768]{1,0:T(8,128)(2,1)}, u32[]{:S(2)}) copy-start(bf16[768,768]{1,0:T(8,128)(2,1)} %w_out.1) | copy-start | bytes 3538948
  7.2 19.2 %all-to-all-start.3 = ((bf16[8,64,768]{2,1,0:T(8,128)(2,1)}), bf16[8,64,768]{2,1,0:T(8,128)(2,1)S(1)}, u32[]{:S(2)}, u32[]{:S(2)}) async-start(bf16[8,64,768]{2,1,0:T(8,128)(2,1)} %param.22), calls=%async_computation.3 | async-start | bytes 1572864 | tf_op jit(solution)/shard_map/all_to_all | solution.py:541
  26.5 18.6 %all-to-all-start.4 = ((bf16[8,64,768]{2,1,0:T(8,128)(2,1)}), bf16[8,64,768]{2,1,0:T(8,128)(2,1)S(1)}, u32[]{:S(2)}, u32[]{:S(2)}) async-start(bf16[8,64,768]{2,1,0:T(8,128)(2,1)} %param.40), calls=%async_computation.4 | async-start | bytes 1572864 | tf_op jit(solution)/shard_map/all_to_all | solution.py:541
  31.2 246.7 %all-reduce.11.cloned.1.call-start = ((), (), s32[]{:S(2)}) async-start(), calls=%async_computation.5 | async-start | bytes 18874368 | tf_op jit(solution)/shard_map/psum | solution.py:603
  45.1 0.9 copy-start.3
  76.5 1.4 copy-start.11
  78.1 9.8 %copy-start.8 = (s32[2]{0:T(128)}, s32[2]{0:T(128)S(1)}, u32[]{:S(2)}) copy-start(s32[2]{0:T(128)S(1)} %get-tuple-element.81) | copy-start | bytes 28 | tf_op jit(solution)/shard_map/cond
  78.2 9.7 %copy-start.10 = (bf16[544,768]{1,0:T(8,128)(2,1)S(1)}, bf16[544,768]{1,0:T(8,128)(2,1)}, u32[]{:S(2)}) copy-start(bf16[544,768]{1,0:T(8,128)(2,1)} %get-tuple-element.62.q) | copy-start | bytes 2506756 | tf_op jit(solution)/shard_map/cond
  118.9 4.9 %collective-permute-start = (bf16[9728,128]{1,0:T(8,128)(2,1)}, bf16[9728,128]{1,0:T(8,128)(2,1)S(1)}, u32[]{:S(2)}, u32[]{:S(2)}) collective-permute-start(bf16[9728,128]{1,0:T(8,128)(2,1)} %get-tuple-element.83), channel_id=1, source_target_pairs={{0,1},{1,0},{2,3},{3,2},{4,5},{5,4},{6,7},{7,6},{8,9},{9,8},{10,11... | collective-permute-start | bytes 7471112 | tf_op jit(solution)/shard_map/cond/branch_1_fun/ppermute | solution.py:537
  172.6 36.7 %all-to-all-start.1 = ((bf16[64,152,128]{2,1,0:T(8,128)(2,1)}), bf16[64,152,128]{2,1,0:T(8,128)(2,1)S(1)}, u32[]{:S(2)}, u32[]{:S(2)}) async-start(bf16[64,152,128]{2,1,0:T(8,128)(2,1)} %broadcast_in_dim.0), calls=%async_computation.1 | async-start | bytes 4980736 | tf_op jit(solution)/shard_map/cond/branch_1_fun/all_to_all | solution.py:635
  181.4 37.3 %copy-start.9 = (s32[2]{0:T(128)S(1)}, s32[2]{0:T(128)}, u32[]{:S(2)}) copy-start(s32[2]{0:T(128)} %copy-done.8) | copy-start | bytes 28 | tf_op jit(solution)/shard_map/cond
  209.4 1.4 copy-start.2
  210.8 40.1 %all-to-all-start.2 = ((bf16[8,192,768]{2,1,0:T(8,128)(2,1)}), bf16[8,192,768]{2,1,0:T(8,128)(2,1)S(1)}, u32[]{:S(2)}, u32[]{:S(2)}) async-start(bf16[8,192,768]{2,1,0:T(8,128)(2,1)} %pad_maximum_fusion), calls=%async_computation.2 | async-start | bytes 4718592 | tf_op jit(solution)/shard_map/cond/branch_1_fun/all_to_all | solution.py:639
  218.5 34.4 %collective-permute-start.1 = (bf16[9728,128]{1,0:T(8,128)(2,1)}, bf16[9728,128]{1,0:T(8,128)(2,1)}, u32[]{:S(2)}, u32[]{:S(2)}) collective-permute-start(bf16[9728,128]{1,0:T(8,128)(2,1)} %bitcast.93), channel_id=1, source_target_pairs={{0,1},{1,0},{2,3},{3,2},{4,5},{5,4},{6,7},{7,6},{8,9},{9,8},{10,11... | collective-permute-start | bytes 7471112 | tf_op jit(solution)/shard_map/cond/branch_1_fun/ppermute | solution.py:537
  266.4 14.2 %copy-start.4 = (bf16[8,20,768]{2,0,1:T(8,128)(2,1)}, bf16[8,20,768]{2,0,1:T(8,128)(2,1)S(1)}, u32[]{:S(2)}) copy-start(bf16[8,20,768]{2,0,1:T(8,128)(2,1)S(1)} %get-tuple-element.264) | copy-start | bytes 737284
  266.4 14.2 %copy-start.5 = (f32[3072]{0:T(1024)}, f32[3072]{0:T(1024)S(1)}, u32[]{:S(2)}) copy-start(f32[3072]{0:T(1024)S(1)} %get-tuple-element.258) | copy-start | bytes 36868
  266.4 14.2 %copy-start.6 = (f32[768]{0:T(1024)}, f32[768]{0:T(1024)S(1)}, u32[]{:S(2)}) copy-start(f32[768]{0:T(1024)S(1)} %get-tuple-element.262) | copy-start | bytes 9220
  277.8 3.6 %slice-start = ((s8[4718592]{0:T(1024)(128)(4,1)}), s8[4194304]{0:T(1024)(128)(4,1)S(1)}, s32[]{:S(2)}) async-start(s8[4718592]{0:T(1024)(128)(4,1)} %bitcast.91), calls=%async_computation.6 | async-start | bytes 8388608
  277.8 3.7 %slice-start.1 = ((s8[4718592]{0:T(1024)(128)(4,1)}), s8[524288]{0:T(1024)(128)(4,1)S(1)}, s32[]{:S(2)}) async-start(s8[4718592]{0:T(1024)(128)(4,1)} %bitcast.91), calls=%async_computation.7 | async-start | bytes 1048576
  286.0 4.3 %copy-start.1 = (s32[8,512]{1,0:T(8,128)S(1)}, s32[8,512]{1,0:T(8,128)}, u32[]{:S(2)}) copy-start(s32[8,512]{1,0:T(8,128)} %param.26) | copy-start | bytes 49156
Sparse Core Ops, SparseCore 0:
  76.7 201.1 all-reduce.10

commit v3 on v2

--- a/solution.py
+++ b/solution.py
@@ -59,6 +59,18 @@
     mean_grad = jnp.mean(grad, axis=-1, keepdims=True)
     mean_prod = jnp.mean(grad * normal, axis=-1, keepdims=True)
     return scale * (grad - mean_grad - normal * mean_prod)
+
+
+def pack_rows(out, value, split):
+    blocks = out.shape[0]
+    each = split // blocks
+    for block in range(blocks):
+        out[block, :each] = value[block * each : (block + 1) * each]
+        out[block, each:] = value[split:]
+
+
+def column_sum(value):
+    return jnp.sum(value, axis=0, keepdims=True)
 
 
 def attend_kernel(text, mem, w_q, w_k, w_v, lines, lines_all, mark_q, mark_k, w_out,
@@ -151,41 +163,32 @@
     )(text, mem, w_qkv, w_qkv, w_qkv, lines, lines, mark_q, mark_k, w_out)
 
 
-def pack_rows(out, value, split):
-    blocks = out.shape[0]
-    each = split // blocks
-    for block in range(blocks):
-        out[block, :each] = value[block * each : (block + 1) * each]
-        out[block, each:] = value[split:]
-
-
-def column_sum(value):
-    return jnp.sum(value, axis=0, keepdims=True)
-
-
-def feed_kernel(resid_one, lines, w_in, w_down, cot_text, cot_mem,
-                slope_out, hidden_out, result_out, g_two, g_low_out, sums_out, grad_out, act_all):
+def feed_kernel(resid, lines, w_in, w_down, cot_text, cot_mem,
+                result_out, g_two, inner_out, sums_out, sums_in_out, grad_down_out, grad_in_out,
+                hidden_low, hidden_turned, g_low, act_all, slope_all):
     step = pl.program_id(0)
-    half = pl.num_programs(0) // 2
+    down_at = act_all.shape[0]
+    in_at = 2 * down_at
 
     @pl.when(step == 0)
     def _():
-        normal, _ = norm_parts(resid_one[...])
+        normal, _ = norm_parts(resid[...])
         hidden = normal * lines[3:4, :] + lines[4:5, :]
-        hidden_out[...] = hidden.astype(BF16)
+        hidden_low[...] = hidden.astype(BF16)
+        hidden_turned[...] = hidden.astype(BF16).T
         g_two[...] = hidden + lines[5:6, :]
 
-    @pl.when(step < half)
-    def _():
-        inner = dot(hidden_out[...], w_in[...]) + lines[pl.ds(8 + step, 1), :]
+    @pl.when(step < down_at)
+    def _():
+        inner = dot(hidden_low[...], w_in[...]) + lines[pl.ds(8 + step, 1), :]
         phi = 0.5 * (1.0 + lax.erf(inner * (0.5**0.5)))
         act = (inner * phi).astype(BF16)
         act_all[step] = act
         slope = phi + inner * jnp.exp(-0.5 * inner * inner) * 0.3989422804014327
-        slope_out[...] = slope.astype(BF16)
+        slope_all[step] = slope.astype(BF16)
         g_two[...] += dot(act, w_down[...])
 
-    @pl.when(step == half - 1)
+    @pl.when(step == down_at - 1)
     def _():
         normal, scale = norm_parts(g_two[...])
         result = normal * lines[6:7, :] + lines[7:8, :]
@@ -196,137 +199,111 @@
         grad = norm_back(grad * lines[6:7, :], normal, scale)
         sums_out[2:3, :] = column_sum(grad)
         g_two[...] = grad
-        g_low_out[...] = grad.astype(BF16)
-
-    @pl.when(step >= half)
-    def _():
-        grad_out[...] = dot_tn(act_all[step - half], g_low_out[...]).astype(BF16)
-
-
-def feed(resid_one, lines, w_in, w_down, cot_text, cot_mem, packed):
-    count, width = resid_one.shape
+        g_low[...] = grad.astype(BF16)
+
+    @pl.when((step >= down_at) & (step < in_at))
+    def _():
+        grad_down_out[...] = dot_tn(act_all[step - down_at], g_low[...]).astype(BF16)
+
+    @pl.when(step >= in_at)
+    def _():
+        g_inner = dot_nt(g_low[...], w_down[...]) * slope_all[step - in_at].astype(F32)
+        sums_in_out[0:1, :] = column_sum(g_inner)
+        g_inner_low = g_inner.astype(BF16)
+        inner_out[...] = g_inner_low
+        grad_in_out[0] = dot(hidden_turned[...], g_inner_low).astype(BF16)
+
+
+def feed(resid, lines, w_in, w_down, cot_text, cot_mem, packed):
+    count, width = resid.shape
     wide = w_in.shape[1]
-    half = wide // width
-    whole = lambda shape: pl.BlockSpec(shape, lambda j: (0, 0))
-    early = lambda height: pl.BlockSpec((height, width), lambda j: (0, jnp.minimum(j, half - 1)))
+    parts = wide // width
+    in_at = 2 * parts
+    whole = lambda shape: pl.BlockSpec(shape, lambda j: (0,) * len(shape))
+    first_part = lambda j: jnp.minimum(j, parts - 1)
+    last_part = lambda j: jnp.maximum(j - in_at, 0)
+    down_part = lambda j: jnp.where(j < in_at, first_part(j), j - in_at)
     full = whole((count, width))
+    high = jax.ShapeDtypeStruct((count, width), F32)
     return pl.pallas_call(
         feed_kernel,
-        grid=(2 * half,),
+        grid=(3 * parts,),
         in_specs=[
             full,
             whole(lines.shape),
-            early(width),
-            pl.BlockSpec((width, width), lambda j: (jnp.minimum(j, half - 1), 0)),
+            pl.BlockSpec((width, width), lambda j: (0, first_part(j))),
+            pl.BlockSpec((width, width), lambda j: (down_part(j), 0)),
             whole(cot_text.shape),
             whole(cot_mem.shape),
         ],
         out_specs=[
-            early(count),
+            whole(packed),
             full,
-            pl.BlockSpec(packed, lambda j: (0, 0, 0)),
-            full,
-            full,
+            pl.BlockSpec((count, width), lambda j: (0, last_part(j))),
             whole((8, width)),
-            pl.BlockSpec((width, width), lambda j: (jnp.maximum(j - half, 0), 0)),
+            pl.BlockSpec((8, width), lambda j: (0, last_part(j))),
+            pl.BlockSpec((width, width), lambda j: (jnp.clip(j - parts, 0, parts - 1), 0)),
+            pl.BlockSpec((1, width, width), lambda j: (last_part(j), 0, 0)),
         ],
         out_shape=[
+            jax.ShapeDtypeStruct(packed, BF16),
+            high,
             jax.ShapeDtypeStruct((count, wide), BF16),
-            jax.ShapeDtypeStruct((count, width), BF16),
-            jax.ShapeDtypeStruct(packed, BF16),
-            jax.ShapeDtypeStruct((count, width), F32),
-            jax.ShapeDtypeStruct((count, width), BF16),
             jax.ShapeDtypeStruct((8, width), F32),
+            jax.ShapeDtypeStruct((8, wide), F32),
             jax.ShapeDtypeStruct((wide, width), BF16),
-        ],
-        scratch_shapes=[pltpu.VMEM((half, count, width), BF16)],
+            jax.ShapeDtypeStruct((parts, width, width), BF16),
+        ],
+        scratch_shapes=[
+            pltpu.VMEM((count, width), BF16),
+            pltpu.VMEM((width, count), BF16),
+            pltpu.VMEM((count, width), BF16),
+            pltpu.VMEM((parts, count, width), BF16),
+            pltpu.VMEM((parts, count, width), BF16),
+        ],
         compiler_params=pltpu.CompilerParams(vmem_limit_bytes=VMEM_ASK),
-        cost_estimate=cost(20),
+        cost_estimate=cost(28),
         name="feed",
-    )(resid_one, lines, w_in, w_down, cot_text, cot_mem)
-
-
-def inner_back_kernel(g_low, slope, hidden, w_down, grad_out, inner_out, sums_out):
-    g_inner = dot_nt(g_low[...], w_down[...]) * slope[...].astype(F32)
-    sums_out[0:1, :] = column_sum(g_inner)
-    g_inner_low = g_inner.astype(BF16)
-    inner_out[...] = g_inner_low
-    grad_out[0] = dot_tn(hidden[...], g_inner_low).astype(BF16)
-
-
-def inner_back(g_low, slope, hidden, w_down):
-    count, width = g_low.shape
-    wide = slope.shape[1]
-    half = wide // width
-    full = pl.BlockSpec((count, width), lambda j: (0, 0))
-    part = lambda height: pl.BlockSpec((height, width), lambda j: (0, j))
-    return pl.pallas_call(
-        inner_back_kernel,
-        grid=(half,),
-        in_specs=[full, part(count), full, pl.BlockSpec((width, width), lambda j: (j, 0))],
-        out_specs=[
-            pl.BlockSpec((1, width, width), lambda j: (j, 0, 0)),
-            part(count),
-            part(8),
-        ],
-        out_shape=[
-            jax.ShapeDtypeStruct((half, width, width), BF16),
-            jax.ShapeDtypeStruct((count, wide), BF16),
-            jax.ShapeDtypeStruct((8, wide), F32),
-        ],
-        compiler_params=pltpu.CompilerParams(vmem_limit_bytes=VMEM_ASK),
-        cost_estimate=cost(10),
-        name="inner_back",
-    )(g_low, slope, hidden, w_down)
-
-
-def norm_one_back_kernel(g_two, g_inner, w_in, resid_one, lines, g_one, g_one_low, sums_out):
+    )(resid, lines, w_in, w_down, cot_text, cot_mem)
+
+
+def backward_kernel(g_two, g_inner, w_in, resid, lines, text, mem, q, k, v, att, logs, mark_q, mark_k,
+                    w_out, w_q, w_k, w_v, sums_two, sums_in, scalars,
+                    mine_out, theirs_out, packed_out, g_rows, g_low, rows_turned, sums):
     step = pl.program_id(0)
+    parts = pl.num_programs(0) - 3
 
     @pl.when(step == 0)
     def _():
-        g_one[...] = g_two[...]
-
-    g_one[...] += dot_nt(g_inner[...], w_in[...])
-
-    @pl.when(step == pl.num_programs(0) - 1)
-    def _():
-        normal, scale = norm_parts(resid_one[...])
-        g_hidden = g_one[...]
-        sums_out[0:1, :] = column_sum(g_hidden * normal)
-        sums_out[1:2, :] = column_sum(g_hidden)
+        x = jnp.concatenate([text[...], mem[...]], axis=0)
+        rows_turned[...] = x.T
+        g_rows[...] = g_two[...]
+
+    @pl.when(step < parts)
+    def _():
+        g_rows[...] += dot_nt(g_inner[...], w_in[...])
+
+    @pl.when(step == parts - 1)
+    def _():
+        normal, scale = norm_parts(resid[...])
+        g_hidden = g_rows[...]
+        sums[2:3, :] = column_sum(g_hidden * normal)
+        sums[3:4, :] = column_sum(g_hidden)
         grad = norm_back(g_hidden * lines[3:4, :], normal, scale)
-        sums_out[2:3, :] = column_sum(grad)
-        g_one[...] = grad
-        g_one_low[...] = grad.astype(BF16)
-
-
-def norm_one_back(g_two, g_inner, w_in, resid_one, lines):
-    count, width = g_two.shape
-    half = w_in.shape[1] // width
-    whole = lambda shape: pl.BlockSpec(shape, lambda j: (0, 0))
-    part = lambda height: pl.BlockSpec((height, width), lambda j: (0, j))
-    full = whole((count, width))
-    return pl.pallas_call(
-        norm_one_back_kernel,
-        grid=(half,),
-        in_specs=[full, part(count), part(width), full, whole(lines.shape)],
-        out_specs=[full, full, whole((8, width))],
-        out_shape=[
-            jax.ShapeDtypeStruct((count, width), F32),
-            jax.ShapeDtypeStruct((count, width), BF16),
-            jax.ShapeDtypeStruct((8, width), F32),
-        ],
-        compiler_params=pltpu.CompilerParams(vmem_limit_bytes=VMEM_ASK),
-        cost_estimate=cost(8),
-        name="norm_one_back",
-    )(g_two, g_inner, w_in, resid_one, lines)
-
-
-def attend_back_kernel(text, mem, q, k, v, att, logs, mark_q, mark_k, g_one, g_low, w_out,
-                       w_q, w_k, w_v, sums_two, sums_one, sums_in, scalars,
-                       mine_out, theirs_out, packed_out, g_rows, sums):
-    step = pl.program_id(0)
+        sums[4:5, :] = column_sum(grad)
+        g_rows[...] = grad
+        g_low[...] = grad.astype(BF16)
+
+    @pl.when(step >= parts)
+    def _():
+        attend_back_step(step - parts, text, mem, q, k, v, att, logs, mark_q, mark_k, g_low, w_out,
+                         w_q, w_k, w_v, sums_two, sums_in, scalars,
+                         mine_out, theirs_out, packed_out, g_rows, rows_turned, sums)
+
+
+def attend_back_step(step, text, mem, q, k, v, att, logs, mark_q, mark_k, g_low, w_out,
+                     w_q, w_k, w_v, sums_two, sums_in, scalars,
+                     mine_out, theirs_out, packed_out, g_rows, rows_turned, sums):
     core = scalars[0, 1]
     split = text.shape[0]
     count = split + mem.shape[0]
@@ -401,30 +378,23 @@
     columns = pl.ds(pl.multiple_of(256 * step, 256), 256)
     sums[0:1, columns] = column_sum(g_query)
     sums[1:2, columns] = column_sum(g_value)
-    x = jnp.concatenate([text[...], mem[...]], axis=0)
-
-    @pl.when(step == 0)
-    def _():
-        g_rows[...] = g_one[...]
-
     total = g_rows[...]
     for place, (grad, weight) in enumerate(((g_query, w_q), (g_key, w_k), (g_value, w_v))):
         low = grad.astype(BF16)
-        grad_w = dot_tn(x, low).astype(BF16)
+        grad_w = dot(rows_turned[...], low).astype(BF16)
         for block in range(2):
             part = grad_w[:, 128 * block : 128 * block + 128]
             put(place // 2, ((place % 2) * blocks + 2 * step + block) * width, part)
         total += dot_nt(low, weight[...])
     g_rows[...] = total
 
-    @pl.when(step == pl.num_programs(0) - 1)
+    @pl.when(step == 2)
     def _():
         reset = scalars[0, 0] == 1
         g_mem = total[split:]
         zero = jnp.zeros_like(g_mem)
         g_kept = jnp.where(reset, zero, g_mem)
         pack_rows(packed_out, jnp.concatenate([total[:split], g_kept], axis=0).astype(BF16), split)
-        sums[2:5, :] = sums_one[0:3, :]
         sums[5:8, :] = sums_two[0:3, :]
         for place in range(4):
             sums[8 + place : 9 + place, :] = sums_in[0:1, place * width : (place + 1) * width]
@@ -440,19 +410,28 @@
             put(0, base + block * small.shape[0], small[:, 128 * block : 128 * block + 128])
 
 
-def attend_back(text, mem, q, k, v, att, logs, mark_q, mark_k, g_one, g_low, w_out, w_qkv,
-                sums_two, sums_one, sums_in, scalars, packed):
+def backward(g_two, g_inner, w_in, resid, lines, text, mem, q, k, v, att, logs, mark_q, mark_k,
+             w_out, w_qkv, sums_two, sums_in, scalars, packed):
     width = text.shape[1]
     count = text.shape[0] + mem.shape[0]
-    whole = lambda shape: pl.BlockSpec(shape, lambda j: (0, 0))
-    cols = lambda height, base: pl.BlockSpec((height, 256), lambda j: (0, base + j))
+    parts = w_in.shape[1] // width
+    whole = lambda shape: pl.BlockSpec(shape, lambda j: (0,) * len(shape))
+    early = lambda height: pl.BlockSpec((height, width), lambda j: (0, jnp.minimum(j, parts - 1)))
+    quad = lambda j: jnp.maximum(j - parts, 0)
+    cols = lambda height, base: pl.BlockSpec((height, 256), lambda j: (0, base + quad(j)))
     full = whole((count, width))
     mark = whole((count, 128))
     height = 2 * (width // 128) * width + 512
+    half = jax.ShapeDtypeStruct((height, 128), BF16)
     return pl.pallas_call(
-        attend_back_kernel,
-        grid=(3,),
+        backward_kernel,
+        grid=(parts + 3,),
         in_specs=[
+            full,
+            early(count),
+            early(width),
+            full,
+            whole(lines.shape),
             whole(text.shape),
             whole(mem.shape),
             cols(count, 0),
@@ -462,33 +441,27 @@
             mark,
             mark,
             mark,
-            full,
-            full,
-            pl.BlockSpec((256, width), lambda j: (j, 0)),
+            pl.BlockSpec((256, width), lambda j: (quad(j), 0)),
             cols(width, 0),
             cols(width, 3),
             cols(width, 6),
             whole(sums_two.shape),
-            whole(sums_one.shape),
             whole(sums_in.shape),
             pl.BlockSpec(memory_space=pltpu.SMEM),
         ],
-        out_specs=[
-            whole((height, 128)),
-            whole((height, 128)),
-            pl.BlockSpec(packed, lambda j: (0, 0, 0)),
-        ],
-        out_shape=[
-            jax.ShapeDtypeStruct((height, 128), BF16),
-            jax.ShapeDtypeStruct((height, 128), BF16),
-            jax.ShapeDtypeStruct(packed, BF16),
-        ],
-        scratch_shapes=[pltpu.VMEM((count, width), F32), pltpu.VMEM((16, width), F32)],
+        out_specs=[whole((height, 128)), whole((height, 128)), whole(packed)],
+        out_shape=[half, half, jax.ShapeDtypeStruct(packed, BF16)],
+        scratch_shapes=[
+            pltpu.VMEM((count, width), F32),
+            pltpu.VMEM((count, width), BF16),
+            pltpu.VMEM((width, count), BF16),
+            pltpu.VMEM((16, width), F32),
+        ],
         compiler_params=pltpu.CompilerParams(vmem_limit_bytes=VMEM_ASK),
-        cost_estimate=cost(25),
-        name="attend_back",
-    )(text, mem, q, k, v, att, logs, mark_q, mark_k, g_one, g_low, w_out, w_qkv, w_qkv, w_qkv,
-      sums_two, sums_one, sums_in, scalars)
+        cost_estimate=cost(33),
+        name="backward",
+    )(g_two, g_inner, w_in, resid, lines, text, mem, q, k, v, att, logs, mark_q, mark_k,
+      w_out, w_qkv, w_qkv, w_qkv, sums_two, sums_in, scalars)
 
 
 def widen_kernel(mine, got, scalars, qkv_out, out_out):
@@ -533,8 +506,84 @@
     )(mine, got, scalars)
 
 
+def widen_feed_kernel(down, inward, down_out, in_out):
+    down_out[...] = down[...].astype(F32)
+    in_out[...] = inward[0].astype(F32)
+
+
+def widen_feed(down, inward):
+    count, height, width = inward.shape
+    cut = 2
+    rows = height // cut
+    return pl.pallas_call(
+        widen_feed_kernel,
+        grid=(count, cut),
+        in_specs=[
+            pl.BlockSpec((rows, width), lambda j, c: (j * cut + c, 0)),
+            pl.BlockSpec((1, rows, width), lambda j, c: (j, c, 0)),
+        ],
+        out_specs=[
+            pl.BlockSpec((rows, width), lambda j, c: (j * cut + c, 0)),
+            pl.BlockSpec((rows, width), lambda j, c: (c, j)),
+        ],
+        out_shape=[
+            jax.ShapeDtypeStruct(down.shape, F32),
+            jax.ShapeDtypeStruct((height, count * width), F32),
+        ],
+        compiler_params=pltpu.CompilerParams(vmem_limit_bytes=VMEM_ASK),
+        cost_estimate=cost(9),
+        name="widen_feed",
+    )(down, inward)
+
+
+def ring_partner(place, way):
+    return place ^ 1 if way == 0 else 3 - place
+
+
+def ring_pairs(step):
+    pairs = []
+    for place in range(4):
+        for core in range(2):
+            other = ring_partner(place, (step + core) % 2)
+            pairs.append((2 * place + core, 2 * other + core))
+    return pairs
+
+
+def ring_side(axis, step):
+    place, core = lax.axis_index(axis), lax.axis_index("core")
+    return jnp.where((step + core) % 2 == 0, (place + 1) // 2 % 2, place // 2)
+
+
+def ring_swap(value, axis, step):
+    return lax.ppermute(value, (axis, "core"), ring_pairs(step))
+
+
 def core_swap(value):
     return lax.ppermute(value, "core", [(0, 1), (1, 0)])
+
+
+def add_pair(pair):
+    return (pair[0].astype(F32) + pair[1].astype(F32)).astype(BF16)
+
+
+def half_of(pair, side):
+    half = pair[0].shape[0] // 2
+    return add_pair([lax.dynamic_slice_in_dim(part, side * half, half, 0) for part in pair])
+
+
+def ring_halve(pair, axis, step):
+    side = ring_side(axis, step)
+    got = ring_swap(half_of(pair, 1 - side), axis, step)
+    return half_of(pair, side), got
+
+
+def ring_join(value, axis, step):
+    got = ring_swap(value, axis, step)
+    return jnp.where(
+        ring_side(axis, step) == 0,
+        jnp.concatenate([value, got], axis=0),
+        jnp.concatenate([got, value], axis=0),
+    )
 
 
 def to_segments(value):
@@ -596,18 +645,21 @@
     )
     lines = jnp.pad(lines.astype(F32).reshape(-1, width), ((0, 4), (0, 0)))
     q, k, v, att, logs, resid = attend(text, mem, w_qkv, lines, mark_q, mark_k, w_out)
-    slope, hidden, result, g_two, g_two_low, sums_two, grad_down = feed(
+    result, g_two, g_inner, sums_two, sums_in, grad_down, grad_in = feed(
         resid, lines, w_in, w_down, cot_text, cot_mem, packed
     )
-    grad_in, g_inner, sums_in = inner_back(g_two_low, slope, hidden, w_down)
     grad_down, grad_in = lax.psum((grad_down, grad_in), ALL)
     scalars = jnp.stack([my_flag, lax.axis_index("core")]).reshape(1, 2).astype(jnp.int32)
     small_count = mem_count + ROW_PAD + 16
 
     def attention_back(operands):
         result, g_two, g_inner, sums_two, sums_in = operands
-        g_one, g_one_low, sums_one = norm_one_back(g_two, g_inner, w_in, resid, lines)
-        mine, theirs, g_packed = attend_back(
+        mine, theirs, g_packed = backward(
+            g_two,
+            g_inner,
+            w_in,
+            resid,
+            lines,
             text,
             mem,
             q,
@@ -617,36 +669,38 @@
             logs,
             mark_q,
             mark_k,
-            g_one,
-            g_one_low,
             w_out,
             w_qkv,
             sums_two,
-            sums_one,
             sums_in,
             scalars,
             packed,
         )
         both = jnp.concatenate([result, g_packed], axis=1)
-        mine = (mine.astype(F32) + core_swap(theirs).astype(F32)).astype(BF16)
-        parts = mine.reshape(CHIPS, -1, 128)
-        parts = lax.all_to_all(parts, XYZ, 0, 0, tiled=True)
-        part = jnp.sum(parts.astype(F32), axis=0).astype(BF16)
-        parts = lax.all_to_all(
-            jnp.broadcast_to(part[None], parts.shape), XYZ, 0, 0, tiled=True
-        )
-        mine = parts.reshape(mine.shape)
-        both = lax.all_to_all(after(both, mine), BLK, 0, 0, tiled=True)
+        pair = (mine, core_swap(theirs))
+        for step in (0, 1):
+            pair = ring_halve(pair, "z", step)
+        both = lax.all_to_all(after(both, pair[0]), BLK, 0, 0, tiled=True)
+        for step in (0, 1):
+            pair = ring_halve(pair, "x", step)
+        for step in (0, 1):
+            part = add_pair(pair)
+            pair = (part, ring_swap(part, "y", step))
+        mine = add_pair(pair)
+        for step in (1, 0):
+            mine = ring_join(mine, "x", step)
+        mine = ring_join(after(mine, both), "z", 1)
+        pieces = []
+        for base in (0, result.shape[1]):
+            pieces.append(both[:, base : base + tok_count])
+            pieces.append(both[:, base + tok_count : base + tok_count + mem_count])
+        mine = ring_join(mine, "z", 0)
         got = core_swap(mine)
         grad_wqkv, grad_wout = widen(mine, got, scalars, width)
         blocks = width // 128
         small = jnp.where(scalars[0, 1] == 0, mine[-512:], got[-512:])
         small = small[: blocks * small_count].reshape(blocks, small_count, 128)
         small = small.astype(F32).transpose(1, 0, 2).reshape(small_count, width)
-        pieces = []
-        for base in (0, result.shape[1]):
-            pieces.append(both[:, base : base + tok_count])
-            pieces.append(both[:, base + tok_count : base + tok_count + mem_count])
         return grad_wqkv, grad_wout, small, *pieces
 
     def nothing(operands):
@@ -665,6 +719,7 @@
     grad_wqkv, grad_wout, small, output, mem_output, grad_tokens, grad_memory = lax.cond(
         reset_flags[0] >= 0, attention_back, nothing, (result, g_two, g_inner, sums_two, sums_in)
     )
+    grad_down, grad_in = widen_feed(grad_down, grad_in)
     grad_bquery, grad_bvalue, grad_gain1, grad_bias1, grad_bout, grad_gain2, grad_bias2, grad_bdown = (
         small[mem_count + ROW_PAD + row] for row in range(8)
     )
@@ -683,9 +738,9 @@
         grad_bout,
         grad_gain1,
         grad_bias1,
-        jnp.concatenate(list(grad_in), axis=1).astype(F32),
+        grad_in,
         grad_bin,
-        grad_down.astype(F32),
+        grad_down,
         grad_bdown,
         grad_gain2,
         grad_bias2,

time: 298 us -> 291 us (0.977)
  blocking collectives: 44.6 us -> 0 us
  waiting for transfers between devices: 74.1 us -> 102 us
  starting transfers between devices: 25.5 us -> 33.7 us
  local copies, waits for them, and re-layouts: 27.2 us -> 20.7 us
  Pallas kernels: 93.8 us -> 99.2 us
    ppermute x0 -> x10, waiting for transfers between devices: none -> 87.6 us  [ring_swap(): return lax.ppermute(value, (axis, 'core'), ring_pairs(step))]
    all_to_all x2 -> x1, waiting for transfers between devices: 57.9 us -> 8.36 us  [attention_back(): both = lax.all_to_all(after(both, pair[0]), BLK, 0, 0, tiled=True)]
    all_to_all x1 -> x0, blocking collectives: 44.6 us -> none  [attention_back(): parts = lax.all_to_all(parts, XYZ, 0, 0, tiled=True)]
    psum x1, waiting for transfers between devices: 11.4 us -> 0.02 us  [local(): grad_down, grad_in = lax.psum((grad_down, grad_in), ALL)]
    ppermute x0 -> x10, starting transfers between devices: none -> 11.3 us  [ring_swap(): return lax.ppermute(value, (axis, 'core'), ring_pairs(step))]
    select_n x0 -> x4, other arithmetic: none -> 8.31 us  [ring_join(): jnp.where(ring_side(axis, step) == 0, jnp.concatenate([value, got], axis=...]
    pallas_call x4 -> x3, Pallas kernels: 71.3 us -> 76.9 us  [the longest x1 37.3 us: backward(): pl.pallas_call(backward_kernel, grid=(parts + 3,), in_specs=[full, early(...]
    convert_element_type x3 -> x7, other arithmetic: 10.8 us -> 5.61 us  [add_pair(): return (pair[0].astype(F32) + pair[1].astype(F32)).astype(BF16)]
  transfers between devices with their start and end apart: 7 -> 16, of which waited for: 5 -> 13; matrix products, arithmetic and copies ran while one was open for 9% -> 12% of each run, Pallas kernels for 21% -> 21%
where the time goes in v3:
time: 291 us; the launch traced here: 290 us
  waiting for transfers between devices  102 us (35%)
  Pallas kernels  99.2 us (34%)
  starting transfers between devices  33.7 us (12%)
  local copies, waits for them, and re-layouts  20.7 us (7%)
  other arithmetic  17.8 us (6%)
  between operations  15.5 us (5%)
    ppermute x10, waiting for transfers between devices, ring_swap(): return lax.ppermute(value, (axis, 'core'), ring_pairs(step))  87.6 us
    pallas_call x1, Pallas kernels, backward(): pl.pallas_call(backward_kernel, grid=(parts + 3,), in_specs=[full, early(...  37.3 us
    pallas_call x1, Pallas kernels, feed(): pl.pallas_call(feed_kernel, grid=(3 * parts,), in_specs=[full, whole(line...  28.3 us
    pallas_call x1, Pallas kernels, attend(): pl.pallas_call(attend_kernel, grid=(3,), in_specs=[whole(text.shape), who...  13.9 us
    all_to_all x2, starting transfers between devices, to_segments(): return lax.all_to_all(value, BLK, 0, 1, tiled=True)[0]  11.6 us
    ppermute x10, starting transfers between devices, ring_swap(): return lax.ppermute(value, (axis, 'core'), ring_pairs(step))  11.3 us
    pallas_call x1, Pallas kernels, widen_feed(): pl.pallas_call(widen_feed_kernel, grid=(count, cut), in_specs=[pl.BlockSp...  11.2 us
    all_to_all x1, starting transfers between devices, attention_back(): both = lax.all_to_all(after(both, pair[0]), BLK, 0, 0, tiled=True)  8.75 us
  transfers between devices with their start and end apart: 16, of which 13 were waited for; matrix products, arithmetic and copies ran while one was open for 12% of the time, Pallas kernels for 21%

profile of v3, /device:TPU:1, one launch (start us, length us, event | category | flops | bytes accessed | tf_op | source)
XLA Modules:
  0.0 289.8 jit_solution(13727926550194490987)
XLA Ops:
  7.2 6.8 %all-to-all-start.1 = ((bf16[8,64,768]{2,1,0:T(8,128)(2,1)}), bf16[8,64,768]{2,1,0:T(8,128)(2,1)S(1)}, u32[]{:S(2)}, u32[]{:S(2)}) async-start(bf16[8,64,768]{2,1,0:T(8,128)(2,1)} %param.22), calls=%async_computation.1 | async-start | bytes 1572864 | tf_op jit(solution)/shard_map/all_to_all | solution.py:590
  14.0 1.4 fusion.7
  16.2 1.2 constant_dynamic-slice_fusion
  17.4 0.9 dynamic-update-slice
  18.3 0.8 dynamic-update-slice.1
  19.1 0.9 dynamic-update-slice.2
  20.0 0.9 dynamic-update-slice.3
  20.8 0.9 dynamic-update-slice.4
  21.7 0.8 dynamic-update-slice.5
  22.5 0.9 dynamic-update-slice.6
  23.4 0.9 dynamic-update-slice.7
  26.3 4.7 %all-to-all-start.2 = ((bf16[8,64,768]{2,1,0:T(8,128)(2,1)}), bf16[8,64,768]{2,1,0:T(8,128)(2,1)S(1)}, u32[]{:S(2)}, u32[]{:S(2)}) async-start(bf16[8,64,768]{2,1,0:T(8,128)(2,1)} %param.40), calls=%async_computation.2 | async-start | bytes 1572864 | tf_op jit(solution)/shard_map/all_to_all | solution.py:590
  31.1 13.9 %attend.1 = (bf16[544,768]{1,0:T(8,128)(2,1)}, bf16[544,768]{1,0:T(8,128)(2,1)}, bf16[544,768]{1,0:T(8,128)(2,1)}, bf16[544,768]{1,0:T(8,128)(2,1)}, f32[544,128]{1,0:T(8,128)}, /*index=5*/f32[544,768]{1,0:T(8,128)}) custom-call(bf16[512,768]{1,0:T(8,128)(2,1)S(1)} %bitcast.80, bf16[32,768]{1,0:T(8,128)(2,1)S(1)} %pad.32.mem, bf16[768,2304]{1,0:T(8,128)(2,1)} %w_v.1, ...), custom_call_target="tpu_custom_call" | custom-call | flops 15000000512 | tf_op jit(solution)/shard_map/attend/pallas_call | solution.py:129
  45.0 0.9 copy-done.5
  45.9 28.3 %feed.1 = (bf16[8,96,768]{2,1,0:T(8,128)(2,1)}, f32[544,768]{1,0:T(8,128)}, bf16[544,3072]{1,0:T(8,128)(2,1)}, f32[8,768]{1,0:T(8,128)S(1)}, f32[8,3072]{1,0:T(8...) custom-call(f32[544,768]{1,0:T(8,128)} %get-tuple-element.137.resid, ...), custom_call_target="tpu_custom_call" | custom-call | flops 28000000000 | tf_op jit(solution)/shard_map/feed/pallas_call | solution.py:228
  75.6 196.0 %conditional.1 = (f32[768,2304]{1,0:T(8,128)}, f32[768,768]{1,0:T(8,128)}, bf16[48,768]{1,0:T(8,128)(2,1)}, bf16[8,64,768]{2,1,0:T(8,128)(2,1)}, bf16[8,64,768]{...) conditional(s32[]{:T(128)} %bitcast.13, () %tuple.21, ...), branch_computations={%region_0.1_spmd, %region_1.2_spmd} | conditional | flops 39036039168 | bytes 117635632 | solution.py:719
  75.8 37.3 %backward.1 = (bf16[9728,128]{1,0:T(8,128)(2,1)}, bf16[9728,128]{1,0:T(8,128)(2,1)}, bf16[8,96,768]{2,1,0:T(8,128)(2,1)}) custom-call(f32[544,768]{1,0:T(8,128)} %get-tuple-element.60.g_two, bf16[544,3072]{1,0:T(8,128)(2,1)} %get-tuple-element.61.g_inner, bf16[768,3072]{1,0:T(8,128)(2,1)} %get-tuple-element.62.w_in, f32[544,768]{1,0:T(8,128)} %get-tuple-element.63.resid, ...), custom_call_target="tpu_custom_call" | custom-call | flops 32999999488 | tf_op jit(solution)/shard_map/cond/branch_1_fun/backward/pallas_call | solution.py:426
  113.4 4.7 %collective-permute-done = bf16[9728,128]{1,0:T(8,128)(2,1)S(1)} collective-permute-done((bf16[9728,128]{1,0:T(8,128)(2,1)}, bf16[9728,128]{1,0:T(8,128)(2,1)S(1)}, u32[]{:S(2)}, u32[]{:S(2)}) %collective-permute-start) | collective-permute-done | bytes 2490400 | tf_op jit(solution)/shard_map/cond/branch_1_fun/ppermute | solution.py:562
  118.1 1.4 copy-done.3
  119.6 4.1 %add_convert_fusion.1 = (bf16[4864,128]{1,0:T(8,128)(2,1)S(1)}, bf16[4864,128]{1,0:T(8,128)(2,1)}) fusion(bf16[9728,128]{1,0:T(8,128)(2,1)} %copy-done.3, s32[]{:T(128)S(6)} %select_n.156, bf16[9728,128]{1,0:T(8,128)(2,1)} %get-tuple-element.79, s32[]{:T(128)S(6)} %select_n.158), kind=kLoop, calls=%fused_computation.2 | loop fusion | flops 4980736 | bytes 7471112 | tf_op jit(solution)/shard_map/cond/branch_1_fun/convert_element_type | solution.py:566
  123.7 2.6 collective-permute-start.1
  126.3 16.7 %collective-permute-done.1 = bf16[4864,128]{1,0:T(8,128)(2,1)S(1)} collective-permute-done((bf16[4864,128]{1,0:T(8,128)(2,1)}, bf16[4864,128]{1,0:T(8,128)(2,1)S(1)}, u32[]{:S(2)}, u32[]{:S(2)}) %collective-permute-start.1) | collective-permute-done | bytes 1245216 | tf_op jit(solution)/shard_map/cond/branch_1_fun/ppermute | solution.py:558
  143.0 1.1 add_convert_fusion.3
  144.6 9.5 %collective-permute-done.2 = bf16[2432,128]{1,0:T(8,128)(2,1)S(1)} collective-permute-done((bf16[2432,128]{1,0:T(8,128)(2,1)}, bf16[2432,128]{1,0:T(8,128)(2,1)S(1)}, u32[]{:S(2)}, u32[]{:S(2)}) %collective-permute-start.2) | collective-permute-done | bytes 622624 | tf_op jit(solution)/shard_map/cond/branch_1_fun/ppermute | solution.py:558
  154.2 3.2 %collective-permute-start.3 = (bf16[1216,128]{1,0:T(8,128)(2,1)S(1)}, bf16[1216,128]{1,0:T(8,128)(2,1)S(1)}, u32[]{:S(2)}, u32[]{:S(2)}) collective-permute-start(bf16[1216,128]{1,0:T(8,128)(2,1)S(1)} %get-tuple-element.272), channel_id=1, source_target_pairs={{0,8},{1,25},{8,0},{9,17},{16,24},{17,9},{24,16},{25,1},{2,10},{3,... | collective-permute-start | bytes 933896 | tf_op jit(solution)/shard_map/cond/branch_1_fun/ppermute | solution.py:558
  157.4 4.3 %collective-permute-done.3 = bf16[1216,128]{1,0:T(8,128)(2,1)S(1)} collective-permute-done((bf16[1216,128]{1,0:T(8,128)(2,1)S(1)}, bf16[1216,128]{1,0:T(8,128)(2,1)S(1)}, u32[]{:S(2)}, u32[]{:S(2)}) %collective-permute-start.3) | collective-permute-done | bytes 311328 | tf_op jit(solution)/shard_map/cond/branch_1_fun/ppermute | solution.py:558
  161.8 0.8 collective-permute-start.4
  162.5 2.8 pad_maximum_fusion
  165.4 8.7 %all-to-all-start = ((bf16[8,192,768]{2,1,0:T(8,128)(2,1)}), bf16[8,192,768]{2,1,0:T(8,128)(2,1)S(1)}, u32[]{:S(2)}, u32[]{:S(2)}) async-start(bf16[8,192,768]{2,1,0:T(8,128)(2,1)} %pad_maximum_fusion), calls=%async_computation | async-start | bytes 4718592 | tf_op jit(solution)/shard_map/cond/branch_1_fun/all_to_all | solution.py:683
  174.2 2.5 collective-permute-start.5
  176.7 3.3 %collective-permute-done.5 = bf16[608,128]{1,0:T(8,128)(2,1)S(1)} collective-permute-done((bf16[608,128]{1,0:T(8,128)(2,1)S(1)}, bf16[608,128]{1,0:T(8,128)(2,1)S(1)}, u32[]{:S(2)}, u32[]{:S(2)}) %collective-permute-start.5) | collective-permute-done | bytes 155680 | tf_op jit(solution)/shard_map/cond/branch_1_fun/ppermute | solution.py:558
  180.1 4.4 %collective-permute-done.6 = bf16[608,128]{1,0:T(8,128)(2,1)S(1)} collective-permute-done((bf16[608,128]{1,0:T(8,128)(2,1)S(1)}, bf16[608,128]{1,0:T(8,128)(2,1)S(1)}, u32[]{:S(2)}, u32[]{:S(2)}) %collective-permute-start.6) | collective-permute-done | bytes 155680 | tf_op jit(solution)/shard_map/cond/branch_1_fun/ppermute | solution.py:558
  184.6 4.4 %collective-permute-done.7 = bf16[608,128]{1,0:T(8,128)(2,1)S(1)} collective-permute-done((bf16[608,128]{1,0:T(8,128)(2,1)S(1)}, bf16[608,128]{1,0:T(8,128)(2,1)S(1)}, u32[]{:S(2)}, u32[]{:S(2)}) %collective-permute-start.7) | collective-permute-done | bytes 155680 | tf_op jit(solution)/shard_map/cond/branch_1_fun/ppermute | solution.py:558
  189.3 7.7 %collective-permute-done.8 = bf16[1216,128]{1,0:T(8,128)(2,1)} collective-permute-done((bf16[1216,128]{1,0:T(8,128)(2,1)S(1)}, bf16[1216,128]{1,0:T(8,128)(2,1)}, u32[]{:S(2)}, u32[]{:S(2)}) %collective-permute-start.8) | collective-permute-done | bytes 311328 | tf_op jit(solution)/shard_map/cond/branch_1_fun/ppermute | solution.py:558
  197.0 1.2 maximum_select_fusion.2
  198.2 8.4 %all-to-all-done = bf16[8,192,768]{2,1,0:T(8,128)(2,1)S(1)} async-done(((bf16[8,192,768]{2,1,0:T(8,128)(2,1)}), bf16[8,192,768]{2,1,0:T(8,128)(2,1)S(1)}, u32[]{:S(2)}, u32[]{:S(2)}) %all-to-all-start) | async-done | bytes 2359328 | tf_op jit(solution)/shard_map/cond/branch_1_fun/all_to_all | solution.py:683
  206.9 9.1 %collective-permute-done.9 = bf16[2432,128]{1,0:T(8,128)(2,1)} collective-permute-done((bf16[2432,128]{1,0:T(8,128)(2,1)S(1)}, bf16[2432,128]{1,0:T(8,128)(2,1)}, u32[]{:S(2)}, u32[]{:S(2)}) %collective-permute-start.9) | collective-permute-done | bytes 622624 | tf_op jit(solution)/shard_map/cond/branch_1_fun/ppermute | solution.py:558
  216.0 2.7 maximum_select_fusion.1
  218.7 1.0 collective-permute-start.10
  219.7 28.3 %collective-permute-done.10 = bf16[4864,128]{1,0:T(8,128)(2,1)} collective-permute-done((bf16[4864,128]{1,0:T(8,128)(2,1)}, bf16[4864,128]{1,0:T(8,128)(2,1)}, u32[]{:S(2)}, u32[]{:S(2)}) %collective-permute-start.10) | collective-permute-done | bytes 1245216 | tf_op jit(solution)/shard_map/cond/branch_1_fun/ppermute | solution.py:558
  248.1 4.3 %maximum_select_fusion.mine = bf16[9728,128]{1,0:T(8,128)(2,1)S(1)} fusion(bf16[4864,128]{1,0:T(8,128)(2,1)} %collective-permute-done.10, bf16[4864,128]{1,0:T(8,128)(2,1)} %maximum_select_fusion.1, pred[]{:T(512)S(6)} %eq.55), kind=kLoop, calls=%fused_computation | loop fusion | flops 11206656 | bytes 4980737 | tf_op jit(solution)/shard_map/cond/branch_1_fun/jit(_where)/select_n | solution.py:582
  252.4 1.8 collective-permute-start.11
  255.5 0.7 copy.69
  256.2 1.2 fusion.6
  257.5 1.0 collective-permute-done.11.got
  258.6 0.8 slice_bitcast_fusion
  263.2 8.5 %widen.1 = (f32[768,2304]{1,0:T(8,128)}, f32[768,768]{1,0:T(8,128)}) custom-call(bf16[9728,128]{1,0:T(8,128)(2,1)} %copy-done.2, bf16[9728,128]{1,0:T(8,128)(2,1)} %copy-done.7, s32[1,2]{1,0:T(1,128)S(1)} %bitcast.98), custom_call_target="tpu_custom_call" | custom-call | flops 6000000000 | tf_op jit(solution)/shard_map/cond/branch_1_fun/widen/pallas_call | solution.py:491
  271.7 11.2 %widen_feed.1 = (f32[3072,768]{1,0:T(8,128)}, f32[768,3072]{1,0:T(8,128)}) custom-call(bf16[3072,768]{1,0:T(8,128)(2,1)} %get-tuple-element.261.down, bf16[4,768,768]{2,1,0:T(8,128)(2,1)} %get-tuple-element.262.inward), custom_call_target="tpu_custom_call" | custom-call | flops 8999999488 | tf_op jit(solution)/shard_map/widen_feed/pallas_call | solution.py:518
  (80 shorter events, 9.4 us)
Async XLA Ops:
  7.2 8.2 %copy-start = (s32[8,512]{1,0:T(8,128)S(1)}, s32[8,512]{1,0:T(8,128)}, u32[]{:S(2)}) copy-start(s32[8,512]{1,0:T(8,128)} %param.26) | copy-start | bytes 49156
  7.2 19.1 %all-to-all-start.1 = ((bf16[8,64,768]{2,1,0:T(8,128)(2,1)}), bf16[8,64,768]{2,1,0:T(8,128)(2,1)S(1)}, u32[]{:S(2)}, u32[]{:S(2)}) async-start(bf16[8,64,768]{2,1,0:T(8,128)(2,1)} %param.22), calls=%async_computation.1 | async-start | bytes 1572864 | tf_op jit(solution)/shard_map/all_to_all | solution.py:590
  14.0 17.0 %copy-start.8 = (bf16[768,768]{1,0:T(8,128)(2,1)S(1)}, bf16[768,768]{1,0:T(8,128)(2,1)}, u32[]{:S(2)}) copy-start(bf16[768,768]{1,0:T(8,128)(2,1)} %w_out.1) | copy-start | bytes 3538948
  26.3 18.6 %all-to-all-start.2 = ((bf16[8,64,768]{2,1,0:T(8,128)(2,1)}), bf16[8,64,768]{2,1,0:T(8,128)(2,1)S(1)}, u32[]{:S(2)}, u32[]{:S(2)}) async-start(bf16[8,64,768]{2,1,0:T(8,128)(2,1)} %param.40), calls=%async_computation.2 | async-start | bytes 1572864 | tf_op jit(solution)/shard_map/all_to_all | solution.py:590
  31.1 240.6 %all-reduce.11.cloned.1.call-start = ((), (), s32[]{:S(2)}) async-start(), calls=%async_computation.3 | async-start | bytes 18874368 | tf_op jit(solution)/shard_map/psum | solution.py:651
  45.0 0.9 copy-start.5
  74.2 1.4 copy-start.11
  75.8 37.3 %copy-start.9 = (s32[2]{0:T(128)}, s32[2]{0:T(128)S(1)}, u32[]{:S(2)}) copy-start(s32[2]{0:T(128)S(1)} %get-tuple-element.78) | copy-start | bytes 28 | tf_op jit(solution)/shard_map/cond
  113.1 5.0 %collective-permute-start = (bf16[9728,128]{1,0:T(8,128)(2,1)}, bf16[9728,128]{1,0:T(8,128)(2,1)S(1)}, u32[]{:S(2)}, u32[]{:S(2)}) collective-permute-start(bf16[9728,128]{1,0:T(8,128)(2,1)} %get-tuple-element.80), channel_id=1, source_target_pairs={{0,1},{1,0},{2,3},{3,2},{4,5},{5,4},{6,7},{7,6},{8,9},{9,8},{10,11... | collective-permute-start | bytes 7471112 | tf_op jit(solution)/shard_map/cond/branch_1_fun/ppermute | solution.py:562
  118.1 1.4 copy-start.3
  123.7 19.3 %collective-permute-start.1 = (bf16[4864,128]{1,0:T(8,128)(2,1)}, bf16[4864,128]{1,0:T(8,128)(2,1)S(1)}, u32[]{:S(2)}, u32[]{:S(2)}) collective-permute-start(bf16[4864,128]{1,0:T(8,128)(2,1)} %get-tuple-element.264), channel_id=1, source_target_pairs={{0,2},{1,7},{2,0},{3,5},{4,6},{5,3},{6,4},{7,1},{8,10},{9,15},{10,... | collective-permute-start | bytes 3735560 | tf_op jit(solution)/shard_map/cond/branch_1_fun/ppermute | solution.py:558
  144.1 18.4 %copy-start.4 = (bf16[8,96,768]{2,1,0:T(8,128)(2,1)S(1)}, bf16[8,96,768]{2,1,0:T(8,128)(2,1)}, u32[]{:S(2)}) copy-start(bf16[8,96,768]{2,1,0:T(8,128)(2,1)} %get-tuple-element.81) | copy-start | bytes 3538948 | tf_op jit(solution)/shard_map/cond
  144.1 9.9 %collective-permute-start.2 = (bf16[2432,128]{1,0:T(8,128)(2,1)}, bf16[2432,128]{1,0:T(8,128)(2,1)S(1)}, u32[]{:S(2)}, u32[]{:S(2)}) collective-permute-start(bf16[2432,128]{1,0:T(8,128)(2,1)} %get-tuple-element.266), channel_id=1, source_target_pairs={{0,6},{1,3},{2,4},{3,1},{4,2},{5,7},{6,0},{7,5},{8,14},{9,11},{10,... | collective-permute-start | bytes 1867784 | tf_op jit(solution)/shard_map/cond/branch_1_fun/ppermute | solution.py:558
  154.2 7.5 %collective-permute-start.3 = (bf16[1216,128]{1,0:T(8,128)(2,1)S(1)}, bf16[1216,128]{1,0:T(8,128)(2,1)S(1)}, u32[]{:S(2)}, u32[]{:S(2)}) collective-permute-start(bf16[1216,128]{1,0:T(8,128)(2,1)S(1)} %get-tuple-element.272), channel_id=1, source_target_pairs={{0,8},{1,25},{8,0},{9,17},{16,24},{17,9},{24,16},{25,1},{2,10},{3,... | collective-permute-start | bytes 933896 | tf_op jit(solution)/shard_map/cond/branch_1_fun/ppermute | solution.py:558
  161.8 12.4 %collective-permute-start.4 = (bf16[608,128]{1,0:T(8,128)(2,1)S(1)}, bf16[608,128]{1,0:T(8,128)(2,1)S(1)}, u32[]{:S(2)}, u32[]{:S(2)}) collective-permute-start(bf16[608,128]{1,0:T(8,128)(2,1)S(1)} %add_convert_fusion.9), channel_id=1, source_target_pairs={{0,24},{1,9},{8,16},{9,1},{16,8},{17,25},{24,0},{25,17},{2,26},{3,... | collective-permute-start | bytes 466952 | tf_op jit(solution)/shard_map/cond/branch_1_fun/ppermute | solution.py:558
  165.4 41.2 %all-to-all-start = ((bf16[8,192,768]{2,1,0:T(8,128)(2,1)}), bf16[8,192,768]{2,1,0:T(8,128)(2,1)S(1)}, u32[]{:S(2)}, u32[]{:S(2)}) async-start(bf16[8,192,768]{2,1,0:T(8,128)(2,1)} %pad_maximum_fusion), calls=%async_computation | async-start | bytes 4718592 | tf_op jit(solution)/shard_map/cond/branch_1_fun/all_to_all | solution.py:683
  174.2 5.8 %collective-permute-start.5 = (bf16[608,128]{1,0:T(8,128)(2,1)S(1)}, bf16[608,128]{1,0:T(8,128)(2,1)S(1)}, u32[]{:S(2)}, u32[]{:S(2)}) collective-permute-start(bf16[608,128]{1,0:T(8,128)(2,1)S(1)} %add_convert_fusion.8), channel_id=1, source_target_pairs={{0,32},{1,97},{32,0},{33,65},{64,96},{65,33},{96,64},{97,1},{2,34}... | collective-permute-start | bytes 466952 | tf_op jit(solution)/shard_map/cond/branch_1_fun/ppermute | solution.py:558
  180.0 4.5 %collective-permute-start.6 = (bf16[608,128]{1,0:T(8,128)(2,1)S(1)}, bf16[608,128]{1,0:T(8,128)(2,1)S(1)}, u32[]{:S(2)}, u32[]{:S(2)}) collective-permute-start(bf16[608,128]{1,0:T(8,128)(2,1)S(1)} %add_convert_fusion.7), channel_id=1, source_target_pairs={{0,96},{1,33},{32,64},{33,1},{64,32},{65,97},{96,0},{97,65},{2,98}... | collective-permute-start | bytes 466952 | tf_op jit(solution)/shard_map/cond/branch_1_fun/ppermute | solution.py:558
  184.5 4.5 %collective-permute-start.7 = (bf16[608,128]{1,0:T(8,128)(2,1)S(1)}, bf16[608,128]{1,0:T(8,128)(2,1)S(1)}, u32[]{:S(2)}, u32[]{:S(2)}) collective-permute-start(bf16[608,128]{1,0:T(8,128)(2,1)S(1)} %add_convert_fusion.6), channel_id=1, source_target_pairs={{0,24},{1,9},{8,16},{9,1},{16,8},{17,25},{24,0},{25,17},{2,26},{3,... | collective-permute-start | bytes 466952 | tf_op jit(solution)/shard_map/cond/branch_1_fun/ppermute | solution.py:558
  189.1 7.9 %collective-permute-start.8 = (bf16[1216,128]{1,0:T(8,128)(2,1)S(1)}, bf16[1216,128]{1,0:T(8,128)(2,1)}, u32[]{:S(2)}, u32[]{:S(2)}) collective-permute-start(bf16[1216,128]{1,0:T(8,128)(2,1)S(1)} %maximum_select_fusion.3), channel_id=1, source_target_pairs={{0,8},{1,25},{8,0},{9,17},{16,24},{17,9},{24,16},{25,1},{2,10},{3,... | collective-permute-start | bytes 933896 | tf_op jit(solution)/shard_map/cond/branch_1_fun/ppermute | solution.py:558
  206.6 9.5 %collective-permute-start.9 = (bf16[2432,128]{1,0:T(8,128)(2,1)S(1)}, bf16[2432,128]{1,0:T(8,128)(2,1)}, u32[]{:S(2)}, u32[]{:S(2)}) collective-permute-start(bf16[2432,128]{1,0:T(8,128)(2,1)S(1)} %maximum_select_fusion.2), channel_id=1, source_target_pairs={{0,6},{1,3},{2,4},{3,1},{4,2},{5,7},{6,0},{7,5},{8,14},{9,11},{10,... | collective-permute-start | bytes 1867784 | tf_op jit(solution)/shard_map/cond/branch_1_fun/ppermute | solution.py:558
  218.7 29.3 %collective-permute-start.10 = (bf16[4864,128]{1,0:T(8,128)(2,1)}, bf16[4864,128]{1,0:T(8,128)(2,1)}, u32[]{:S(2)}, u32[]{:S(2)}) collective-permute-start(bf16[4864,128]{1,0:T(8,128)(2,1)} %maximum_select_fusion.1), channel_id=1, source_target_pairs={{0,2},{1,7},{2,0},{3,5},{4,6},{5,3},{6,4},{7,1},{8,10},{9,15},{10,... | collective-permute-start | bytes 3735560 | tf_op jit(solution)/shard_map/cond/branch_1_fun/ppermute | solution.py:558
  219.7 34.4 %copy-start.10 = (s32[2]{0:T(128)S(1)}, s32[2]{0:T(128)}, u32[]{:S(2)}) copy-start(s32[2]{0:T(128)} %copy-done.9) | copy-start | bytes 28 | tf_op jit(solution)/shard_map/cond
  252.4 5.1 %copy-start.2 = (bf16[9728,128]{1,0:T(8,128)(2,1)}, bf16[9728,128]{1,0:T(8,128)(2,1)S(1)}, u32[]{:S(2)}) copy-start(bf16[9728,128]{1,0:T(8,128)(2,1)S(1)} %maximum_select_fusion.mine) | copy-start | bytes 7471108 | tf_op jit(solution)/shard_map/cond
  252.4 6.1 %collective-permute-start.11 = (bf16[9728,128]{1,0:T(8,128)(2,1)S(1)}, bf16[9728,128]{1,0:T(8,128)(2,1)S(1)}, u32[]{:S(2)}, u32[]{:S(2)}) collective-permute-start(bf16[9728,128]{1,0:T(8,128)(2,1)S(1)} %maximum_select_fusion.mine), channel_id=1, source_target_pairs={{0,1},{1,0},{2,3},{3,2},{4,5},{5,4},{6,7},{7,6},{8,9},{9,8},{10,11... | collective-permute-start | bytes 7471112 | tf_op jit(solution)/shard_map/cond/branch_1_fun/ppermute | solution.py:562
  258.5 1.6 copy-start.7
  271.6 11.3 %copy-start.6 = (bf16[8,20,768]{2,0,1:T(8,128)(2,1)}, bf16[8,20,768]{2,0,1:T(8,128)(2,1)S(1)}, u32[]{:S(2)}) copy-start(bf16[8,20,768]{2,0,1:T(8,128)(2,1)S(1)} %get-tuple-element.260) | copy-start | bytes 737284
  271.7 11.3 %copy-start.1 = (s32[8,512]{1,0:T(8,128)S(1)}, s32[8,512]{1,0:T(8,128)}, u32[]{:S(2)}) copy-start(s32[8,512]{1,0:T(8,128)} %param.26) | copy-start | bytes 49156
Sparse Core Ops, SparseCore 0:
  74.3 173.5 all-reduce.10

commit v4 on v3

--- a/solution.py
+++ b/solution.py
@@ -17,6 +17,8 @@
 XYZ = ("x", "y", "z")
 CHIPS = 64
 ROW_PAD = 12
+SPARE_ROWS = 320
+RING = ("z", "x", "y")
 
 
 def dot(left, right):
@@ -61,12 +63,13 @@
     return scale * (grad - mean_grad - normal * mean_prod)
 
 
-def pack_rows(out, value, split):
+def pack_rows(out, value, split, base=0):
     blocks = out.shape[0]
     each = split // blocks
+    rest = value.shape[0] - split
     for block in range(blocks):
-        out[block, :each] = value[block * each : (block + 1) * each]
-        out[block, each:] = value[split:]
+        out[block, base : base + each] = value[block * each : (block + 1) * each]
+        out[block, base + each : base + each + rest] = value[split:]
 
 
 def column_sum(value):
@@ -167,8 +170,9 @@
                 result_out, g_two, inner_out, sums_out, sums_in_out, grad_down_out, grad_in_out,
                 hidden_low, hidden_turned, g_low, act_all, slope_all):
     step = pl.program_id(0)
-    down_at = act_all.shape[0]
-    in_at = 2 * down_at
+    half = pl.num_programs(0) // 2
+    width = resid.shape[1]
+    cuts = w_in.shape[1] // width
 
     @pl.when(step == 0)
     def _():
@@ -178,17 +182,22 @@
         hidden_turned[...] = hidden.astype(BF16).T
         g_two[...] = hidden + lines[5:6, :]
 
-    @pl.when(step < down_at)
-    def _():
-        inner = dot(hidden_low[...], w_in[...]) + lines[pl.ds(8 + step, 1), :]
-        phi = 0.5 * (1.0 + lax.erf(inner * (0.5**0.5)))
-        act = (inner * phi).astype(BF16)
-        act_all[step] = act
-        slope = phi + inner * jnp.exp(-0.5 * inner * inner) * 0.3989422804014327
-        slope_all[step] = slope.astype(BF16)
-        g_two[...] += dot(act, w_down[...])
-
-    @pl.when(step == down_at - 1)
+    @pl.when(step < half)
+    def _():
+        total = g_two[...]
+        for cut in range(cuts):
+            span = slice(cut * width, (cut + 1) * width)
+            part = step * cuts + cut
+            inner = dot(hidden_low[...], w_in[:, span]) + lines[pl.ds(8 + part, 1), :]
+            phi = 0.5 * (1.0 + lax.erf(inner * (0.5**0.5)))
+            act = (inner * phi).astype(BF16)
+            act_all[part] = act
+            slope = phi + inner * jnp.exp(-0.5 * inner * inner) * 0.3989422804014327
+            slope_all[part] = slope.astype(BF16)
+            total += dot(act, w_down[span, :])
+        g_two[...] = total
+
+    @pl.when(step == half - 1)
     def _():
         normal, scale = norm_parts(g_two[...])
         result = normal * lines[6:7, :] + lines[7:8, :]
@@ -201,49 +210,48 @@
         g_two[...] = grad
         g_low[...] = grad.astype(BF16)
 
-    @pl.when((step >= down_at) & (step < in_at))
-    def _():
-        grad_down_out[...] = dot_tn(act_all[step - down_at], g_low[...]).astype(BF16)
-
-    @pl.when(step >= in_at)
-    def _():
-        g_inner = dot_nt(g_low[...], w_down[...]) * slope_all[step - in_at].astype(F32)
-        sums_in_out[0:1, :] = column_sum(g_inner)
-        g_inner_low = g_inner.astype(BF16)
-        inner_out[...] = g_inner_low
-        grad_in_out[0] = dot(hidden_turned[...], g_inner_low).astype(BF16)
+    @pl.when(step >= half)
+    def _():
+        for cut in range(cuts):
+            span = slice(cut * width, (cut + 1) * width)
+            part = (step - half) * cuts + cut
+            g_inner = dot_nt(g_low[...], w_down[span, :]) * slope_all[part].astype(F32)
+            sums_in_out[0:1, span] = column_sum(g_inner)
+            g_inner_low = g_inner.astype(BF16)
+            inner_out[:, span] = g_inner_low
+            grad_down_out[span, :] = dot_tn(act_all[part], g_low[...]).astype(BF16)
+            grad_in_out[cut] = dot(hidden_turned[...], g_inner_low).astype(BF16)
 
 
 def feed(resid, lines, w_in, w_down, cot_text, cot_mem, packed):
     count, width = resid.shape
     wide = w_in.shape[1]
-    parts = wide // width
-    in_at = 2 * parts
+    parts, cuts = wide // width, 2
+    half = parts // cuts
+    chunk = cuts * width
     whole = lambda shape: pl.BlockSpec(shape, lambda j: (0,) * len(shape))
-    first_part = lambda j: jnp.minimum(j, parts - 1)
-    last_part = lambda j: jnp.maximum(j - in_at, 0)
-    down_part = lambda j: jnp.where(j < in_at, first_part(j), j - in_at)
+    late = lambda j: jnp.maximum(j - half, 0)
     full = whole((count, width))
     high = jax.ShapeDtypeStruct((count, width), F32)
     return pl.pallas_call(
         feed_kernel,
-        grid=(3 * parts,),
+        grid=(2 * half,),
         in_specs=[
             full,
             whole(lines.shape),
-            pl.BlockSpec((width, width), lambda j: (0, first_part(j))),
-            pl.BlockSpec((width, width), lambda j: (down_part(j), 0)),
+            pl.BlockSpec((width, chunk), lambda j: (0, jnp.minimum(j, half - 1))),
+            pl.BlockSpec((chunk, width), lambda j: (j % half, 0)),
             whole(cot_text.shape),
             whole(cot_mem.shape),
         ],
         out_specs=[
             whole(packed),
             full,
-            pl.BlockSpec((count, width), lambda j: (0, last_part(j))),
+            pl.BlockSpec((count, chunk), lambda j: (0, late(j))),
             whole((8, width)),
-            pl.BlockSpec((8, width), lambda j: (0, last_part(j))),
-            pl.BlockSpec((width, width), lambda j: (jnp.clip(j - parts, 0, parts - 1), 0)),
-            pl.BlockSpec((1, width, width), lambda j: (last_part(j), 0, 0)),
+            pl.BlockSpec((8, chunk), lambda j: (0, late(j))),
+            pl.BlockSpec((chunk, width), lambda j: (late(j), 0)),
+            pl.BlockSpec((cuts, width, width), lambda j: (late(j), 0, 0)),
         ],
         out_shape=[
             jax.ShapeDtypeStruct(packed, BF16),
@@ -268,7 +276,7 @@
 
 
 def backward_kernel(g_two, g_inner, w_in, resid, lines, text, mem, q, k, v, att, logs, mark_q, mark_k,
-                    w_out, w_q, w_k, w_v, sums_two, sums_in, scalars,
+                    w_out, w_q, w_k, w_v, sums_two, sums_in, scalars, result,
                     mine_out, theirs_out, packed_out, g_rows, g_low, rows_turned, sums):
     step = pl.program_id(0)
     parts = pl.num_programs(0) - 3
@@ -278,6 +286,7 @@
         x = jnp.concatenate([text[...], mem[...]], axis=0)
         rows_turned[...] = x.T
         g_rows[...] = g_two[...]
+        packed_out[:, : result.shape[1]] = result[...]
 
     @pl.when(step < parts)
     def _():
@@ -322,10 +331,11 @@
             theirs_out[rows, :] = part
 
     blocks = width // 128
+    group_rows = mine_out.shape[0] // 2
     grad_w_out = dot_tn(attended, g_low[...]).astype(BF16)
     for block in range(blocks):
         part = grad_w_out[:, 128 * block : 128 * block + 128]
-        put(1, (blocks + block) * width + 256 * step, part)
+        put(1, group_rows + block * width + 256 * step, part)
     g_att = dot_nt(g_low[...], w_out[...])
     g_att_low = g_att.astype(BF16)
     scaled = query * jnp.asarray(0.125, BF16)
@@ -384,7 +394,7 @@
         grad_w = dot(rows_turned[...], low).astype(BF16)
         for block in range(2):
             part = grad_w[:, 128 * block : 128 * block + 128]
-            put(place // 2, ((place % 2) * blocks + 2 * step + block) * width, part)
+            put(place // 2, (place % 2) * group_rows + (2 * step + block) * width, part)
         total += dot_nt(low, weight[...])
     g_rows[...] = total
 
@@ -394,35 +404,41 @@
         g_mem = total[split:]
         zero = jnp.zeros_like(g_mem)
         g_kept = jnp.where(reset, zero, g_mem)
-        pack_rows(packed_out, jnp.concatenate([total[:split], g_kept], axis=0).astype(BF16), split)
+        g_all = jnp.concatenate([total[:split], g_kept], axis=0).astype(BF16)
+        pack_rows(packed_out, g_all, split, packed_out.shape[1] // 2)
         sums[5:8, :] = sums_two[0:3, :]
         for place in range(4):
             sums[8 + place : 9 + place, :] = sums_in[0:1, place * width : (place + 1) * width]
         sums[12:16, :] = jnp.zeros((4, width), F32)
         small = [jnp.where(reset, g_mem, zero).astype(BF16), sums[...].astype(BF16)]
         small = jnp.concatenate(small, axis=0)
-        base = 2 * blocks * width
-        spare = mine_out.shape[0] - base
-        empty = jnp.zeros((spare, 128), BF16)
-        mine_out[base:, :] = empty
-        theirs_out[base:, :] = empty
-        for block in range(blocks):
-            put(0, base + block * small.shape[0], small[:, 128 * block : 128 * block + 128])
+        base = blocks * width
+        empty = jnp.zeros((SPARE_ROWS, 128), BF16)
+        for place in range(2):
+            rows = slice(place * group_rows + base, (place + 1) * group_rows)
+            mine_out[rows, :] = empty
+            theirs_out[rows, :] = empty
+        for place in range(2):
+            for block in range(blocks):
+                start = place * group_rows + base + block * small.shape[0]
+                put(0, start, small[:, 128 * block : 128 * block + 128])
 
 
 def backward(g_two, g_inner, w_in, resid, lines, text, mem, q, k, v, att, logs, mark_q, mark_k,
-             w_out, w_qkv, sums_two, sums_in, scalars, packed):
+             w_out, w_qkv, sums_two, sums_in, scalars, result):
     width = text.shape[1]
     count = text.shape[0] + mem.shape[0]
-    parts = w_in.shape[1] // width
+    chunk = 2 * width
+    parts = w_in.shape[1] // chunk
     whole = lambda shape: pl.BlockSpec(shape, lambda j: (0,) * len(shape))
-    early = lambda height: pl.BlockSpec((height, width), lambda j: (0, jnp.minimum(j, parts - 1)))
+    early = lambda height: pl.BlockSpec((height, chunk), lambda j: (0, jnp.minimum(j, parts - 1)))
     quad = lambda j: jnp.maximum(j - parts, 0)
     cols = lambda height, base: pl.BlockSpec((height, 256), lambda j: (0, base + quad(j)))
     full = whole((count, width))
     mark = whole((count, 128))
-    height = 2 * (width // 128) * width + 512
+    height = 2 * (width // 128 * width + SPARE_ROWS)
     half = jax.ShapeDtypeStruct((height, 128), BF16)
+    packed = (result.shape[0], 2 * result.shape[1], width)
     return pl.pallas_call(
         backward_kernel,
         grid=(parts + 3,),
@@ -448,6 +464,7 @@
             whole(sums_two.shape),
             whole(sums_in.shape),
             pl.BlockSpec(memory_space=pltpu.SMEM),
+            whole(result.shape),
         ],
         out_specs=[whole((height, 128)), whole((height, 128)), whole(packed)],
         out_shape=[half, half, jax.ShapeDtypeStruct(packed, BF16)],
@@ -461,74 +478,124 @@
         cost_estimate=cost(33),
         name="backward",
     )(g_two, g_inner, w_in, resid, lines, text, mem, q, k, v, att, logs, mark_q, mark_k,
-      w_out, w_qkv, w_qkv, w_qkv, sums_two, sums_in, scalars)
-
-
-def widen_kernel(mine, got, scalars, qkv_out, out_out):
-    group = pl.program_id(0)
-    own = group // 2 == scalars[0, 1]
-    width = out_out.shape[0]
-
-    def fill(ref):
+      w_out, w_qkv, w_qkv, w_qkv, sums_two, sums_in, scalars, result)
+
+
+def widen_kernel(first, second, groups, *refs):
+    early = len(refs) == 5
+    if early:
+        qkv_out, out_out, small_out, wide, sems = refs
+    else:
+        qkv_out, out_out, wide, sems = refs[-4:]
+    width = wide.shape[1]
+
+    def copies(place):
+        group = groups[0, place]
+        columns = pl.ds(pl.multiple_of(jnp.minimum(group, 2) * width, width), width)
+        to_qkv = pltpu.make_async_copy(wide.at[place], qkv_out.at[:, columns], sems.at[place])
+        to_out = pltpu.make_async_copy(wide.at[place], out_out, sems.at[place])
+        return group < 3, to_qkv, to_out
+
+    for place, piece in enumerate((first, second)):
         for block in range(width // 128):
             rows = slice(block * width, (block + 1) * width)
-            ref[:, 128 * block : 128 * block + 128] = jnp.where(
-                own, mine[rows, :].astype(F32), got[rows, :].astype(F32)
-            )
-
-    @pl.when(group < 3)
-    def _():
-        fill(qkv_out)
-
-    @pl.when(group == 3)
-    def _():
-        fill(out_out)
-
-
-def widen(mine, got, scalars, width):
-    tall = width // 128 * width
-    half = pl.BlockSpec((tall, 128), lambda g: (g % 2, 0))
+            wide[place, :, 128 * block : 128 * block + 128] = piece[rows, :].astype(F32)
+        in_qkv, to_qkv, to_out = copies(place)
+
+        if early:
+
+            @pl.when(groups[0, place] < 2)
+            def _():
+                height = small_out.shape[0]
+                for block in range(width // 128):
+                    start = width // 128 * width + block * height
+                    part = piece[start : start + height, :].astype(F32)
+                    small_out[:, 128 * block : 128 * block + 128] = part
+
+        @pl.when(in_qkv)
+        def _():
+            to_qkv.start()
+
+        @pl.when(jnp.logical_not(in_qkv))
+        def _():
+            to_out.start()
+
+    for place in range(2):
+        in_qkv, to_qkv, to_out = copies(place)
+
+        @pl.when(in_qkv)
+        def _():
+            to_qkv.wait()
+
+        @pl.when(jnp.logical_not(in_qkv))
+        def _():
+            to_out.wait()
+
+
+def widen(first, second, groups, width, partly=()):
+    vmem = pl.BlockSpec(memory_space=pltpu.VMEM)
+    hbm = pl.BlockSpec(memory_space=pl.ANY)
     return pl.pallas_call(
         widen_kernel,
-        grid=(4,),
-        in_specs=[half, half, pl.BlockSpec(memory_space=pltpu.SMEM)],
-        out_specs=[
-            pl.BlockSpec((width, width), lambda g: (0, jnp.minimum(g, 2))),
-            pl.BlockSpec((width, width), lambda g: (0, 0)),
-        ],
+        in_specs=[vmem, vmem, pl.BlockSpec(memory_space=pltpu.SMEM)]
+        + [hbm] * len(partly),
+        out_specs=[hbm, hbm] + ([] if partly else [vmem]),
         out_shape=[
             jax.ShapeDtypeStruct((width, 3 * width), F32),
             jax.ShapeDtypeStruct((width, width), F32),
-        ],
+        ]
+        + ([] if partly else [jax.ShapeDtypeStruct((48, width), F32)]),
+        scratch_shapes=[pltpu.VMEM((2, width, width), F32), pltpu.SemaphoreType.DMA((2,))],
+        input_output_aliases={3: 0, 4: 1} if partly else {},
         compiler_params=pltpu.CompilerParams(vmem_limit_bytes=VMEM_ASK),
-        cost_estimate=cost(6),
+        cost_estimate=cost(4),
         name="widen",
-    )(mine, got, scalars)
-
-
-def widen_feed_kernel(down, inward, down_out, in_out):
-    down_out[...] = down[...].astype(F32)
-    in_out[...] = inward[0].astype(F32)
+    )(first, second, groups, *partly)
+
+
+def widen_feed_kernel(down, inward, down_out, in_out, low, high, in_sems, out_sems):
+    count, width = inward.shape[0], inward.shape[2]
+    low_rows = low.shape[1]
+    cut = width // low_rows
+    places = []
+    for part in range(count):
+        for piece in range(cut):
+            rows = pl.ds(piece * low_rows, low_rows)
+            tall = pl.ds(part * width + piece * low_rows, low_rows)
+            columns = pl.ds(part * width, width)
+            places.append((inward.at[part, rows], in_out.at[rows, columns]))
+            places.append((down.at[tall], down_out.at[tall]))
+    fetches, sends = [], []
+    for place, (source, target) in enumerate(places):
+        fetches.append(pltpu.make_async_copy(source, low.at[place], in_sems.at[place]))
+        sends.append(pltpu.make_async_copy(high.at[place], target, out_sems.at[place]))
+        fetches[-1].start()
+    for place in range(len(places)):
+        fetches[place].wait()
+        high[place] = low[place].astype(F32)
+        sends[place].start()
+    for send in sends:
+        send.wait()
 
 
 def widen_feed(down, inward):
     count, height, width = inward.shape
     cut = 2
-    rows = height // cut
+    blocks = 2 * count * cut
+    hbm = pl.BlockSpec(memory_space=pl.ANY)
     return pl.pallas_call(
         widen_feed_kernel,
-        grid=(count, cut),
-        in_specs=[
-            pl.BlockSpec((rows, width), lambda j, c: (j * cut + c, 0)),
-            pl.BlockSpec((1, rows, width), lambda j, c: (j, c, 0)),
-        ],
-        out_specs=[
-            pl.BlockSpec((rows, width), lambda j, c: (j * cut + c, 0)),
-            pl.BlockSpec((rows, width), lambda j, c: (c, j)),
-        ],
+        in_specs=[hbm, hbm],
+        out_specs=[hbm, hbm],
         out_shape=[
             jax.ShapeDtypeStruct(down.shape, F32),
             jax.ShapeDtypeStruct((height, count * width), F32),
+        ],
+        scratch_shapes=[
+            pltpu.VMEM((blocks, height // cut, width), BF16),
+            pltpu.VMEM((blocks, height // cut, width), F32),
+            pltpu.SemaphoreType.DMA((blocks,)),
+            pltpu.SemaphoreType.DMA((blocks,)),
         ],
         compiler_params=pltpu.CompilerParams(vmem_limit_bytes=VMEM_ASK),
         cost_estimate=cost(9),
@@ -674,63 +741,85 @@
             sums_two,
             sums_in,
             scalars,
-            packed,
+            result,
         )
-        both = jnp.concatenate([result, g_packed], axis=1)
         pair = (mine, core_swap(theirs))
         for step in (0, 1):
-            pair = ring_halve(pair, "z", step)
-        both = lax.all_to_all(after(both, pair[0]), BLK, 0, 0, tiled=True)
+            pair = ring_halve(pair, RING[0], step)
+        both = lax.all_to_all(after(g_packed, pair[0]), BLK, 0, 0, tiled=True)
         for step in (0, 1):
-            pair = ring_halve(pair, "x", step)
+            pair = ring_halve(pair, RING[1], step)
         for step in (0, 1):
             part = add_pair(pair)
-            pair = (part, ring_swap(part, "y", step))
+            pair = (part, ring_swap(part, RING[2], step))
         mine = add_pair(pair)
         for step in (1, 0):
-            mine = ring_join(mine, "x", step)
-        mine = ring_join(after(mine, both), "z", 1)
+            mine = ring_join(mine, RING[1], step)
+        mine = ring_join(mine, RING[0], 1)
         pieces = []
         for base in (0, result.shape[1]):
             pieces.append(both[:, base : base + tok_count])
             pieces.append(both[:, base + tok_count : base + tok_count + mem_count])
-        mine = ring_join(mine, "z", 0)
-        got = core_swap(mine)
-        grad_wqkv, grad_wout = widen(mine, got, scalars, width)
-        blocks = width // 128
-        small = jnp.where(scalars[0, 1] == 0, mine[-512:], got[-512:])
-        small = small[: blocks * small_count].reshape(blocks, small_count, 128)
-        small = small.astype(F32).transpose(1, 0, 2).reshape(small_count, width)
-        return grad_wqkv, grad_wout, small, *pieces
+        mine = after(mine, tuple(pieces))
+        far, near = ring_swap(mine, RING[0], 0), core_swap(mine)
+        core, height = lax.axis_index("core"), lax.axis_index(RING[0])
+        sides = [(height + 1) // 2 % 2, height // 2]
+        own = 2 * core + jnp.where(core == 0, sides[0], sides[1])
+        other = 2 * (1 - core) + jnp.where(core == 0, sides[1], sides[0])
+        groups = jnp.stack([own, other, own ^ 1, other ^ 1]).astype(jnp.int32).reshape(1, 4)
+        *wide, small = widen(mine, near, groups[:, :2], width)
+        start = small_count - 16
+        vectors = [small[start + row] for row in range(8)]
+        bin_rows = w_in.shape[1] // width
+        vectors.append(small[start + 8 : start + 8 + bin_rows].reshape(-1))
+        vectors.append(small[:mem_count])
+        far, wide, vectors = lax.optimization_barrier((far, wide, vectors))
+        wide = widen(far, core_swap(far), groups[:, 2:], width, wide)
+        return *wide, *vectors, *pieces
 
     def nothing(operands):
         text_zero = jnp.zeros(tokens.shape, BF16)
         mem_zero = jnp.zeros(memory.shape, BF16)
+        line = jnp.zeros((width,), F32)
         return (
             jnp.zeros(w_qkv.shape, F32),
             jnp.zeros(w_out.shape, F32),
-            jnp.zeros((small_count, width), F32),
+            *[line] * 8,
+            jnp.zeros(b_in.shape, F32),
+            jnp.zeros(mem_init.shape, F32),
             text_zero,
             mem_zero,
             text_zero,
             mem_zero,
         )
 
-    grad_wqkv, grad_wout, small, output, mem_output, grad_tokens, grad_memory = lax.cond(
+    (
+        grad_wqkv,
+        grad_wout,
+        grad_bquery,
+        grad_bvalue,
+        grad_gain1,
+        grad_bias1,
+        grad_bout,
+        grad_gain2,
+        grad_bias2,
+        grad_bdown,
+        grad_bin,
+        grad_init,
+        output,
+        mem_output,
+        grad_tokens,
+        grad_memory,
+    ) = lax.cond(
         reset_flags[0] >= 0, attention_back, nothing, (result, g_two, g_inner, sums_two, sums_in)
     )
     grad_down, grad_in = widen_feed(grad_down, grad_in)
-    grad_bquery, grad_bvalue, grad_gain1, grad_bias1, grad_bout, grad_gain2, grad_bias2, grad_bdown = (
-        small[mem_count + ROW_PAD + row] for row in range(8)
-    )
-    start = mem_count + ROW_PAD + 8
-    grad_bin = small[start : start + w_in.shape[1] // width].reshape(-1)
     return (
         output,
         mem_output,
         grad_tokens,
         grad_memory,
-        small[:mem_count],
+        grad_init,
         grad_wqkv,
         grad_bquery,
         grad_bvalue,

time: 291 us -> 269 us (0.924)
  waiting for transfers between devices: 102 us -> 86.2 us
  other arithmetic: 17.8 us -> 9.21 us
  starting transfers between devices: 33.7 us -> 37.5 us
  Pallas kernels: 99.2 us -> 96.2 us
    ppermute x10, waiting for transfers between devices: 87.6 us -> 73.6 us  [ring_swap(): return lax.ppermute(value, (axis, 'core'), ring_pairs(step))]
    select_n x4 -> x3, other arithmetic: 8.31 us -> 3 us  [ring_join(): jnp.where(ring_side(axis, step) == 0, jnp.concatenate([value, got], axis=...]
    pallas_call x3 -> x4, Pallas kernels: 48 us -> 44.3 us  [the longest x1 26.2 us: feed(): pl.pallas_call(feed_kernel, grid=(2 * half,), in_specs=[full, whole(lines...]
    ppermute x10, starting transfers between devices: 11.3 us -> 14.2 us  [ring_swap(): return lax.ppermute(value, (axis, 'core'), ring_pairs(step))]
    ppermute x2 -> x3, waiting for transfers between devices: 5.71 us -> 6.31 us  [core_swap(): return lax.ppermute(value, 'core', [(0, 1), (1, 0)])]
    unnamed x22 -> x26, local copies, waits for them, and re-layouts: 7.84 us -> 7.86 us
  transfers between devices with their start and end apart: 16 -> 17, of which waited for: 13 -> 13; matrix products, arithmetic and copies ran while one was open for 12% -> 10% of each run, Pallas kernels for 21% -> 23%
where the time goes in v4:
time: 269 us; the launch traced here: 267 us
  Pallas kernels  96.2 us (36%)
  waiting for transfers between devices  86.2 us (32%)
  starting transfers between devices  37.5 us (14%)
  local copies, waits for them, and re-layouts  22 us (8%)
  between operations  15.6 us (6%)
  other arithmetic  9.21 us (3%)
    ppermute x10, waiting for transfers between devices, ring_swap(): return lax.ppermute(value, (axis, 'core'), ring_pairs(step))  73.6 us
    pallas_call x1, Pallas kernels, backward(): pl.pallas_call(backward_kernel, grid=(parts + 3,), in_specs=[full, early(...  38 us
    pallas_call x1, Pallas kernels, feed(): pl.pallas_call(feed_kernel, grid=(2 * half,), in_specs=[full, whole(lines...  26.2 us
    ppermute x10, starting transfers between devices, ring_swap(): return lax.ppermute(value, (axis, 'core'), ring_pairs(step))  14.2 us
    pallas_call x1, Pallas kernels, attend(): pl.pallas_call(attend_kernel, grid=(3,), in_specs=[whole(text.shape), who...  13.9 us
    all_to_all x2, starting transfers between devices, to_segments(): return lax.all_to_all(value, BLK, 0, 1, tiled=True)[0]  12.1 us
    pallas_call x1, Pallas kernels, widen_feed(): pl.pallas_call(widen_feed_kernel, in_specs=[hbm, hbm], out_specs=[hbm, hb...  9.23 us
    all_to_all x1, starting transfers between devices, attention_back(): both = lax.all_to_all(after(g_packed, pair[0]), BLK, 0, 0, tiled=True)  9.11 us
  transfers between devices with their start and end apart: 17, of which 13 were waited for; matrix products, arithmetic and copies ran while one was open for 10% of the time, Pallas kernels for 23%

profile of v4, /device:TPU:1, one launch (start us, length us, event | category | flops | bytes accessed | tf_op | source)
XLA Modules:
  0.0 267.2 jit_solution(14251320210612509042)
XLA Ops:
  7.2 6.8 %all-to-all-start.1 = ((bf16[8,64,768]{2,1,0:T(8,128)(2,1)}), bf16[8,64,768]{2,1,0:T(8,128)(2,1)S(1)}, u32[]{:S(2)}, u32[]{:S(2)}) async-start(bf16[8,64,768]{2,1,0:T(8,128)(2,1)} %param.22), calls=%async_computation.1 | async-start | bytes 1572864 | tf_op jit(solution)/shard_map/all_to_all | solution.py:657
  14.0 1.4 fusion.8
  16.2 1.2 constant_dynamic-slice_fusion
  17.4 0.9 dynamic-update-slice
  18.3 0.8 dynamic-update-slice.1
  19.1 0.9 dynamic-update-slice.2
  20.0 0.9 dynamic-update-slice.3
  20.8 0.9 dynamic-update-slice.4
  21.7 0.8 dynamic-update-slice.5
  22.5 0.9 dynamic-update-slice.6
  23.4 0.9 dynamic-update-slice.7
  26.3 5.3 %all-to-all-start.2 = ((bf16[8,64,768]{2,1,0:T(8,128)(2,1)}), bf16[8,64,768]{2,1,0:T(8,128)(2,1)S(1)}, u32[]{:S(2)}, u32[]{:S(2)}) async-start(bf16[8,64,768]{2,1,0:T(8,128)(2,1)} %param.40), calls=%async_computation.2 | async-start | bytes 1572864 | tf_op jit(solution)/shard_map/all_to_all | solution.py:657
  31.6 13.9 %attend.1 = (bf16[544,768]{1,0:T(8,128)(2,1)}, bf16[544,768]{1,0:T(8,128)(2,1)}, bf16[544,768]{1,0:T(8,128)(2,1)}, bf16[544,768]{1,0:T(8,128)(2,1)}, f32[544,128]{1,0:T(8,128)}, /*index=5*/f32[544,768]{1,0:T(8,128)}) custom-call(bf16[512,768]{1,0:T(8,128)(2,1)S(1)} %bitcast.20, bf16[32,768]{1,0:T(8,128)(2,1)S(1)} %pad.32.mem, bf16[768,2304]{1,0:T(8,128)(2,1)} %w_v.1, ...), custom_call_target="tpu_custom_call" | custom-call | flops 15000000512 | tf_op jit(solution)/shard_map/attend/pallas_call | solution.py:132
  45.5 0.9 copy-done.5
  46.3 26.2 %feed.1 = (bf16[8,96,768]{2,1,0:T(8,128)(2,1)}, f32[544,768]{1,0:T(8,128)}, bf16[544,3072]{1,0:T(8,128)(2,1)}, f32[8,768]{1,0:T(8,128)S(1)}, f32[8,3072]{1,0:T(8...) custom-call(f32[544,768]{1,0:T(8,128)} %get-tuple-element.134.resid, ...), custom_call_target="tpu_custom_call" | custom-call | flops 28000000000 | tf_op jit(solution)/shard_map/feed/pallas_call | solution.py:236
  74.0 177.0 %conditional.1 = (f32[768,2304]{1,0:T(8,128)}, f32[768,768]{1,0:T(8,128)}, f32[768]{0:T(1024)}, f32[768]{0:T(1024)}, f32[768]{0:T(1024)}, /*index=5*/f32[768]{0:...) conditional(s32[]{:T(128)} %bitcast.6, () %tuple.20, ...), branch_computations={%region_0.1_spmd, %region_1.2_spmd} | conditional | flops 41020342272 | bytes 98710104 | solution.py:813
  74.0 38.0 %backward.1 = (bf16[9856,128]{1,0:T(8,128)(2,1)}, bf16[9856,128]{1,0:T(8,128)(2,1)}, bf16[8,192,768]{2,1,0:T(8,128)(2,1)}) custom-call(f32[544,768]{1,0:T(8,128)} %get-tuple-element.41.g_two, bf16[544,3072]{1,0:T(8,128)(2,1)} %get-tuple-element.42.g_inner, bf16[768,3072]{1,0:T(8,128)(2,1)} %get-tuple-element.43.w_in, f32[544,768]{1,0:T(8,128)} %get-tuple-element.44.resid, ...), custom_call_target="tpu_custom_call" | custom-call | flops 32999999488 | tf_op jit(solution)/shard_map/cond/branch_1_fun/backward/pallas_call | solution.py:442
  112.1 4.9 %collective-permute-done = bf16[9856,128]{1,0:T(8,128)(2,1)S(1)} collective-permute-done((bf16[9856,128]{1,0:T(8,128)(2,1)}, bf16[9856,128]{1,0:T(8,128)(2,1)S(1)}, u32[]{:S(2)}, u32[]{:S(2)}) %collective-permute-start) | collective-permute-done | bytes 2523168 | tf_op jit(solution)/shard_map/cond/branch_1_fun/ppermute | solution.py:629
  117.0 1.4 copy-done.2
  118.5 3.1 %add_convert_fusion.1 = (bf16[4928,128]{1,0:T(8,128)(2,1)S(1)}, bf16[4928,128]{1,0:T(8,128)(2,1)S(1)}) fusion(bf16[9856,128]{1,0:T(8,128)(2,1)} %copy-done.2, s32[]{:T(128)S(6)} %select_n.144, bf16[9856,128]{1,0:T(8,128)(2,1)} %get-tuple-element.61, s32[]{:T(128)S(6)} %select_n.146), kind=kLoop, calls=%fused_computation.1 | loop fusion | flops 5046272 | bytes 7569416 | tf_op jit(solution)/shard_map/cond/branch_1_fun/convert_element_type | solution.py:633
  121.6 2.7 %collective-permute-start.1 = (bf16[4928,128]{1,0:T(8,128)(2,1)S(1)}, bf16[4928,128]{1,0:T(8,128)(2,1)}, u32[]{:S(2)}, u32[]{:S(2)}) collective-permute-start(bf16[4928,128]{1,0:T(8,128)(2,1)S(1)} %get-tuple-element.251), channel_id=1, source_target_pairs={{0,2},{1,7},{2,0},{3,5},{4,6},{5,3},{6,4},{7,1},{8,10},{9,15},{10,... | collective-permute-start | bytes 3784712 | tf_op jit(solution)/shard_map/cond/branch_1_fun/ppermute | solution.py:625
  124.2 16.8 %collective-permute-done.1 = bf16[4928,128]{1,0:T(8,128)(2,1)} collective-permute-done((bf16[4928,128]{1,0:T(8,128)(2,1)S(1)}, bf16[4928,128]{1,0:T(8,128)(2,1)}, u32[]{:S(2)}, u32[]{:S(2)}) %collective-permute-start.1) | collective-permute-done | bytes 1261600 | tf_op jit(solution)/shard_map/cond/branch_1_fun/ppermute | solution.py:625
  141.0 1.6 add_convert_fusion.3
  143.2 9.3 %collective-permute-done.2 = bf16[2464,128]{1,0:T(8,128)(2,1)S(1)} collective-permute-done((bf16[2464,128]{1,0:T(8,128)(2,1)S(1)}, bf16[2464,128]{1,0:T(8,128)(2,1)S(1)}, u32[]{:S(2)}, u32[]{:S(2)}) %collective-permute-start.2) | collective-permute-done | bytes 630816 | tf_op jit(solution)/shard_map/cond/branch_1_fun/ppermute | solution.py:625
  152.7 3.0 %collective-permute-start.3 = (bf16[1232,128]{1,0:T(8,128)(2,1)S(1)}, bf16[1232,128]{1,0:T(8,128)(2,1)S(1)}, u32[]{:S(2)}, u32[]{:S(2)}) collective-permute-start(bf16[1232,128]{1,0:T(8,128)(2,1)S(1)} %get-tuple-element.259), channel_id=1, source_target_pairs={{0,8},{1,25},{8,0},{9,17},{16,24},{17,9},{24,16},{25,1},{2,10},{3,... | collective-permute-start | bytes 946184 | tf_op jit(solution)/shard_map/cond/branch_1_fun/ppermute | solution.py:625
  155.7 4.4 %collective-permute-done.3 = bf16[1232,128]{1,0:T(8,128)(2,1)S(1)} collective-permute-done((bf16[1232,128]{1,0:T(8,128)(2,1)S(1)}, bf16[1232,128]{1,0:T(8,128)(2,1)S(1)}, u32[]{:S(2)}, u32[]{:S(2)}) %collective-permute-start.3) | collective-permute-done | bytes 315424 | tf_op jit(solution)/shard_map/cond/branch_1_fun/ppermute | solution.py:625
  160.4 9.1 %all-to-all-start = ((bf16[8,192,768]{2,1,0:T(8,128)(2,1)}), bf16[8,192,768]{2,1,0:T(8,128)(2,1)S(1)}, u32[]{:S(2)}, u32[]{:S(2)}) async-start(bf16[8,192,768]{2,1,0:T(8,128)(2,1)} %get-tuple-element.64), calls=%async_computation | async-start | bytes 4718592 | tf_op jit(solution)/shard_map/cond/branch_1_fun/all_to_all | solution.py:749
  169.6 2.7 %collective-permute-start.5 = (bf16[616,128]{1,0:T(8,128)(2,1)S(1)}, bf16[616,128]{1,0:T(8,128)(2,1)S(1)}, u32[]{:S(2)}, u32[]{:S(2)}) collective-permute-start(bf16[616,128]{1,0:T(8,128)(2,1)S(1)} %add_convert_fusion.8), channel_id=1, source_target_pairs={{0,32},{1,97},{32,0},{33,65},{64,96},{65,33},{96,64},{97,1},{2,34}... | collective-permute-start | bytes 473096 | tf_op jit(solution)/shard_map/cond/branch_1_fun/ppermute | solution.py:625
  172.3 3.1 %collective-permute-done.5 = bf16[616,128]{1,0:T(8,128)(2,1)S(1)} collective-permute-done((bf16[616,128]{1,0:T(8,128)(2,1)S(1)}, bf16[616,128]{1,0:T(8,128)(2,1)S(1)}, u32[]{:S(2)}, u32[]{:S(2)}) %collective-permute-start.5) | collective-permute-done | bytes 157728 | tf_op jit(solution)/shard_map/cond/branch_1_fun/ppermute | solution.py:625
  175.5 4.4 %collective-permute-done.6 = bf16[616,128]{1,0:T(8,128)(2,1)S(1)} collective-permute-done((bf16[616,128]{1,0:T(8,128)(2,1)S(1)}, bf16[616,128]{1,0:T(8,128)(2,1)S(1)}, u32[]{:S(2)}, u32[]{:S(2)}) %collective-permute-start.6) | collective-permute-done | bytes 157728 | tf_op jit(solution)/shard_map/cond/branch_1_fun/ppermute | solution.py:625
  180.1 4.4 %collective-permute-done.7 = bf16[616,128]{1,0:T(8,128)(2,1)S(1)} collective-permute-done((bf16[616,128]{1,0:T(8,128)(2,1)S(1)}, bf16[616,128]{1,0:T(8,128)(2,1)S(1)}, u32[]{:S(2)}, u32[]{:S(2)}) %collective-permute-start.7) | collective-permute-done | bytes 157728 | tf_op jit(solution)/shard_map/cond/branch_1_fun/ppermute | solution.py:625
  185.0 7.9 %collective-permute-done.8 = bf16[1232,128]{1,0:T(8,128)(2,1)} collective-permute-done((bf16[1232,128]{1,0:T(8,128)(2,1)S(1)}, bf16[1232,128]{1,0:T(8,128)(2,1)}, u32[]{:S(2)}, u32[]{:S(2)}) %collective-permute-start.8) | collective-permute-done | bytes 315424 | tf_op jit(solution)/shard_map/cond/branch_1_fun/ppermute | solution.py:625
  192.9 1.3 maximum_select_fusion.1
  194.2 1.6 collective-permute-start.9
  195.8 6.2 %all-to-all-done = bf16[8,192,768]{2,1,0:T(8,128)(2,1)S(1)} async-done(((bf16[8,192,768]{2,1,0:T(8,128)(2,1)}), bf16[8,192,768]{2,1,0:T(8,128)(2,1)S(1)}, u32[]{:S(2)}, u32[]{:S(2)}) %all-to-all-start) | async-done | bytes 2359328 | tf_op jit(solution)/shard_map/cond/branch_1_fun/all_to_all | solution.py:749
  202.8 1.2 fusion.6
  204.0 3.9 %collective-permute-done.9 = bf16[2464,128]{1,0:T(8,128)(2,1)} collective-permute-done((bf16[2464,128]{1,0:T(8,128)(2,1)S(1)}, bf16[2464,128]{1,0:T(8,128)(2,1)}, u32[]{:S(2)}, u32[]{:S(2)}) %collective-permute-start.9) | collective-permute-done | bytes 630816 | tf_op jit(solution)/shard_map/cond/branch_1_fun/ppermute | solution.py:625
  207.9 1.6 maximum_select_fusion.first
  209.5 2.1 collective-permute-start.11
  211.6 2.6 collective-permute-start.10
  214.9 4.8 %widen.2 = (f32[768,2304]{1,0:T(8,128)}, f32[768,768]{1,0:T(8,128)}, f32[48,768]{1,0:T(8,128)}) custom-call(bf16[4928,128]{1,0:T(8,128)(2,1)} %copy-done.3, bf16[4928,128]{1,0:T(8,128)(2,1)} %collective-permute-done.11.second, s32[1,2]{1,0:T(1,128)} %get-tuple-element.261.groups), custom_call_target="tpu_custom_call" | custom-call | flops 4000000000 | tf_op jit(solution)/shard_map/cond/branch_1_fun/widen/pallas_call | solution.py:538
  220.5 0.9 slice.48
  221.4 1.7 slice_reduce_fusion
  223.1 19.6 %collective-permute-done.10.first = bf16[4928,128]{1,0:T(8,128)(2,1)S(1)} collective-permute-done((bf16[4928,128]{1,0:T(8,128)(2,1)S(1)}, bf16[4928,128]{1,0:T(8,128)(2,1)S(1)}, u32[]{:S(2)}, u32[]{:S(2)}) %collective-permute-start.10) | collective-permute-done | bytes 1261600 | tf_op jit(solution)/shard_map/cond/branch_1_fun/ppermute | solution.py:625
  244.2 1.4 collective-permute-done.12.second
  245.6 1.0 copy-done.10
  246.7 4.0 %widen.3 = (f32[768,2304]{1,0:T(8,128)}, f32[768,768]{1,0:T(8,128)}) custom-call(bf16[4928,128]{1,0:T(8,128)(2,1)} %copy-done.9, bf16[4928,128]{1,0:T(8,128)(2,1)} %copy-done.10, s32[1,2]{1,0:T(1,128)} %get-tuple-element.260.groups, f32[768,2304]{1,0:T(8,128)} %get-tuple-element.70.refs_0_, ...), custom_call_target="tpu_custom_call", output_to_operand_aliasing={{0}: (3, {}), {1}: (4, {})} | custom-call | flops 4000000000 | tf_op jit(solution)/shard_map/cond/branch_1_fun/widen/pallas_call | solution.py:538
  251.1 9.2 %widen_feed.1 = (f32[3072,768]{1,0:T(8,128)}, f32[768,3072]{1,0:T(8,128)}) custom-call(bf16[3072,768]{1,0:T(8,128)(2,1)} %get-tuple-element.248.down, bf16[4,768,768]{2,1,0:T(8,128)(2,1)} %get-tuple-element.249.inward), custom_call_target="tpu_custom_call" | custom-call | flops 8999999488 | tf_op jit(solution)/shard_map/widen_feed/pallas_call | solution.py:586
  (69 shorter events, 8.9 us)
Async XLA Ops:
  7.2 8.2 %copy-start = (s32[8,512]{1,0:T(8,128)S(1)}, s32[8,512]{1,0:T(8,128)}, u32[]{:S(2)}) copy-start(s32[8,512]{1,0:T(8,128)} %param.26) | copy-start | bytes 49156
  7.2 19.1 %all-to-all-start.1 = ((bf16[8,64,768]{2,1,0:T(8,128)(2,1)}), bf16[8,64,768]{2,1,0:T(8,128)(2,1)S(1)}, u32[]{:S(2)}, u32[]{:S(2)}) async-start(bf16[8,64,768]{2,1,0:T(8,128)(2,1)} %param.22), calls=%async_computation.1 | async-start | bytes 1572864 | tf_op jit(solution)/shard_map/all_to_all | solution.py:657
  14.0 17.6 %copy-start.11 = (bf16[768,768]{1,0:T(8,128)(2,1)S(1)}, bf16[768,768]{1,0:T(8,128)(2,1)}, u32[]{:S(2)}) copy-start(bf16[768,768]{1,0:T(8,128)(2,1)} %w_out.1) | copy-start | bytes 3538948
  26.3 19.1 %all-to-all-start.2 = ((bf16[8,64,768]{2,1,0:T(8,128)(2,1)}), bf16[8,64,768]{2,1,0:T(8,128)(2,1)S(1)}, u32[]{:S(2)}, u32[]{:S(2)}) async-start(bf16[8,64,768]{2,1,0:T(8,128)(2,1)} %param.40), calls=%async_computation.2 | async-start | bytes 1572864 | tf_op jit(solution)/shard_map/all_to_all | solution.py:657
  31.6 219.5 %all-reduce.11.cloned.1.call-start = ((), (), s32[]{:S(2)}) async-start(), calls=%async_computation.3 | async-start | bytes 18874368 | tf_op jit(solution)/shard_map/psum | solution.py:718
  45.5 0.9 copy-start.5
  72.6 1.4 copy-start.12
  112.0 5.0 %collective-permute-start = (bf16[9856,128]{1,0:T(8,128)(2,1)}, bf16[9856,128]{1,0:T(8,128)(2,1)S(1)}, u32[]{:S(2)}, u32[]{:S(2)}) collective-permute-start(bf16[9856,128]{1,0:T(8,128)(2,1)} %get-tuple-element.62), channel_id=1, source_target_pairs={{0,1},{1,0},{2,3},{3,2},{4,5},{5,4},{6,7},{7,6},{8,9},{9,8},{10,11... | collective-permute-start | bytes 7569416 | tf_op jit(solution)/shard_map/cond/branch_1_fun/ppermute | solution.py:629
  117.0 1.4 copy-start.2
  121.6 19.4 %collective-permute-start.1 = (bf16[4928,128]{1,0:T(8,128)(2,1)S(1)}, bf16[4928,128]{1,0:T(8,128)(2,1)}, u32[]{:S(2)}, u32[]{:S(2)}) collective-permute-start(bf16[4928,128]{1,0:T(8,128)(2,1)S(1)} %get-tuple-element.251), channel_id=1, source_target_pairs={{0,2},{1,7},{2,0},{3,5},{4,6},{5,3},{6,4},{7,1},{8,10},{9,15},{10,... | collective-permute-start | bytes 3784712 | tf_op jit(solution)/shard_map/cond/branch_1_fun/ppermute | solution.py:625
  142.6 9.9 %collective-permute-start.2 = (bf16[2464,128]{1,0:T(8,128)(2,1)S(1)}, bf16[2464,128]{1,0:T(8,128)(2,1)S(1)}, u32[]{:S(2)}, u32[]{:S(2)}) collective-permute-start(bf16[2464,128]{1,0:T(8,128)(2,1)S(1)} %get-tuple-element.253), channel_id=1, source_target_pairs={{0,6},{1,3},{2,4},{3,1},{4,2},{5,7},{6,0},{7,5},{8,14},{9,11},{10,... | collective-permute-start | bytes 1892360 | tf_op jit(solution)/shard_map/cond/branch_1_fun/ppermute | solution.py:625
  152.7 7.3 %collective-permute-start.3 = (bf16[1232,128]{1,0:T(8,128)(2,1)S(1)}, bf16[1232,128]{1,0:T(8,128)(2,1)S(1)}, u32[]{:S(2)}, u32[]{:S(2)}) collective-permute-start(bf16[1232,128]{1,0:T(8,128)(2,1)S(1)} %get-tuple-element.259), channel_id=1, source_target_pairs={{0,8},{1,25},{8,0},{9,17},{16,24},{17,9},{24,16},{25,1},{2,10},{3,... | collective-permute-start | bytes 946184 | tf_op jit(solution)/shard_map/cond/branch_1_fun/ppermute | solution.py:625
  160.1 9.5 %collective-permute-start.4 = (bf16[616,128]{1,0:T(8,128)(2,1)S(1)}, bf16[616,128]{1,0:T(8,128)(2,1)S(1)}, u32[]{:S(2)}, u32[]{:S(2)}) collective-permute-start(bf16[616,128]{1,0:T(8,128)(2,1)S(1)} %add_convert_fusion.9), channel_id=1, source_target_pairs={{0,24},{1,9},{8,16},{9,1},{16,8},{17,25},{24,0},{25,17},{2,26},{3,... | collective-permute-start | bytes 473096 | tf_op jit(solution)/shard_map/cond/branch_1_fun/ppermute | solution.py:625
  160.4 41.6 %all-to-all-start = ((bf16[8,192,768]{2,1,0:T(8,128)(2,1)}), bf16[8,192,768]{2,1,0:T(8,128)(2,1)S(1)}, u32[]{:S(2)}, u32[]{:S(2)}) async-start(bf16[8,192,768]{2,1,0:T(8,128)(2,1)} %get-tuple-element.64), calls=%async_computation | async-start | bytes 4718592 | tf_op jit(solution)/shard_map/cond/branch_1_fun/all_to_all | solution.py:749
  169.6 5.8 %collective-permute-start.5 = (bf16[616,128]{1,0:T(8,128)(2,1)S(1)}, bf16[616,128]{1,0:T(8,128)(2,1)S(1)}, u32[]{:S(2)}, u32[]{:S(2)}) collective-permute-start(bf16[616,128]{1,0:T(8,128)(2,1)S(1)} %add_convert_fusion.8), channel_id=1, source_target_pairs={{0,32},{1,97},{32,0},{33,65},{64,96},{65,33},{96,64},{97,1},{2,34}... | collective-permute-start | bytes 473096 | tf_op jit(solution)/shard_map/cond/branch_1_fun/ppermute | solution.py:625
  175.5 4.5 %collective-permute-start.6 = (bf16[616,128]{1,0:T(8,128)(2,1)S(1)}, bf16[616,128]{1,0:T(8,128)(2,1)S(1)}, u32[]{:S(2)}, u32[]{:S(2)}) collective-permute-start(bf16[616,128]{1,0:T(8,128)(2,1)S(1)} %add_convert_fusion.7), channel_id=1, source_target_pairs={{0,96},{1,33},{32,64},{33,1},{64,32},{65,97},{96,0},{97,65},{2,98}... | collective-permute-start | bytes 473096 | tf_op jit(solution)/shard_map/cond/branch_1_fun/ppermute | solution.py:625
  180.0 4.5 %collective-permute-start.7 = (bf16[616,128]{1,0:T(8,128)(2,1)S(1)}, bf16[616,128]{1,0:T(8,128)(2,1)S(1)}, u32[]{:S(2)}, u32[]{:S(2)}) collective-permute-start(bf16[616,128]{1,0:T(8,128)(2,1)S(1)} %add_convert_fusion.6), channel_id=1, source_target_pairs={{0,24},{1,9},{8,16},{9,1},{16,8},{17,25},{24,0},{25,17},{2,26},{3,... | collective-permute-start | bytes 473096 | tf_op jit(solution)/shard_map/cond/branch_1_fun/ppermute | solution.py:625
  184.6 8.4 %collective-permute-start.8 = (bf16[1232,128]{1,0:T(8,128)(2,1)S(1)}, bf16[1232,128]{1,0:T(8,128)(2,1)}, u32[]{:S(2)}, u32[]{:S(2)}) collective-permute-start(bf16[1232,128]{1,0:T(8,128)(2,1)S(1)} %maximum_select_fusion.2), channel_id=1, source_target_pairs={{0,8},{1,25},{8,0},{9,17},{16,24},{17,9},{24,16},{25,1},{2,10},{3,... | collective-permute-start | bytes 946184 | tf_op jit(solution)/shard_map/cond/branch_1_fun/ppermute | solution.py:625
  194.2 13.7 %collective-permute-start.9 = (bf16[2464,128]{1,0:T(8,128)(2,1)S(1)}, bf16[2464,128]{1,0:T(8,128)(2,1)}, u32[]{:S(2)}, u32[]{:S(2)}) collective-permute-start(bf16[2464,128]{1,0:T(8,128)(2,1)S(1)} %maximum_select_fusion.1), channel_id=1, source_target_pairs={{0,6},{1,3},{2,4},{3,1},{4,2},{5,7},{6,0},{7,5},{8,14},{9,11},{10,... | collective-permute-start | bytes 1892360 | tf_op jit(solution)/shard_map/cond/branch_1_fun/ppermute | solution.py:625
  209.5 5.3 %copy-start.3 = (bf16[4928,128]{1,0:T(8,128)(2,1)}, bf16[4928,128]{1,0:T(8,128)(2,1)S(1)}, u32[]{:S(2)}) copy-start(bf16[4928,128]{1,0:T(8,128)(2,1)S(1)} %maximum_select_fusion.first) | copy-start | bytes 3784708 | tf_op jit(solution)/shard_map/cond
  209.5 5.3 %collective-permute-start.11 = (bf16[4928,128]{1,0:T(8,128)(2,1)S(1)}, bf16[4928,128]{1,0:T(8,128)(2,1)}, u32[]{:S(2)}, u32[]{:S(2)}) collective-permute-start(bf16[4928,128]{1,0:T(8,128)(2,1)S(1)} %maximum_select_fusion.first), channel_id=1, source_target_pairs={{0,1},{1,0},{2,3},{3,2},{4,5},{5,4},{6,7},{7,6},{8,9},{9,8},{10,11... | collective-permute-start | bytes 3784712 | tf_op jit(solution)/shard_map/cond/branch_1_fun/ppermute | solution.py:629
  211.6 31.0 %collective-permute-start.10 = (bf16[4928,128]{1,0:T(8,128)(2,1)S(1)}, bf16[4928,128]{1,0:T(8,128)(2,1)S(1)}, u32[]{:S(2)}, u32[]{:S(2)}) collective-permute-start(bf16[4928,128]{1,0:T(8,128)(2,1)S(1)} %maximum_select_fusion.first), channel_id=1, source_target_pairs={{0,2},{1,7},{2,0},{3,5},{4,6},{5,3},{6,4},{7,1},{8,10},{9,15},{10,... | collective-permute-start | bytes 3784712 | tf_op jit(solution)/shard_map/cond/branch_1_fun/ppermute | solution.py:625
  214.9 27.8 %copy-start.4 = (bf16[8,20,768]{2,1,0:T(8,128)(2,1)S(1)}, bf16[8,20,768]{2,1,0:T(8,128)(2,1)}, u32[]{:S(2)}) copy-start(bf16[8,20,768]{2,1,0:T(8,128)(2,1)} %get-tuple-element.254) | copy-start | bytes 737284 | tf_op jit(solution)/shard_map/cond
  242.6 3.0 %copy-start.9 = (bf16[4928,128]{1,0:T(8,128)(2,1)}, bf16[4928,128]{1,0:T(8,128)(2,1)S(1)}, u32[]{:S(2)}) copy-start(bf16[4928,128]{1,0:T(8,128)(2,1)S(1)} %collective-permute-done.10.first) | copy-start | bytes 3784708 | tf_op jit(solution)/shard_map/cond
  242.6 3.0 %collective-permute-start.12 = (bf16[4928,128]{1,0:T(8,128)(2,1)S(1)}, bf16[4928,128]{1,0:T(8,128)(2,1)S(1)}, u32[]{:S(2)}, u32[]{:S(2)}) collective-permute-start(bf16[4928,128]{1,0:T(8,128)(2,1)S(1)} %collective-permute-done.10.first), channel_id=1, source_target_pairs={{0,1},{1,0},{2,3},{3,2},{4,5},{5,4},{6,7},{7,6},{8,9},{9,8},{10,11... | collective-permute-start | bytes 3784712 | tf_op jit(solution)/shard_map/cond/branch_1_fun/ppermute | solution.py:629
  245.6 1.1 copy-start.10
  251.0 9.3 %copy-start.6 = (f32[20,768]{1,0:T(8,128)}, f32[20,768]{1,0:T(8,128)S(1)}, u32[]{:S(2)}) copy-start(f32[20,768]{1,0:T(8,128)S(1)} %get-tuple-element.224) | copy-start | bytes 184324
  251.0 9.3 %copy-start.7 = (f32[3072]{0:T(1024)}, f32[3072]{0:T(1024)S(1)}, u32[]{:S(2)}) copy-start(f32[3072]{0:T(1024)S(1)} %get-tuple-element.233) | copy-start | bytes 36868
  251.0 9.3 %copy-start.8 = (f32[768]{0:T(1024)}, f32[768]{0:T(1024)S(1)}, u32[]{:S(2)}) copy-start(f32[768]{0:T(1024)S(1)} %get-tuple-element.235) | copy-start | bytes 9220
  251.1 9.3 %copy-start.1 = (s32[8,512]{1,0:T(8,128)S(1)}, s32[8,512]{1,0:T(8,128)}, u32[]{:S(2)}) copy-start(s32[8,512]{1,0:T(8,128)} %param.26) | copy-start | bytes 49156
Sparse Core Ops, SparseCore 0:
  72.7 172.0 all-reduce.10
